TPU v7x, 32 devices: a whole 2x2x4 slice. The times are simulated.
32 devices in a mesh: grp: 2 (over y), lat: 4 (over z), tm: 2 (over x), chan: 2 (over core).
Axes of the slice: x: 2, y: 2, z: 4, core: 2. Of those that a mesh axis runs over, the one named last changes fastest.
Arguments:
- innovations: bfloat16 [4, 4, 73, 32, 128], P(None, ('grp', 'tm'), None, ('lat', 'chan')), parts along dimension 1, may hold values from -6 to 6
- obs_mask: int32 [4, 8, 4], P(('grp', 'tm'), ('lat', 'chan')), parts along dimension 0, may hold values 0 or 1
- slopes: bfloat16 [4, 128, 32, 128], P(('grp', 'tm'), 'chan', 'lat'), parts along dimension 0, may hold values from -0.14941406 to 1.09375
- layer_of: int32 [2], replicated, may hold values from 0 to 7
- weight_in: bfloat16 [8, 3, 3, 73, 128], P(None, None, None, None, 'chan'), may hold values from -0.1875 to 0.1875
- weight_out: bfloat16 [8, 3, 3, 128, 73], P(None, None, None, 'chan'), may hold values from -0.25 to 0.25
Outputs:
- gradients: float32 [4, 4, 73, 32, 128], P(None, ('grp', 'tm'), None, ('lat', 'chan')), parts along dimension 1
There are 2 independent parts, one for each index of `grp`. A program takes and returns all parts, laid end to end along the dimension named above; an argument that names none is the same for every part. Nothing has to cross between parts.
All inputs are finite; a program needn't handle non-finite values. No bound on the sum of `obs_mask` on one device may be relied on, other than what follows from the above.
Results may differ from a plain program's by a relative error of at most 0.011.
Values may be sent and summed in bfloat16 or wider, within the bound.
No kernel may reach another device: no remote copies, remote signals or barrier semaphores. Data moves between devices by JAX's collectives and lax.ppermute only.
A program may use at most 64 MiB of HBM per device.

v0:
```python
import jax
import jax.numpy as jnp
from jax import lax
from jax.sharding import PartitionSpec as P


def with_halo(cells, sides, width):
    for axis, dim in sides:
        count = lax.axis_size(axis)
        ends = count - 1
        head = lax.slice_in_dim(cells, 0, width, axis=dim)
        tail = lax.slice_in_dim(cells, cells.shape[dim] - width, cells.shape[dim], axis=dim)
        cells = jnp.concatenate(
            [
                lax.ppermute(tail, axis, [(i, (i + 1) % count) for i in range(ends)]),
                cells,
                lax.ppermute(head, axis, [((i + 1) % count, i) for i in range(ends)]),
            ],
            axis=dim,
        )
    return cells


def from_behind(block, axis, distance):
    devices = range(lax.axis_size(axis))
    route = [(i - distance, i) for i in devices if i - distance in devices]
    return lax.ppermute(block, axis, route)


def spread_tiles(obs_tiles):
    return jnp.repeat(jnp.repeat(obs_tiles, 4, axis=-2), 32, axis=-1).astype(jnp.float32)


def local_conv(rimmed, kernel):
    height = rimmed.shape[2] - 2
    width = rimmed.shape[3]
    padded = jnp.pad(rimmed, ((0, 0), (0, 0), (0, 0), (1, 1)))
    summed = None
    for row_off in range(3):
        for col_off in range(3):
            shifted = padded[
                :, :, 2 - row_off : 2 - row_off + height, 2 - col_off : 2 - col_off + width
            ]
            contrib = jnp.einsum(
                "ij,fjhw->fihw",
                kernel[row_off, col_off],
                shifted,
                preferred_element_type=jnp.float32,
            )
            summed = contrib if summed is None else summed + contrib
    return summed


def section_step(adjoint, slope_rows, forcing_rows, layer_no, weight_in, weight_out):
    kernel_out = lax.dynamic_index_in_dim(weight_out, layer_no, 0, keepdims=False)
    kernel_in = lax.dynamic_index_in_dim(weight_in, layer_no, 0, keepdims=False)
    rounded = lax.all_gather(adjoint.astype(jnp.bfloat16), "chan", axis=2, tiled=True)
    rimmed = with_halo(rounded, (("lat", 2),), 1)
    hidden_grad = local_conv(rimmed, kernel_out)
    scaled = (slope_rows.astype(jnp.float32)[None] * hidden_grad).astype(jnp.bfloat16)
    scaled_rims = with_halo(scaled, (("lat", 2),), 1)
    partial_sum = local_conv(scaled_rims, kernel_in)
    combined = lax.psum_scatter(
        partial_sum.astype(jnp.bfloat16), "chan", scatter_dimension=2, tiled=True
    ).astype(jnp.float32)
    return adjoint + combined + forcing_rows


def run_sections(incoming, slopes, forcing, layers, weight_in, weight_out):

    def one_section(adjoint, items):
        slope_rows, forcing_rows, layer_no = items
        updated = section_step(adjoint, slope_rows, forcing_rows, layer_no, weight_in, weight_out)
        return (updated, updated)

    adjoint, fresh = lax.scan(
        one_section, incoming, (slopes, jnp.moveaxis(forcing, 1, 0), layers), reverse=True
    )
    return (adjoint, jnp.moveaxis(fresh, 0, 1))


def per_device(innovations, obs_mask, slopes, layer_of, weight_in, weight_out):
    owners = lax.axis_size("tm")
    owner = lax.axis_index("tm")
    sec_count = slopes.shape[0]
    state_shape = (
        innovations.shape[0],
        innovations.shape[2],
        innovations.shape[3],
        innovations.shape[4],
    )
    forcing = innovations.astype(jnp.float32) * spread_tiles(obs_mask)[None, :, None]
    layers_here = lax.dynamic_slice_in_dim(layer_of, owner * sec_count, sec_count)
    incoming = jnp.zeros(state_shape, jnp.float32)
    gradients = jnp.zeros(forcing.shape, jnp.float32)
    for segment_no in range(owners):
        adjoint, fresh = run_sections(incoming, slopes, forcing, layers_here, weight_in, weight_out)
        gradients = jnp.where(owner == owners - 1 - segment_no, fresh, gradients)
        if segment_no + 1 < owners:
            incoming = from_behind(adjoint.astype(jnp.bfloat16), "tm", -1).astype(adjoint.dtype)
    return gradients


def solution(mesh):
    return jax.shard_map(
        per_device,
        mesh=mesh,
        in_specs=(
            P(None, ("grp", "tm"), None, ("lat", "chan"), None),
            P(("grp", "tm"), ("lat", "chan"), None),
            P(("grp", "tm"), "chan", "lat", None),
            P(),
            P(None, None, None, None, "chan"),
            P(None, None, None, "chan", None),
        ),
        out_specs=P(None, ("grp", "tm"), None, ("lat", "chan"), None),
        check_vma=False,
    )
```

profile of v0, /device:TPU:0, one launch (start us, length us, event | category | flops | bytes accessed | tf_op | source)
XLA Modules:
  0.0 126.0 jit_solution(16905465113636334349)
XLA Ops:
  6.6 1.4 %collective-permute-start.1 = (bf16[4,73,1,128]{3,1,2,0:T(8,128)(2,1)S(1)}, bf16[4,73,1,128]{3,1,2,0:T(8,128)(2,1)S(1)}, u32[]{:S(2)}, u32[]{:S(2)}) collective-permute-start(bf16[4,73,1,128]{3,1,2,0:T(8,128)(2,1)S(1)} %slice.294), channel_id=1, source_target_pairs={{4,0},{8,4},{12,8},{5,1},{9,5},{13,9},{6,2},{10,6},{14,10},{7,3},{... | collective-permute-start | bytes 224264 | tf_op jit(solution)/shard_map/while/body/eval_jaxpr/ppermute | solution.py:17
  8.0 5.6 %collective-permute-start = (bf16[4,73,1,128]{3,1,2,0:T(8,128)(2,1)S(1)}, bf16[4,73,1,128]{3,1,2,0:T(8,128)(2,1)S(1)}, u32[]{:S(2)}, u32[]{:S(2)}) collective-permute-start(bf16[4,73,1,128]{3,1,2,0:T(8,128)(2,1)S(1)} %slice.294), channel_id=1, source_target_pairs={{0,4},{4,8},{8,12},{1,5},{5,9},{9,13},{2,6},{6,10},{10,14},{3,7},{... | collective-permute-start | bytes 224264 | tf_op jit(solution)/shard_map/while/body/eval_jaxpr/ppermute | solution.py:15
  13.6 1.2 dynamic_slice.32
  17.2 0.9 select_maximum_fusion.2
  18.1 0.4 fusion.50
  18.5 0.4 fusion.53
  19.7 0.4 fusion.21
  20.3 0.6 fusion.25
  20.9 3.9 %collective-permute-start.2 = (bf16[4,64,1,128]{3,1,2,0:T(8,128)(2,1)S(1)}, bf16[4,64,1,128]{3,1,2,0:T(8,128)(2,1)S(1)}, u32[]{:S(2)}, u32[]{:S(2)}) collective-permute-start(bf16[4,64,1,128]{3,1,2,0:T(8,128)(2,1)S(1)} %get-tuple-element.39), channel_id=1, source_target_pairs={{0,4},{4,8},{8,12},{1,5},{5,9},{9,13},{2,6},{6,10},{10,14},{3,7},{... | collective-permute-start | bytes 196616 | tf_op jit(solution)/shard_map/while/body/eval_jaxpr/ppermute | solution.py:15
  24.9 1.3 %collective-permute-start.3 = (bf16[4,64,1,128]{3,1,2,0:T(8,128)(2,1)S(1)}, bf16[4,64,1,128]{3,1,2,0:T(8,128)(2,1)S(1)}, u32[]{:S(2)}, u32[]{:S(2)}) collective-permute-start(bf16[4,64,1,128]{3,1,2,0:T(8,128)(2,1)S(1)} %get-tuple-element.48), channel_id=1, source_target_pairs={{4,0},{8,4},{12,8},{5,1},{9,5},{13,9},{6,2},{10,6},{14,10},{7,3},{... | collective-permute-start | bytes 196616 | tf_op jit(solution)/shard_map/while/body/eval_jaxpr/ppermute | solution.py:17
  26.2 0.9 dynamic-slice_bitcast_fusion
  27.1 3.9 %collective-permute-done.3 = bf16[4,64,1,128]{3,1,2,0:T(8,128)(2,1)S(1)} collective-permute-done((bf16[4,64,1,128]{3,1,2,0:T(8,128)(2,1)S(1)}, bf16[4,64,1,128]{3,1,2,0:T(8,128)(2,1)S(1)}, u32[]{:S(2)}, u32[]{:S(2)}) %collective-permute-start.3) | collective-permute-done | bytes 65568 | tf_op jit(solution)/shard_map/while/body/eval_jaxpr/ppermute | solution.py:17
  31.0 0.7 select_maximum_fusion.6
  32.5 0.4 convolution_add_fusion.13
  32.9 0.4 convolution_add_fusion.12
  33.3 0.4 convolution_add_fusion.11
  34.1 0.4 convolution_add_fusion.9
  34.4 0.4 convolution_add_fusion.8
  34.9 0.4 fusion.27
  35.3 1.3 %copy.11 = bf16[4,73,8,128]{3,0,1,2:T(4,128)(2,1)} copy(bf16[4,73,8,128]{3,1,2,0:T(8,128)(2,1)S(1)} %fusion.27) | data formatting | bytes 1196032 | tf_op jit(solution)/shard_map/while/body/eval_jaxpr/convert_element_type | solution.py:64
  36.9 0.6 dynamic-slice
  38.2 17.0 %all-reduce.11.cloned.1.call-done = bf16[4,73,8,128]{3,0,1,2:T(4,128)(2,1)} async-done(((bf16[4,73,8,128]{3,0,1,2:T(4,128)(2,1)}), bf16[4,73,8,128]{3,0,1,2:T(4,128)(2,1)}) %all-reduce.11.cloned.1.call-update) | async-done | bytes 598032
  55.2 1.1 constant_dynamic-slice_fusion.1
  56.4 1.3 %collective-permute-start.4 = (bf16[4,73,4,128]{3,1,2,0:T(8,128)(2,1)S(1)}, bf16[4,73,4,128]{3,1,2,0:T(8,128)(2,1)S(1)}, u32[]{:S(2)}, u32[]{:S(2)}) collective-permute-start(bf16[4,73,4,128]{3,1,2,0:T(8,128)(2,1)S(1)} %fusion.60), channel_id=1, source_target_pairs={{2,0},{3,1},{6,4},{7,5},{10,8},{11,9},{14,12},{15,13},{18,16},{19,... | collective-permute-start | bytes 897032 | tf_op jit(solution)/shard_map/ppermute | solution.py:27
  57.6 10.4 %collective-permute-done.4 = bf16[4,73,4,128]{3,1,2,0:T(8,128)(2,1)S(1)} collective-permute-done((bf16[4,73,4,128]{3,1,2,0:T(8,128)(2,1)S(1)}, bf16[4,73,4,128]{3,1,2,0:T(8,128)(2,1)S(1)}, u32[]{:S(2)}, u32[]{:S(2)}) %collective-permute-start.4) | collective-permute-done | bytes 299040 | tf_op jit(solution)/shard_map/ppermute | solution.py:27
  68.1 2.3 %all_gather.6 = bf16[4,73,8,128]{3,1,2,0:T(8,128)(2,1)S(1)} all-gather(bf16[4,73,4,128]{3,1,2,0:T(8,128)(2,1)S(1)} %collective-permute-done.4), channel_id=1, replica_groups=mesh['grp'=2,'lat'=4,'tm'=2,'chan'=2] {'chan'}, dimensions={2}, use_global_device_ids=true | all-gather | bytes 897024 | tf_op jit(solution)/shard_map/while/body/eval_jaxpr/all_gather | solution.py:57
  70.4 3.7 %collective-permute-start.5 = (bf16[4,73,1,128]{3,1,2,0:T(8,128)(2,1)S(1)}, bf16[4,73,1,128]{3,1,2,0:T(8,128)(2,1)S(1)}, u32[]{:S(2)}, u32[]{:S(2)}) collective-permute-start(bf16[4,73,1,128]{3,1,2,0:T(8,128)(2,1)S(1)} %get-tuple-element.35), channel_id=1, source_target_pairs={{0,4},{4,8},{8,12},{1,5},{5,9},{9,13},{2,6},{6,10},{10,14},{3,7},{... | collective-permute-start | bytes 224264 | tf_op jit(solution)/shard_map/while/body/eval_jaxpr/ppermute | solution.py:15
  74.1 1.5 %collective-permute-start.6 = (bf16[4,73,1,128]{3,1,2,0:T(8,128)(2,1)S(1)}, bf16[4,73,1,128]{3,1,2,0:T(8,128)(2,1)S(1)}, u32[]{:S(2)}, u32[]{:S(2)}) collective-permute-start(bf16[4,73,1,128]{3,1,2,0:T(8,128)(2,1)S(1)} %get-tuple-element.36), channel_id=1, source_target_pairs={{4,0},{8,4},{12,8},{5,1},{9,5},{13,9},{6,2},{10,6},{14,10},{7,3},{... | collective-permute-start | bytes 224264 | tf_op jit(solution)/shard_map/while/body/eval_jaxpr/ppermute | solution.py:17
  76.2 4.3 %collective-permute-done.6 = bf16[4,73,1,128]{3,1,2,0:T(8,128)(2,1)S(1)} collective-permute-done((bf16[4,73,1,128]{3,1,2,0:T(8,128)(2,1)S(1)}, bf16[4,73,1,128]{3,1,2,0:T(8,128)(2,1)S(1)}, u32[]{:S(2)}, u32[]{:S(2)}) %collective-permute-start.6) | collective-permute-done | bytes 74784 | tf_op jit(solution)/shard_map/while/body/eval_jaxpr/ppermute | solution.py:17
  80.5 0.9 select_maximum_fusion
  81.3 0.4 fusion.39
  82.0 0.4 fusion.43
  83.6 0.9 fusion.26
  84.5 3.4 %collective-permute-start.7 = (bf16[4,64,1,128]{3,1,2,0:T(8,128)(2,1)S(1)}, bf16[4,64,1,128]{3,1,2,0:T(8,128)(2,1)S(1)}, u32[]{:S(2)}, u32[]{:S(2)}) collective-permute-start(bf16[4,64,1,128]{3,1,2,0:T(8,128)(2,1)S(1)} %get-tuple-element.37), channel_id=1, source_target_pairs={{0,4},{4,8},{8,12},{1,5},{5,9},{9,13},{2,6},{6,10},{10,14},{3,7},{... | collective-permute-start | bytes 196616 | tf_op jit(solution)/shard_map/while/body/eval_jaxpr/ppermute | solution.py:15
  87.9 1.3 %collective-permute-start.8 = (bf16[4,64,1,128]{3,1,2,0:T(8,128)(2,1)S(1)}, bf16[4,64,1,128]{3,1,2,0:T(8,128)(2,1)S(1)}, u32[]{:S(2)}, u32[]{:S(2)}) collective-permute-start(bf16[4,64,1,128]{3,1,2,0:T(8,128)(2,1)S(1)} %get-tuple-element.38), channel_id=1, source_target_pairs={{4,0},{8,4},{12,8},{5,1},{9,5},{13,9},{6,2},{10,6},{14,10},{7,3},{... | collective-permute-start | bytes 196616 | tf_op jit(solution)/shard_map/while/body/eval_jaxpr/ppermute | solution.py:17
  89.2 0.6 collective-permute-done.7
  89.8 4.3 %collective-permute-done.8 = bf16[4,64,1,128]{3,1,2,0:T(8,128)(2,1)S(1)} collective-permute-done((bf16[4,64,1,128]{3,1,2,0:T(8,128)(2,1)S(1)}, bf16[4,64,1,128]{3,1,2,0:T(8,128)(2,1)S(1)}, u32[]{:S(2)}, u32[]{:S(2)}) %collective-permute-start.8) | collective-permute-done | bytes 65568 | tf_op jit(solution)/shard_map/while/body/eval_jaxpr/ppermute | solution.py:17
  94.0 0.7 select_maximum_fusion.4
  95.5 0.4 convolution_add_fusion.7
  96.3 0.4 convolution_add_fusion.5
  96.7 0.4 convolution_add_fusion.4
  97.1 0.4 convolution_add_fusion.3
  97.5 0.4 convolution_add_fusion.2
  97.9 0.4 fusion.28
  98.3 1.3 %copy.14 = bf16[4,73,8,128]{3,0,1,2:T(4,128)(2,1)} copy(bf16[4,73,8,128]{3,1,2,0:T(8,128)(2,1)S(1)} %fusion.28) | data formatting | bytes 1196032 | tf_op jit(solution)/shard_map/while/body/eval_jaxpr/convert_element_type | solution.py:64
  99.6 17.2 %all-reduce.13.cloned.1.call-done = bf16[4,73,8,128]{3,0,1,2:T(4,128)(2,1)} async-done(((bf16[4,73,8,128]{3,0,1,2:T(4,128)(2,1)}), bf16[4,73,8,128]{3,0,1,2:T(4,128)(2,1)}) %all-reduce.13.cloned.1.call-update) | async-done | bytes 598032
  116.8 1.1 constant_dynamic-slice_fusion
  118.1 1.1 copy.16
  (48 shorter events, 6.1 us)
Async XLA Ops:
  6.5 10.2 %copy-start = (bf16[8,3,3,64,73]{4,3,2,1,0:T(8,128)(2,1)S(1)}, bf16[8,3,3,64,73]{4,3,2,1,0:T(8,128)(2,1)}, u32[]{:S(2)}) copy-start(bf16[8,3,3,64,73]{4,3,2,1,0:T(8,128)(2,1)} %param.11) | copy-start | bytes 2018308
  6.5 10.5 %copy-start.2 = (bf16[1,64,8,128]{3,2,1,0:T(8,128)(2,1)S(1)}, bf16[1,64,8,128]{3,2,1,0:T(8,128)(2,1)}, u32[]{:S(2)}) copy-start(bf16[1,64,8,128]{3,2,1,0:T(8,128)(2,1)} %param.8) | copy-start | bytes 393220
  6.5 48.6 %all-reduce.11.cloned.1.call-start = ((), (), s32[]{:S(2)}) async-start(), calls=%async_computation | async-start | bytes 1196032
  6.6 10.5 %collective-permute-start.1 = (bf16[4,73,1,128]{3,1,2,0:T(8,128)(2,1)S(1)}, bf16[4,73,1,128]{3,1,2,0:T(8,128)(2,1)S(1)}, u32[]{:S(2)}, u32[]{:S(2)}) collective-permute-start(bf16[4,73,1,128]{3,1,2,0:T(8,128)(2,1)S(1)} %slice.294), channel_id=1, source_target_pairs={{4,0},{8,4},{12,8},{5,1},{9,5},{13,9},{6,2},{10,6},{14,10},{7,3},{... | collective-permute-start | bytes 224264 | tf_op jit(solution)/shard_map/while/body/eval_jaxpr/ppermute | solution.py:17
  8.0 9.1 %collective-permute-start = (bf16[4,73,1,128]{3,1,2,0:T(8,128)(2,1)S(1)}, bf16[4,73,1,128]{3,1,2,0:T(8,128)(2,1)S(1)}, u32[]{:S(2)}, u32[]{:S(2)}) collective-permute-start(bf16[4,73,1,128]{3,1,2,0:T(8,128)(2,1)S(1)} %slice.294), channel_id=1, source_target_pairs={{0,4},{4,8},{8,12},{1,5},{5,9},{9,13},{2,6},{6,10},{10,14},{3,7},{... | collective-permute-start | bytes 224264 | tf_op jit(solution)/shard_map/while/body/eval_jaxpr/ppermute | solution.py:15
  20.9 6.2 %collective-permute-start.2 = (bf16[4,64,1,128]{3,1,2,0:T(8,128)(2,1)S(1)}, bf16[4,64,1,128]{3,1,2,0:T(8,128)(2,1)S(1)}, u32[]{:S(2)}, u32[]{:S(2)}) collective-permute-start(bf16[4,64,1,128]{3,1,2,0:T(8,128)(2,1)S(1)} %get-tuple-element.39), channel_id=1, source_target_pairs={{0,4},{4,8},{8,12},{1,5},{5,9},{9,13},{2,6},{6,10},{10,14},{3,7},{... | collective-permute-start | bytes 196616 | tf_op jit(solution)/shard_map/while/body/eval_jaxpr/ppermute | solution.py:15
  24.9 6.2 %collective-permute-start.3 = (bf16[4,64,1,128]{3,1,2,0:T(8,128)(2,1)S(1)}, bf16[4,64,1,128]{3,1,2,0:T(8,128)(2,1)S(1)}, u32[]{:S(2)}, u32[]{:S(2)}) collective-permute-start(bf16[4,64,1,128]{3,1,2,0:T(8,128)(2,1)S(1)} %get-tuple-element.48), channel_id=1, source_target_pairs={{4,0},{8,4},{12,8},{5,1},{9,5},{13,9},{6,2},{10,6},{14,10},{7,3},{... | collective-permute-start | bytes 196616 | tf_op jit(solution)/shard_map/while/body/eval_jaxpr/ppermute | solution.py:17
  35.3 1.4 %copy-start.3 = (s32[1,1,4]{2,1,0:T(1,128)S(1)}, s32[1,1,4]{2,1,0:T(1,128)}, u32[]{:S(2)}) copy-start(s32[1,1,4]{2,1,0:T(1,128)} %param.7) | copy-start | bytes 52
  35.3 1.6 %copy-start.4 = (u32[32]{0:T(128)S(1)}, u32[32]{0:T(128)}, u32[]{:S(2)}) copy-start(u32[32]{0:T(128)} %constant.69) | copy-start | bytes 388
  35.3 20.9 %copy-start.1 = (bf16[4,1,73,4,128]{4,3,2,1,0:T(4,128)(2,1)S(1)}, bf16[4,1,73,4,128]{4,3,2,1,0:T(4,128)(2,1)}, u32[]{:S(2)}) copy-start(bf16[4,1,73,4,128]{4,3,2,1,0:T(4,128)(2,1)} %param.6) | copy-start | bytes 897028
  36.7 80.2 %all-reduce.13.cloned.1.call-start = ((), (), s32[]{:S(2)}) async-start(), calls=%async_computation.1 | async-start | bytes 1196032
  56.4 11.7 %collective-permute-start.4 = (bf16[4,73,4,128]{3,1,2,0:T(8,128)(2,1)S(1)}, bf16[4,73,4,128]{3,1,2,0:T(8,128)(2,1)S(1)}, u32[]{:S(2)}, u32[]{:S(2)}) collective-permute-start(bf16[4,73,4,128]{3,1,2,0:T(8,128)(2,1)S(1)} %fusion.60), channel_id=1, source_target_pairs={{2,0},{3,1},{6,4},{7,5},{10,8},{11,9},{14,12},{15,13},{18,16},{19,... | collective-permute-start | bytes 897032 | tf_op jit(solution)/shard_map/ppermute | solution.py:27
  70.4 5.8 %collective-permute-start.5 = (bf16[4,73,1,128]{3,1,2,0:T(8,128)(2,1)S(1)}, bf16[4,73,1,128]{3,1,2,0:T(8,128)(2,1)S(1)}, u32[]{:S(2)}, u32[]{:S(2)}) collective-permute-start(bf16[4,73,1,128]{3,1,2,0:T(8,128)(2,1)S(1)} %get-tuple-element.35), channel_id=1, source_target_pairs={{0,4},{4,8},{8,12},{1,5},{5,9},{9,13},{2,6},{6,10},{10,14},{3,7},{... | collective-permute-start | bytes 224264 | tf_op jit(solution)/shard_map/while/body/eval_jaxpr/ppermute | solution.py:15
  74.1 6.3 %collective-permute-start.6 = (bf16[4,73,1,128]{3,1,2,0:T(8,128)(2,1)S(1)}, bf16[4,73,1,128]{3,1,2,0:T(8,128)(2,1)S(1)}, u32[]{:S(2)}, u32[]{:S(2)}) collective-permute-start(bf16[4,73,1,128]{3,1,2,0:T(8,128)(2,1)S(1)} %get-tuple-element.36), channel_id=1, source_target_pairs={{4,0},{8,4},{12,8},{5,1},{9,5},{13,9},{6,2},{10,6},{14,10},{7,3},{... | collective-permute-start | bytes 224264 | tf_op jit(solution)/shard_map/while/body/eval_jaxpr/ppermute | solution.py:17
  84.5 5.3 %collective-permute-start.7 = (bf16[4,64,1,128]{3,1,2,0:T(8,128)(2,1)S(1)}, bf16[4,64,1,128]{3,1,2,0:T(8,128)(2,1)S(1)}, u32[]{:S(2)}, u32[]{:S(2)}) collective-permute-start(bf16[4,64,1,128]{3,1,2,0:T(8,128)(2,1)S(1)} %get-tuple-element.37), channel_id=1, source_target_pairs={{0,4},{4,8},{8,12},{1,5},{5,9},{9,13},{2,6},{6,10},{10,14},{3,7},{... | collective-permute-start | bytes 196616 | tf_op jit(solution)/shard_map/while/body/eval_jaxpr/ppermute | solution.py:15
  87.9 6.2 %collective-permute-start.8 = (bf16[4,64,1,128]{3,1,2,0:T(8,128)(2,1)S(1)}, bf16[4,64,1,128]{3,1,2,0:T(8,128)(2,1)S(1)}, u32[]{:S(2)}, u32[]{:S(2)}) collective-permute-start(bf16[4,64,1,128]{3,1,2,0:T(8,128)(2,1)S(1)} %get-tuple-element.38), channel_id=1, source_target_pairs={{4,0},{8,4},{12,8},{5,1},{9,5},{13,9},{6,2},{10,6},{14,10},{7,3},{... | collective-permute-start | bytes 196616 | tf_op jit(solution)/shard_map/while/body/eval_jaxpr/ppermute | solution.py:17
Sparse Core Ops, SparseCore 0:
  36.8 18.3 all-reduce.10
  99.8 17.0 all-reduce.12
where the time goes:
time: 126 us
  waiting for transfers between devices  57.9 us (46%)
  starting transfers between devices  23.4 us (19%)
  between operations  16.5 us (13%)
  matrix products  13.4 us (11%)
  local copies, waits for them, and re-layouts  8.96 us (7%)
  other arithmetic  3.43 us (3%)
  blocking collectives  2.26 us (2%)
    unnamed x4, waiting for transfers between devices  34.2 us
    ppermute x4, starting transfers between devices, with_halo(): lax.ppermute(tail, axis, [(i, (i + 1) % count) for i in range(ends)])  16.6 us
    dot_general x36, matrix products, local_conv(): jnp.einsum('ij,fjhw->fihw', kernel[row_off, col_off], shifted, preferred_...  13.4 us
    ppermute x4, waiting for transfers between devices, with_halo(): lax.ppermute(head, axis, [((i + 1) % count, i) for i in range(ends)])  12.5 us
    ppermute x1, waiting for transfers between devices, from_behind(): return lax.ppermute(block, axis, route)  10.4 us
    ppermute x4, starting transfers between devices, with_halo(): lax.ppermute(head, axis, [((i + 1) % count, i) for i in range(ends)])  5.48 us
    concatenate x4, other arithmetic, with_halo(): jnp.concatenate([lax.ppermute(tail, axis, [(i, (i + 1) % count) for i in...  3.13 us
    unnamed x13, local copies, waits for them, and re-layouts  2.81 us
  transfers between devices with their start and end apart: 11, of which 8 were waited for; matrix products, arithmetic and copies ran while one was open for 3% of the time, Pallas kernels for 0%

commit v1 on v0

v1 whole, which is shorter than its diff:
```python
import functools

import jax
import jax.numpy as jnp
from jax import lax
from jax.experimental import pallas as pl
from jax.experimental.pallas import tpu as pltpu
from jax.sharding import PartitionSpec as P


def swap_chan(block):
    return lax.ppermute(block, "chan", [(0, 1), (1, 0)])


def swap_lat(block):
    bands = lax.axis_size("lat")
    pairs = []
    for band in range(bands - 1):
        pairs += [(2 * band + 1, 2 * band + 2), (2 * band + 2, 2 * band + 1)]
    return lax.ppermute(block, ("lat", "chan"), pairs)


def to_earlier(block):
    count = lax.axis_size("tm")
    return lax.ppermute(block, "tm", [(i, i - 1) for i in range(1, count)])


def lane_shift(values, step):
    lanes = lax.broadcasted_iota(jnp.int32, values.shape, 1)
    edge = 0 if step == 1 else values.shape[1] - 1
    rolled = pltpu.roll(values, step % values.shape[1], 1)
    return jnp.where(lanes == edge, 0.0, rolled)


def step_kernel(
    dims, chan_ref, mask_ref, halo_ref, outer_ref, inner_ref, other_ref, innov_ref,
    slope_own_ref, slope_other_ref, slope_halo_ref,
    out_own_ref, out_other_ref, in_own_ref, in_other_ref,
    result_ref, field, hidden_own, hidden_other,
):
    fronts, states, pitch, half, cells = dims
    chan = chan_ref[0]
    rows = 4
    field[...] = jnp.zeros_like(field)
    for spot, piece in enumerate((halo_ref, outer_ref, inner_ref, other_ref)):
        place = spot + chan * (3 - 2 * spot)
        for i in range(2):
            start = pl.multiple_of(place * (2 * pitch) + i * pitch, 16)
            field[pl.ds(start, states), :] = piece[i]

    for j in range(rows + 2):
        near = field[j * pitch:(j + 3) * pitch, :]
        lat_row = jnp.clip(4 * chan + j - 1, 0, 7)
        for kernel_ref, slope_ref, hidden, part in (
            (out_own_ref, slope_own_ref, hidden_own, 0),
            (out_other_ref, slope_other_ref, hidden_other, 1),
        ):
            taps = jnp.dot(kernel_ref[...], near, preferred_element_type=jnp.float32)
            slope = slope_ref[lat_row].astype(jnp.float32)
            if j in (0, rows + 1):
                outside = chan == (0 if j == 0 else 1)
                edge = slope_halo_ref[(1 - part) * half:(2 - part) * half, :].astype(jnp.float32)
                slope = jnp.where(outside, edge, slope)
            for f in range(fronts):
                lanes = slice(f * cells, (f + 1) * cells)
                total = (
                    taps[half:2 * half, lanes]
                    + lane_shift(taps[0:half, lanes], -1)
                    + lane_shift(taps[2 * half:3 * half, lanes], 1)
                )
                hidden[j * half:(j + 1) * half, lanes] = (slope * total).astype(jnp.bfloat16)

    for h in range(rows):
        taps = jnp.dot(
            in_own_ref[...], hidden_own[h * half:(h + 3) * half, :], preferred_element_type=jnp.float32
        ) + jnp.dot(
            in_other_ref[...], hidden_other[h * half:(h + 3) * half, :], preferred_element_type=jnp.float32
        )
        before = field[(h + 2) * pitch:(h + 3) * pitch, :].astype(jnp.float32)
        for f in range(fronts):
            lanes = slice(f * cells, (f + 1) * cells)
            total = (
                before[:, lanes]
                + taps[pitch:2 * pitch, lanes]
                + lane_shift(taps[0:pitch, lanes], -1)
                + lane_shift(taps[2 * pitch:3 * pitch, lanes], 1)
            )
            result_ref[pl.ds(f * states * rows + h, states, stride=rows), :] = total[:states]

    tile = lax.broadcasted_iota(jnp.int32, (1, cells), 1) // 32
    seen = jnp.zeros((1, cells), jnp.float32)
    for t in range(cells // 32):
        seen = jnp.where(tile == t, mask_ref[t].astype(jnp.float32), seen)
    result_ref[...] += innov_ref[...].astype(jnp.float32) * seen


def per_device(innovations, obs_mask, slopes, layer_of, weight_in, weight_out):
    fronts, _, states, rows, cells = innovations.shape
    half = slopes.shape[1]
    pitch = -(-states // 16) * 16
    owners = lax.axis_size("tm")
    chan = lax.axis_index("chan")

    seen = jnp.repeat(obs_mask[0, 0], 32).astype(jnp.bfloat16)

    def to_send(adjoint):
        field = adjoint.transpose(2, 1, 0, 3).reshape(rows, states, fronts * cells)
        return (
            lax.dynamic_slice_in_dim(field, 2 * chan, 2),
            lax.dynamic_slice_in_dim(field, 2 - 2 * chan, 2),
        )

    outer, inner = to_send(innovations[:, 0] * seen)
    layer = layer_of[lax.axis_index("tm")]
    k_out = lax.dynamic_index_in_dim(weight_out, layer, 0, keepdims=False)
    k_in = lax.dynamic_index_in_dim(weight_in, layer, 0, keepdims=False)
    lap = ((0, 0),) * 3 + ((0, pitch - states),)
    out_own = jnp.pad(k_out[::-1].transpose(1, 2, 0, 3), lap).reshape(3 * half, 3 * pitch)
    in_own = jnp.pad(k_in[::-1].transpose(0, 3, 1, 2), lap).reshape(3 * half, 3 * pitch).T
    slope_own = slopes[0].transpose(1, 0, 2)
    out_other = swap_chan(out_own)
    in_other = swap_chan(in_own)
    slope_other = swap_chan(slope_own)
    edge = jnp.concatenate([slope_own, slope_other], axis=1)
    edge = lax.dynamic_index_in_dim(edge, 7 * chan, 0, keepdims=False)
    slope_halo = swap_lat(edge)

    vm = pl.BlockSpec(memory_space=pltpu.VMEM)
    sm = pl.BlockSpec(memory_space=pltpu.SMEM)
    step = pl.pallas_call(
        functools.partial(step_kernel, (fronts, states, pitch, half, cells)),
        out_shape=jax.ShapeDtypeStruct((fronts * states * rows, cells), jnp.float32),
        in_specs=[sm, sm] + [vm] * 12,
        out_specs=vm,
        scratch_shapes=[
            pltpu.VMEM((8 * pitch, fronts * cells), jnp.bfloat16),
            pltpu.VMEM((6 * half, fronts * cells), jnp.bfloat16),
            pltpu.VMEM((6 * half, fronts * cells), jnp.bfloat16),
        ],
        compiler_params=pltpu.CompilerParams(vmem_limit_bytes=32 << 20),
    )
    for hop in range(1, owners):
        outer_in = to_earlier(outer)
        inner_in = to_earlier(inner)
        halo = swap_lat(outer_in)
        other = swap_chan(inner_in)
        result = step(
            chan.reshape(1), obs_mask[0, 0], halo, outer_in, inner_in, other,
            innovations.reshape(fronts * states * rows, cells),
            slope_own, slope_other, slope_halo, out_own, out_other, in_own, in_other,
        )
        if hop + 1 < owners:
            outer, inner = to_send(result.reshape(innovations.shape)[:, 0].astype(jnp.bfloat16))
    return result.reshape(innovations.shape)


def solution(mesh):
    return jax.shard_map(
        per_device,
        mesh=mesh,
        in_specs=(
            P(None, ("grp", "tm"), None, ("lat", "chan"), None),
            P(("grp", "tm"), ("lat", "chan"), None),
            P(("grp", "tm"), "chan", "lat", None),
            P(),
            P(None, None, None, None, "chan"),
            P(None, None, None, "chan", None),
        ),
        out_specs=P(None, ("grp", "tm"), None, ("lat", "chan"), None),
        check_vma=False,
    )
```

time: 126 us -> 28.9 us (0.23)
  the two profiles are of different devices: /device:TPU:0 before, /device:TPU:1 now
where the time goes in v1:
time: 28.9 us; the launch traced here: 28.7 us
  starting transfers between devices  12.6 us (44%)
  waiting for transfers between devices  5.29 us (18%)
  local copies, waits for them, and re-layouts  3.91 us (14%)
  Pallas kernels  2.97 us (10%)
  between operations  2.16 us (7%)
  other arithmetic  1.77 us (6%)
    ppermute x2, starting transfers between devices, swap_lat(): return lax.ppermute(block, ('lat', 'chan'), pairs)  8.23 us
    ppermute x2, waiting for transfers between devices, to_earlier(): return lax.ppermute(block, 'tm', [(i, i - 1) for i in range(1, count)])  3.62 us
    pallas_call x1, Pallas kernels, per_device(): step(chan.reshape(1), obs_mask[0, 0], halo, outer_in, inner_in, other, in...  2.97 us
    ppermute x2, starting transfers between devices, to_earlier(): return lax.ppermute(block, 'tm', [(i, i - 1) for i in range(1, count)])  2.58 us
    ppermute x4, starting transfers between devices, swap_chan(): return lax.ppermute(block, 'chan', [(0, 1), (1, 0)])  1.76 us
    ppermute x2, waiting for transfers between devices, swap_lat(): return lax.ppermute(block, ('lat', 'chan'), pairs)  1.66 us
    unnamed x11, local copies, waits for them, and re-layouts  1.37 us
    transpose x1, other arithmetic, to_send(): field = adjoint.transpose(2, 1, 0, 3).reshape(rows, states, fronts * cells)  1.1 us
  transfers between devices with their start and end apart: 8, of which 3 were waited for; matrix products, arithmetic and copies ran while one was open for 16% of the time, Pallas kernels for 0%

profile of v1, /device:TPU:1, one launch (start us, length us, event | category | flops | bytes accessed | tf_op | source)
XLA Modules:
  0.0 28.7 jit_solution(14885383495002067166)
XLA Ops:
  0.0 0.0 copy-start
  0.0 1.0 %copy.25 = bf16[1,64,8,128]{3,1,2,0:T(8,128)(2,1)S(1)} copy(bf16[1,64,8,128]{3,2,1,0:T(8,128)(2,1)} %param.8) | data formatting | bytes 262144 | tf_op args[2]
  1.0 0.1 collective-permute-start.4
  1.1 0.7 %bitcast_convert_fusion = bf16[4]{0:T(256)(128)(2,1)S(1)} fusion(s32[1,1,4]{2,1,0:T(1,128)} %param.7), kind=kLoop, calls=%fused_computation.13 | loop fusion | flops 4 | bytes 24 | tf_op jit(solution)/shard_map/convert_element_type | solution.py:104
  1.8 0.1 broadcast_in_dim.4
  1.9 0.1 convert_element_type.15
  2.0 0.0 copy-start.3
  2.0 1.1 %fusion = bf16[4,73,4,128]{3,0,1,2:T(4,128)(2,1)S(1)} fusion(bf16[4,1,73,4,128]{4,3,2,1,0:T(4,128)(2,1)} %param.6, bf16[128]{0:T(256)(128)(2,1)S(1)} %convert_element_type.15), kind=kLoop, calls=%fused_computation.1 | loop fusion | flops 149504 | bytes 598272 | tf_op jit(solution)/shard_map/transpose | solution.py:107
  3.1 0.1 copy.18
  3.2 0.1 reshape.31
  3.4 1.3 %collective-permute-start.2 = (bf16[2,73,512]{2,1,0:T(8,128)(2,1)S(1)}, bf16[2,73,512]{2,1,0:T(8,128)(2,1)S(1)}, u32[]{:S(2)}, u32[]{:S(2)}) collective-permute-start(bf16[2,73,512]{2,1,0:T(8,128)(2,1)S(1)} %get-tuple-element.5), channel_id=1, source_target_pairs={{2,0},{3,1},{6,4},{7,5},{10,8},{11,9},{14,12},{15,13},{18,16},{19,... | collective-permute-start | bytes 448520 | tf_op jit(solution)/shard_map/ppermute | solution.py:25
  4.7 1.3 %collective-permute-start = (bf16[2,73,512]{2,1,0:T(8,128)(2,1)S(1)}, bf16[2,73,512]{2,1,0:T(8,128)(2,1)S(1)}, u32[]{:S(2)}, u32[]{:S(2)}) collective-permute-start(bf16[2,73,512]{2,1,0:T(8,128)(2,1)S(1)} %get-tuple-element.6), channel_id=1, source_target_pairs={{2,0},{3,1},{6,4},{7,5},{10,8},{11,9},{14,12},{15,13},{18,16},{19,... | collective-permute-start | bytes 448520 | tf_op jit(solution)/shard_map/ppermute | solution.py:25
  6.0 0.0 copy-done.3
  6.0 0.6 %dynamic_slice.24 = s32[1]{0:T(128)} dynamic-slice(s32[2]{0:T(128)S(1)} %copy-done.3, s32[]{:T(128)S(6)} %select_n.22), dynamic_slice_sizes={1} | dynamic-slice | bytes 12 | tf_op jit(solution)/shard_map/dynamic_slice | solution.py:114
  8.5 0.0 copy-done
  8.6 0.2 copy.23
  8.8 0.1 pad.8.clone
  8.9 0.0 copy-start.1
  8.9 0.0 copy-start.2
  8.9 0.2 reshape.32
  9.1 0.5 %collective-permute-start.7 = (bf16[240,192]{1,0:T(8,128)(2,1)S(1)}, bf16[240,192]{1,0:T(8,128)(2,1)S(1)}, u32[]{:S(2)}, u32[]{:S(2)}) collective-permute-start(bf16[240,192]{1,0:T(8,128)(2,1)S(1)} %bitcast.36), channel_id=1, source_target_pairs={{0,1},{1,0},{2,3},{3,2},{4,5},{5,4},{6,7},{7,6},{8,9},{9,8},{10,11... | collective-permute-start | bytes 276488 | tf_op jit(solution)/shard_map/ppermute | solution.py:12
  9.6 0.9 %dynamic-slice_bitcast_fusion.1 = bf16[3,3,64,73]{3,2,1,0:T(8,128)(2,1)S(1)} fusion(bf16[8,3,3,64,73]{4,3,2,1,0:T(8,128)(2,1)} %param.11, s32[]{:T(128)S(6)} %select_n.23), kind=kLoop, calls=%fused_computation.7 | loop fusion | bytes 168196 | tf_op jit(solution)/shard_map/jit(dynamic_index_in_dim)/squeeze | solution.py:115
  10.6 1.2 %collective-permute-done.2.inner_ref = bf16[2,73,512]{2,1,0:T(8,128)(2,1)S(1)} collective-permute-done((bf16[2,73,512]{2,1,0:T(8,128)(2,1)S(1)}, bf16[2,73,512]{2,1,0:T(8,128)(2,1)S(1)}, u32[]{:S(2)}, u32[]{:S(2)}) %collective-permute-start.2) | collective-permute-done | bytes 149536 | tf_op jit(solution)/shard_map/ppermute | solution.py:25
  11.7 1.1 %collective-permute-start.3 = (bf16[2,73,512]{2,1,0:T(8,128)(2,1)S(1)}, bf16[2,73,512]{2,1,0:T(8,128)(2,1)S(1)}, u32[]{:S(2)}, u32[]{:S(2)}) collective-permute-start(bf16[2,73,512]{2,1,0:T(8,128)(2,1)S(1)} %collective-permute-done.2.inner_ref), channel_id=1, source_target_pairs={{0,1},{1,0},{2,3},{3,2},{4,5},{5,4},{6,7},{7,6},{8,9},{9,8},{10,11... | collective-permute-start | bytes 448520 | tf_op jit(solution)/shard_map/ppermute | solution.py:12
  12.8 2.5 %collective-permute-done.outer_ref = bf16[2,73,512]{2,1,0:T(8,128)(2,1)S(1)} collective-permute-done((bf16[2,73,512]{2,1,0:T(8,128)(2,1)S(1)}, bf16[2,73,512]{2,1,0:T(8,128)(2,1)S(1)}, u32[]{:S(2)}, u32[]{:S(2)}) %collective-permute-start) | collective-permute-done | bytes 149536 | tf_op jit(solution)/shard_map/ppermute | solution.py:25
  15.2 4.7 %collective-permute-start.1 = (bf16[2,73,512]{2,1,0:T(8,128)(2,1)S(1)}, bf16[2,73,512]{2,1,0:T(8,128)(2,1)S(1)}, u32[]{:S(2)}, u32[]{:S(2)}) collective-permute-start(bf16[2,73,512]{2,1,0:T(8,128)(2,1)S(1)} %collective-permute-done.outer_ref), channel_id=1, source_target_pairs={{1,4},{4,1},{5,8},{8,5},{9,12},{12,9},{3,6},{6,3},{7,10},{10,7},{1... | collective-permute-start | bytes 448520 | tf_op jit(solution)/shard_map/ppermute | solution.py:20
  19.9 0.1 copy.22
  20.1 0.1 pad.7.clone
  20.2 0.1 reshape.28.out_own_ref
  20.3 0.1 collective-permute-start.6
  20.4 0.0 collective-permute-done.4.slope_other_ref
  20.4 3.6 %collective-permute-start.5 = (bf16[128,128]{1,0:T(8,128)(2,1)S(1)}, bf16[128,128]{1,0:T(8,128)(2,1)S(1)}, u32[]{:S(2)}, u32[]{:S(2)}) collective-permute-start(bf16[128,128]{1,0:T(8,128)(2,1)S(1)} %fusion.2), channel_id=1, source_target_pairs={{1,4},{4,1},{5,8},{8,5},{9,12},{12,9},{3,6},{6,3},{7,10},{10,7},{1... | collective-permute-start | bytes 98312 | tf_op jit(solution)/shard_map/ppermute | solution.py:20
  24.0 0.0 collective-permute-done.7.in_other_ref
  24.0 0.0 collective-permute-done.6.out_other_ref
  24.0 1.7 %collective-permute-done.5.slope_halo_ref = bf16[128,128]{1,0:T(8,128)(2,1)S(1)} collective-permute-done((bf16[128,128]{1,0:T(8,128)(2,1)S(1)}, bf16[128,128]{1,0:T(8,128)(2,1)S(1)}, u32[]{:S(2)}, u32[]{:S(2)}) %collective-permute-start.5) | collective-permute-done | bytes 32800 | tf_op jit(solution)/shard_map/ppermute | solution.py:20
  25.7 0.0 collective-permute-done.3.other_ref
  25.7 0.0 collective-permute-done.1.halo_ref
  25.7 0.0 copy-done.1
  25.7 0.0 copy-done.2
  25.7 3.0 %shard_map.64 = f32[1168,128]{1,0:T(8,128)} custom-call(s32[1]{0:T(128)} %bitcast.chan_ref, s32[4]{0:T(128)S(1)} %bitcast.38, bf16[2,73,512]{2,1,0:T(8,128)(2,1)S(1)} %collective-permute-done.1.halo_ref, bf16[2,73,512]{2,1,0:T(8,128)(2,1)S(1)} %collective-permute-done.outer_ref, bf16[2,73,512]{2,1,0:T(8,128)(2,1)S(1)} %collective-permute-done.2.inner_ref, ...), custom_call_target="tpu_custom_call" | custom-call | tf_op jit(solution)/shard_map/pallas_call | solution.py:147
  (5 shorter events, 0.1 us)
Async XLA Ops:
  0.0 8.5 %copy-start = (bf16[8,3,3,73,64]{3,4,2,1,0:T(8,128)(2,1)S(1)}, bf16[8,3,3,73,64]{3,4,2,1,0:T(8,128)(2,1)}, u32[]{:S(2)}) copy-start(bf16[8,3,3,73,64]{3,4,2,1,0:T(8,128)(2,1)} %param.10) | copy-start | bytes 2018308
  1.0 19.4 %collective-permute-start.4 = (bf16[8,64,128]{2,1,0:T(8,128)(2,1)S(1)}, bf16[8,64,128]{2,1,0:T(8,128)(2,1)S(1)}, u32[]{:S(2)}, u32[]{:S(2)}) collective-permute-start(bf16[8,64,128]{2,1,0:T(8,128)(2,1)S(1)} %bitcast.33), channel_id=1, source_target_pairs={{0,1},{1,0},{2,3},{3,2},{4,5},{5,4},{6,7},{7,6},{8,9},{9,8},{10,11... | collective-permute-start | bytes 393224 | tf_op jit(solution)/shard_map/ppermute | solution.py:12
  2.0 4.0 %copy-start.3 = (s32[2]{0:T(128)S(1)}, s32[2]{0:T(128)}, u32[]{:S(2)}) copy-start(s32[2]{0:T(128)} %param.9) | copy-start | bytes 28
  3.4 8.4 %collective-permute-start.2 = (bf16[2,73,512]{2,1,0:T(8,128)(2,1)S(1)}, bf16[2,73,512]{2,1,0:T(8,128)(2,1)S(1)}, u32[]{:S(2)}, u32[]{:S(2)}) collective-permute-start(bf16[2,73,512]{2,1,0:T(8,128)(2,1)S(1)} %get-tuple-element.5), channel_id=1, source_target_pairs={{2,0},{3,1},{6,4},{7,5},{10,8},{11,9},{14,12},{15,13},{18,16},{19,... | collective-permute-start | bytes 448520 | tf_op jit(solution)/shard_map/ppermute | solution.py:25
  4.7 10.6 %collective-permute-start = (bf16[2,73,512]{2,1,0:T(8,128)(2,1)S(1)}, bf16[2,73,512]{2,1,0:T(8,128)(2,1)S(1)}, u32[]{:S(2)}, u32[]{:S(2)}) collective-permute-start(bf16[2,73,512]{2,1,0:T(8,128)(2,1)S(1)} %get-tuple-element.6), channel_id=1, source_target_pairs={{2,0},{3,1},{6,4},{7,5},{10,8},{11,9},{14,12},{15,13},{18,16},{19,... | collective-permute-start | bytes 448520 | tf_op jit(solution)/shard_map/ppermute | solution.py:25
  8.9 16.8 %copy-start.1 = (bf16[4,1,73,4,128]{4,3,2,1,0:T(4,128)(2,1)S(1)}, bf16[4,1,73,4,128]{4,3,2,1,0:T(4,128)(2,1)}, u32[]{:S(2)}) copy-start(bf16[4,1,73,4,128]{4,3,2,1,0:T(4,128)(2,1)} %param.6) | copy-start | bytes 897028
  8.9 16.8 %copy-start.2 = (s32[1,1,4]{2,1,0:T(1,128)S(1)}, s32[1,1,4]{2,1,0:T(1,128)}, u32[]{:S(2)}) copy-start(s32[1,1,4]{2,1,0:T(1,128)} %param.7) | copy-start | bytes 52
  9.1 14.9 %collective-permute-start.7 = (bf16[240,192]{1,0:T(8,128)(2,1)S(1)}, bf16[240,192]{1,0:T(8,128)(2,1)S(1)}, u32[]{:S(2)}, u32[]{:S(2)}) collective-permute-start(bf16[240,192]{1,0:T(8,128)(2,1)S(1)} %bitcast.36), channel_id=1, source_target_pairs={{0,1},{1,0},{2,3},{3,2},{4,5},{5,4},{6,7},{7,6},{8,9},{9,8},{10,11... | collective-permute-start | bytes 276488 | tf_op jit(solution)/shard_map/ppermute | solution.py:12
  11.7 14.0 %collective-permute-start.3 = (bf16[2,73,512]{2,1,0:T(8,128)(2,1)S(1)}, bf16[2,73,512]{2,1,0:T(8,128)(2,1)S(1)}, u32[]{:S(2)}, u32[]{:S(2)}) collective-permute-start(bf16[2,73,512]{2,1,0:T(8,128)(2,1)S(1)} %collective-permute-done.2.inner_ref), channel_id=1, source_target_pairs={{0,1},{1,0},{2,3},{3,2},{4,5},{5,4},{6,7},{7,6},{8,9},{9,8},{10,11... | collective-permute-start | bytes 448520 | tf_op jit(solution)/shard_map/ppermute | solution.py:12
  15.2 10.4 %collective-permute-start.1 = (bf16[2,73,512]{2,1,0:T(8,128)(2,1)S(1)}, bf16[2,73,512]{2,1,0:T(8,128)(2,1)S(1)}, u32[]{:S(2)}, u32[]{:S(2)}) collective-permute-start(bf16[2,73,512]{2,1,0:T(8,128)(2,1)S(1)} %collective-permute-done.outer_ref), channel_id=1, source_target_pairs={{1,4},{4,1},{5,8},{8,5},{9,12},{12,9},{3,6},{6,3},{7,10},{10,7},{1... | collective-permute-start | bytes 448520 | tf_op jit(solution)/shard_map/ppermute | solution.py:20
  20.3 3.7 %collective-permute-start.6 = (bf16[192,240]{1,0:T(8,128)(2,1)S(1)}, bf16[192,240]{1,0:T(8,128)(2,1)S(1)}, u32[]{:S(2)}, u32[]{:S(2)}) collective-permute-start(bf16[192,240]{1,0:T(8,128)(2,1)S(1)} %reshape.28.out_own_ref), channel_id=1, source_target_pairs={{0,1},{1,0},{2,3},{3,2},{4,5},{5,4},{6,7},{7,6},{8,9},{9,8},{10,11... | collective-permute-start | bytes 276488 | tf_op jit(solution)/shard_map/ppermute | solution.py:12
  20.4 5.2 %collective-permute-start.5 = (bf16[128,128]{1,0:T(8,128)(2,1)S(1)}, bf16[128,128]{1,0:T(8,128)(2,1)S(1)}, u32[]{:S(2)}, u32[]{:S(2)}) collective-permute-start(bf16[128,128]{1,0:T(8,128)(2,1)S(1)} %fusion.2), channel_id=1, source_target_pairs={{1,4},{4,1},{5,8},{8,5},{9,12},{12,9},{3,6},{6,3},{7,10},{10,7},{1... | collective-permute-start | bytes 98312 | tf_op jit(solution)/shard_map/ppermute | solution.py:20

commit v2 on v1

v2 whole, which is shorter than its diff:
```python
import functools

import jax
import jax.numpy as jnp
from jax import lax
from jax.experimental import pallas as pl
from jax.experimental.pallas import tpu as pltpu
from jax.sharding import PartitionSpec as P

VMEM = pl.BlockSpec(memory_space=pltpu.VMEM)
HBM = pl.BlockSpec(memory_space=pltpu.HBM)


def swap_chan(block):
    return lax.ppermute(block, "chan", [(0, 1), (1, 0)])


def swap_lat(block):
    bands, groups = lax.axis_size("lat"), lax.axis_size("grp")
    last = 2 * bands - 1
    pairs = []
    for group in range(groups):
        for i in range(1, last, 2):
            pairs += [(group, i, group, i + 1), (group, i + 1, group, i)]
        mate = group ^ 1 if group ^ 1 < groups else group
        pairs += [(group, 0, mate, 0), (group, last, mate, last)]
    route = [(g * 2 * bands + i, m * 2 * bands + k) for g, i, m, k in pairs]
    return lax.ppermute(block, ("grp", "lat", "chan"), route)


def to_earlier(block):
    count = lax.axis_size("tm")
    return lax.ppermute(block, "tm", [(i, (i - 1) % count) for i in range(count)])


def lane_shift(values, step):
    lanes = lax.broadcasted_iota(jnp.int32, values.shape, 1)
    edge = 0 if step == 1 else values.shape[1] - 1
    return jnp.where(lanes == edge, 0.0, pltpu.roll(values, step % values.shape[1], 1))


def tile_mask(mask_ref, cells):
    tile = lax.broadcasted_iota(jnp.int32, (1, cells), 1) // 32
    seen = jnp.zeros((1, cells), jnp.float32)
    for t in range(cells // 32):
        seen = jnp.where(tile == t, mask_ref[t].astype(jnp.float32), seen)
    return seen


def split_rows(dims, wide, outer_ref, inner_ref):
    fronts, states, cells = dims
    chan = lax.axis_index("chan")
    for piece, first in ((outer_ref, 2 * chan), (inner_ref, 2 - 2 * chan)):
        for i in range(2):
            for f in range(fronts):
                rows = wide[pl.ds(f * states * 4 + first + i, states, stride=4), :]
                piece[i, :, f * cells:(f + 1) * cells] = rows.astype(jnp.bfloat16)


def split_kernel(dims, state_ref, outer_ref, inner_ref, wide):
    wide[...] = state_ref[...]
    split_rows(dims, wide, outer_ref, inner_ref)


def first_kernel(
    dims, layer_ref, mask_ref, innov_ref, slope_ref, out_ref, in_ref,
    outer_ref, inner_ref, forcing_ref, raw_ref,
    layers, mask, innov, slope, taps_out, taps_in, wide, sem,
):
    fronts, states, cells, half = dims

    def fetch(i, src, dst):
        copy = pltpu.make_async_copy(src, dst, sem.at[i])
        copy.start()
        return copy

    fetches = [
        fetch(i, src, dst)
        for i, (src, dst) in enumerate(
            ((layer_ref, layers), (mask_ref, mask), (innov_ref, innov), (slope_ref, slope))
        )
    ]
    fetches[0].wait()
    layer = layers[lax.axis_index("tm")]
    fetches += [fetch(4, out_ref.at[layer], taps_out), fetch(5, in_ref.at[layer], taps_in)]
    fetches[1].wait()
    fetches[2].wait()
    wide[...] = innov[...].astype(jnp.float32) * tile_mask(mask, cells)
    split_rows((fronts, states, cells), wide, outer_ref, inner_ref)
    forcing_ref[...] = wide[...].astype(jnp.bfloat16)
    fetches[3].wait()
    raw_ref[18 * half:, :] = slope[...]
    for i, taps in enumerate((taps_out, taps_in)):
        fetches[4 + i].wait()
        for t in range(9):
            start = (9 * i + t) * half
            raw_ref[start:start + half, :states] = taps[t // 3, t % 3]


def order_kernel(dims, own_ref, away_ref, first_ref, second_ref, slope_ref, edge_ref, wide):
    states, pitch, half, cells = dims
    hidden, lanes = 2 * half, 2 * cells
    chan = lax.axis_index("chan")
    inside = lax.broadcasted_iota(jnp.int32, (half, lanes), 1) < states

    def placed(raw_ref, i, a, b, spot):
        start = (9 * i + 3 * a + b) * half
        block = raw_ref[start:start + half, :].astype(jnp.float32)
        block = jnp.where(inside, jnp.concatenate([block, block], axis=1), 0.0)
        return block if spot == 0 else pltpu.roll(block, spot * pitch, 1)

    turned = [[None, None] for _ in range(3)]
    for part, raw_ref in enumerate((own_ref, away_ref)):
        for b in range(3):
            rows = sum(placed(raw_ref, 0, a, b, 2 - a) for a in range(3))
            start = b * hidden + part * half
            first_ref[start:start + half, :] = rows.astype(jnp.bfloat16)
        for a in range(3):
            turned[2 - a][part] = sum(placed(raw_ref, 1, a, b, b) for b in range(3))
        wide[...] = raw_ref[18 * half:, :].astype(jnp.float32)
        for j in range(6):
            lat_row = jnp.clip(4 * chan + j - 1, 0, 7)
            start = j * hidden + part * half
            slope_ref[start:start + half, :] = wide[pl.ds(lat_row, half, stride=8), :].astype(jnp.bfloat16)
        start = (1 - part) * half
        edge_ref[start:start + half, :] = wide[pl.ds(7 * chan, half, stride=8), :].astype(jnp.bfloat16)
    turned = jnp.concatenate([block for pair in turned for block in pair], axis=0).T
    second_ref[...] = turned[:3 * pitch].astype(jnp.bfloat16)


def step_kernel(
    dims, halo_ref, outer_ref, inner_ref, other_ref, forcing_ref,
    first_ref, second_ref, slope_ref, edge_ref, result_ref, field, hidden_grad,
):
    fronts, states, pitch, hidden, cells = dims
    chan, band = lax.axis_index("chan"), lax.axis_index("lat")
    rows = 4
    live = lax.axis_index("tm") < lax.axis_size("tm") - 1
    border = (band == 0) & (chan == 0) | (band == lax.axis_size("lat") - 1) & (chan == 1)
    field[...] = jnp.zeros_like(field)
    for spot, piece in enumerate((halo_ref, outer_ref, inner_ref, other_ref)):

        @pl.when(live & ~border if spot == 0 else live)
        def _():
            place = spot + chan * (3 - 2 * spot)
            for i in range(2):
                start = pl.multiple_of(place * (2 * pitch) + i * pitch, 16)
                field[pl.ds(start, states), :] = piece[i]

    for j in range(rows + 2):
        taps = jnp.dot(
            first_ref[:, :3 * pitch], field[j * pitch:(j + 3) * pitch, :],
            preferred_element_type=jnp.float32,
        )
        slope = slope_ref[j * hidden:(j + 1) * hidden, :].astype(jnp.float32)
        if j in (0, rows + 1):
            beyond = jnp.where(border, 0.0, edge_ref[...].astype(jnp.float32))
            slope = jnp.where(chan == (0 if j == 0 else 1), beyond, slope)
        for f in range(fronts):
            lanes = slice(f * cells, (f + 1) * cells)
            total = (
                taps[hidden:2 * hidden, lanes]
                + lane_shift(taps[0:hidden, lanes], -1)
                + lane_shift(taps[2 * hidden:3 * hidden, lanes], 1)
            )
            hidden_grad[j * hidden:(j + 1) * hidden, lanes] = (slope * total).astype(jnp.bfloat16)

    result_ref[...] = forcing_ref[...].astype(jnp.float32)
    for h in range(rows):
        taps = jnp.dot(
            second_ref[...], hidden_grad[h * hidden:(h + 3) * hidden, :],
            preferred_element_type=jnp.float32,
        )
        before = field[(h + 2) * pitch:(h + 3) * pitch, :].astype(jnp.float32)
        for f in range(fronts):
            lanes = slice(f * cells, (f + 1) * cells)
            total = (
                before[:, lanes]
                + taps[pitch:2 * pitch, lanes]
                + lane_shift(taps[0:pitch, lanes], -1)
                + lane_shift(taps[2 * pitch:3 * pitch, lanes], 1)
            )
            spots = pl.ds(f * states * rows + h, states, stride=rows)
            result_ref[spots, :] = result_ref[spots, :] + total[:states]


def per_device(innovations, obs_mask, slopes, layer_of, weight_in, weight_out):
    fronts, _, states, rows, cells = innovations.shape
    half = slopes.shape[1]
    hidden = 2 * half
    pitch = -(-states // 16) * 16
    owners = lax.axis_size("tm")
    flat = (fronts * states * rows, cells)

    def array(shape, dtype=jnp.bfloat16):
        return jax.ShapeDtypeStruct(shape, dtype)

    piece = array((2, states, fronts * cells))
    modest = pltpu.CompilerParams(vmem_limit_bytes=8 << 20)
    outer, inner, forcing, raw_own = pl.pallas_call(
        functools.partial(first_kernel, (fronts, states, cells, half)),
        out_shape=(piece, piece, array(flat), array((26 * half, cells))),
        in_specs=[HBM] * 6,
        out_specs=(VMEM,) * 4,
        scratch_shapes=[
            pltpu.SMEM(layer_of.shape, jnp.int32),
            pltpu.SMEM(obs_mask.shape[2:], jnp.int32),
            pltpu.VMEM(flat, jnp.bfloat16),
            pltpu.VMEM((8 * half, cells), jnp.bfloat16),
            pltpu.VMEM((3, 3, half, states), jnp.bfloat16),
            pltpu.VMEM((3, 3, half, states), jnp.bfloat16),
            pltpu.VMEM(flat, jnp.float32),
            pltpu.SemaphoreType.DMA((6,)),
        ],
        compiler_params=modest,
    )(
        *(
            pltpu.with_memory_space_constraint(argument, pltpu.HBM)
            for argument in (
                layer_of, obs_mask[0, 0], innovations.reshape(flat), slopes.reshape(8 * half, cells),
                weight_out, weight_in.transpose(0, 1, 2, 4, 3),
            )
        )
    )
    outer_in = to_earlier(outer)
    raw_away = swap_chan(raw_own)
    first, second, slope, edge = pl.pallas_call(
        functools.partial(order_kernel, (states, pitch, half, cells)),
        out_shape=(
            array((3 * hidden, 2 * cells)), array((3 * pitch, 3 * hidden)),
            array((6 * hidden, cells)), array((hidden, cells)),
        ),
        in_specs=[VMEM] * 2,
        out_specs=(VMEM,) * 4,
        scratch_shapes=[pltpu.VMEM((8 * half, cells), jnp.float32)],
        compiler_params=modest,
    )(raw_own, raw_away)
    edge, inner = lax.optimization_barrier((edge, inner))
    inner_in = to_earlier(inner)
    edge = swap_lat(edge)
    edge, outer_in = lax.optimization_barrier((edge, outer_in))

    for hop in range(1, owners):
        if hop > 1:
            outer, inner = pl.pallas_call(
                functools.partial(split_kernel, (fronts, states, cells)),
                out_shape=(piece, piece),
                in_specs=[VMEM],
                out_specs=(VMEM, VMEM),
                scratch_shapes=[pltpu.VMEM(flat, jnp.float32)],
                compiler_params=modest,
            )(result)
            outer_in, inner_in = to_earlier(outer), to_earlier(inner)
        halo = swap_lat(outer_in)
        other = swap_chan(inner_in)
        result = pl.pallas_call(
            functools.partial(step_kernel, (fronts, states, pitch, hidden, cells)),
            out_shape=array(flat, jnp.float32),
            in_specs=[VMEM] * 9,
            out_specs=VMEM,
            scratch_shapes=[
                pltpu.VMEM((8 * pitch, fronts * cells), jnp.bfloat16),
                pltpu.VMEM((6 * hidden, fronts * cells), jnp.bfloat16),
            ],
            compiler_params=modest,
        )(halo, outer_in, inner_in, other, forcing, first, second, slope, edge)
    return result.reshape(innovations.shape)


def solution(mesh):
    return jax.shard_map(
        per_device,
        mesh=mesh,
        in_specs=(
            P(None, ("grp", "tm"), None, ("lat", "chan"), None),
            P(("grp", "tm"), ("lat", "chan"), None),
            P(("grp", "tm"), "chan", "lat", None),
            P(),
            P(None, None, None, None, "chan"),
            P(None, None, None, "chan", None),
        ),
        out_specs=P(None, ("grp", "tm"), None, ("lat", "chan"), None),
        check_vma=False,
    )
```

time: 28.9 us -> 18.9 us (0.65)
  the two profiles are of different devices: /device:TPU:1 before, /device:TPU:0 now
where the time goes in v2:
time: 18.9 us; the launch traced here: 18.8 us
  starting transfers between devices  7.88 us (42%)
  waiting for transfers between devices  6.19 us (33%)
  Pallas kernels  4.69 us (25%)
    ppermute x2, waiting for transfers between devices, swap_lat(): return lax.ppermute(block, ('grp', 'lat', 'chan'), route)  4.35 us
    ppermute x2, starting transfers between devices, to_earlier(): lax.ppermute(block, 'tm', [(i, (i - 1) % count) for i in range(count)])  4.32 us
    ppermute x2, starting transfers between devices, swap_lat(): return lax.ppermute(block, ('grp', 'lat', 'chan'), route)  3.04 us
    pallas_call x1, Pallas kernels, per_device(): pl.pallas_call(functools.partial(step_kernel, (fronts, states, pitch, hid...  2.4 us
    ppermute x2, waiting for transfers between devices, to_earlier(): lax.ppermute(block, 'tm', [(i, (i - 1) % count) for i in range(count)])  1.84 us
    pallas_call x1, Pallas kernels, per_device(): pl.pallas_call(functools.partial(first_kernel, (fronts, states, cells, ha...  1.77 us
    ppermute x2, starting transfers between devices, swap_chan(): return lax.ppermute(block, 'chan', [(0, 1), (1, 0)])  0.52 us
    pallas_call x1, Pallas kernels, per_device(): pl.pallas_call(functools.partial(order_kernel, (states, pitch, half, cell...  0.52 us
  transfers between devices with their start and end apart: 6, of which 4 were waited for; matrix products, arithmetic and copies ran while one was open for 0% of the time, Pallas kernels for 3%

profile of v2, /device:TPU:0, one launch (start us, length us, event | category | flops | bytes accessed | tf_op | source)
XLA Modules:
  0.0 18.8 jit_solution(2699839459113868973)
XLA Ops:
  0.0 1.8 %shard_map.64 = (bf16[2,73,512]{2,1,0:T(8,128)(2,1)S(1)}, bf16[2,73,512]{2,1,0:T(8,128)(2,1)S(1)}, bf16[1168,128]{1,0:T(8,128)(2,1)S(1)}, bf16[1664,128]{1,0:T(8,128)(2,1)S(1)}) custom-call(s32[2]{0:T(128)} %layer_ref.1, s32[4]{0:T(128)} %bitcast.10, bf16[1168,128]{1,0:T(8,128)(2,1)} %bitcast.8, bf16[512,128]{1,0:T(8,128)(2,1)} %bitcast.9, ...), custom_call_target="tpu_custom_call" | custom-call | tf_op jit(solution)/shard_map/pallas_call | solution.py:200
  1.8 0.5 %collective-permute-start = (bf16[1664,128]{1,0:T(8,128)(2,1)S(1)}, bf16[1664,128]{1,0:T(8,128)(2,1)S(1)}, u32[]{:S(2)}, u32[]{:S(2)}) collective-permute-start(bf16[1664,128]{1,0:T(8,128)(2,1)S(1)} %get-tuple-element.17.own_ref), channel_id=1, source_target_pairs={{0,1},{1,0},{2,3},{3,2},{4,5},{5,4},{6,7},{7,6},{8,9},{9,8},{10,11... | collective-permute-start | bytes 1277960 | tf_op jit(solution)/shard_map/ppermute | solution.py:15
  2.3 2.6 %collective-permute-start.2 = (bf16[2,73,512]{2,1,0:T(8,128)(2,1)S(1)}, bf16[2,73,512]{2,1,0:T(8,128)(2,1)S(1)}, u32[]{:S(2)}, u32[]{:S(2)}) collective-permute-start(bf16[2,73,512]{2,1,0:T(8,128)(2,1)S(1)} %get-tuple-element.21), channel_id=1, source_target_pairs={{0,2},{2,0},{1,3},{3,1},{4,6},{6,4},{5,7},{7,5},{8,10},{10,8},{9,1... | collective-permute-start | bytes 448520 | tf_op jit(solution)/shard_map/ppermute | solution.py:33
  4.9 0.0 collective-permute-done.away_ref
  4.9 0.5 %shard_map.65 = (bf16[384,256]{1,0:T(8,128)(2,1)S(1)}, bf16[240,384]{1,0:T(8,128)(2,1)S(1)}, bf16[768,128]{1,0:T(8,128)(2,1)S(1)}, bf16[128,128]{1,0:T(8,128)(2,1)S(1)}) custom-call(bf16[1664,128]{1,0:T(8,128)(2,1)S(1)} %get-tuple-element.17.own_ref, bf16[1664,128]{1,0:T(8,128)(2,1)S(1)} %collective-permute-done.away_ref), custom_call_target="tpu_custom_call" | custom-call | tf_op jit(solution)/shard_map/pallas_call | solution.py:227
  5.4 1.8 %collective-permute-start.4 = (bf16[2,73,512]{2,1,0:T(8,128)(2,1)S(1)}, bf16[2,73,512]{2,1,0:T(8,128)(2,1)S(1)}, u32[]{:S(2)}, u32[]{:S(2)}) collective-permute-start(bf16[2,73,512]{2,1,0:T(8,128)(2,1)S(1)} %get-tuple-element.23), channel_id=1, source_target_pairs={{0,2},{2,0},{1,3},{3,1},{4,6},{6,4},{5,7},{7,5},{8,10},{10,8},{9,1... | collective-permute-start | bytes 448520 | tf_op jit(solution)/shard_map/ppermute | solution.py:33
  7.1 1.5 %collective-permute-start.1 = (bf16[128,128]{1,0:T(8,128)(2,1)S(1)}, bf16[128,128]{1,0:T(8,128)(2,1)S(1)}, u32[]{:S(2)}, u32[]{:S(2)}) collective-permute-start(bf16[128,128]{1,0:T(8,128)(2,1)S(1)} %get-tuple-element.20), channel_id=1, source_target_pairs={{1,4},{4,1},{5,8},{8,5},{9,12},{12,9},{0,16},{13,29},{17,20},{20,1... | collective-permute-start | bytes 98312 | tf_op jit(solution)/shard_map/ppermute | solution.py:28
  8.7 1.3 %collective-permute-done.2.outer_ref = bf16[2,73,512]{2,1,0:T(8,128)(2,1)S(1)} collective-permute-done((bf16[2,73,512]{2,1,0:T(8,128)(2,1)S(1)}, bf16[2,73,512]{2,1,0:T(8,128)(2,1)S(1)}, u32[]{:S(2)}, u32[]{:S(2)}) %collective-permute-start.2) | collective-permute-done | bytes 149536 | tf_op jit(solution)/shard_map/ppermute | solution.py:33
  9.9 1.1 %collective-permute-done.1.edge_ref = bf16[128,128]{1,0:T(8,128)(2,1)S(1)} collective-permute-done((bf16[128,128]{1,0:T(8,128)(2,1)S(1)}, bf16[128,128]{1,0:T(8,128)(2,1)S(1)}, u32[]{:S(2)}, u32[]{:S(2)}) %collective-permute-start.1) | collective-permute-done | bytes 32800 | tf_op jit(solution)/shard_map/ppermute | solution.py:28
  11.1 1.5 %collective-permute-start.3 = (bf16[2,73,512]{2,1,0:T(8,128)(2,1)S(1)}, bf16[2,73,512]{2,1,0:T(8,128)(2,1)S(1)}, u32[]{:S(2)}, u32[]{:S(2)}) collective-permute-start(bf16[2,73,512]{2,1,0:T(8,128)(2,1)S(1)} %collective-permute-done.2.outer_ref), channel_id=1, source_target_pairs={{1,4},{4,1},{5,8},{8,5},{9,12},{12,9},{0,16},{13,29},{17,20},{20,1... | collective-permute-start | bytes 448520 | tf_op jit(solution)/shard_map/ppermute | solution.py:28
  12.6 0.6 %collective-permute-done.4.inner_ref = bf16[2,73,512]{2,1,0:T(8,128)(2,1)S(1)} collective-permute-done((bf16[2,73,512]{2,1,0:T(8,128)(2,1)S(1)}, bf16[2,73,512]{2,1,0:T(8,128)(2,1)S(1)}, u32[]{:S(2)}, u32[]{:S(2)}) %collective-permute-start.4) | collective-permute-done | bytes 149536 | tf_op jit(solution)/shard_map/ppermute | solution.py:33
  13.2 0.0 collective-permute-start.5
  13.2 3.2 %collective-permute-done.3.halo_ref = bf16[2,73,512]{2,1,0:T(8,128)(2,1)S(1)} collective-permute-done((bf16[2,73,512]{2,1,0:T(8,128)(2,1)S(1)}, bf16[2,73,512]{2,1,0:T(8,128)(2,1)S(1)}, u32[]{:S(2)}, u32[]{:S(2)}) %collective-permute-start.3) | collective-permute-done | bytes 149536 | tf_op jit(solution)/shard_map/ppermute | solution.py:28
  16.4 0.0 collective-permute-done.5.other_ref
  16.4 2.4 %shard_map.66 = f32[1168,128]{1,0:T(8,128)} custom-call(bf16[2,73,512]{2,1,0:T(8,128)(2,1)S(1)} %collective-permute-done.3.halo_ref, bf16[2,73,512]{2,1,0:T(8,128)(2,1)S(1)} %collective-permute-done.2.outer_ref, bf16[2,73,512]{2,1,0:T(8,128)(2,1)S(1)} %collective-permute-done.4.inner_ref, bf16[2,73,512]{2,1,0:T(8,128)(2,1)S(1)} %collective-permute-done.5.other_ref, ...), custom_call_target="tpu_custom_call" | custom-call | tf_op jit(solution)/shard_map/pallas_call | solution.py:256
Async XLA Ops:
  1.8 3.1 %collective-permute-start = (bf16[1664,128]{1,0:T(8,128)(2,1)S(1)}, bf16[1664,128]{1,0:T(8,128)(2,1)S(1)}, u32[]{:S(2)}, u32[]{:S(2)}) collective-permute-start(bf16[1664,128]{1,0:T(8,128)(2,1)S(1)} %get-tuple-element.17.own_ref), channel_id=1, source_target_pairs={{0,1},{1,0},{2,3},{3,2},{4,5},{5,4},{6,7},{7,6},{8,9},{9,8},{10,11... | collective-permute-start | bytes 1277960 | tf_op jit(solution)/shard_map/ppermute | solution.py:15
  2.3 7.6 %collective-permute-start.2 = (bf16[2,73,512]{2,1,0:T(8,128)(2,1)S(1)}, bf16[2,73,512]{2,1,0:T(8,128)(2,1)S(1)}, u32[]{:S(2)}, u32[]{:S(2)}) collective-permute-start(bf16[2,73,512]{2,1,0:T(8,128)(2,1)S(1)} %get-tuple-element.21), channel_id=1, source_target_pairs={{0,2},{2,0},{1,3},{3,1},{4,6},{6,4},{5,7},{7,5},{8,10},{10,8},{9,1... | collective-permute-start | bytes 448520 | tf_op jit(solution)/shard_map/ppermute | solution.py:33
  5.4 7.8 %collective-permute-start.4 = (bf16[2,73,512]{2,1,0:T(8,128)(2,1)S(1)}, bf16[2,73,512]{2,1,0:T(8,128)(2,1)S(1)}, u32[]{:S(2)}, u32[]{:S(2)}) collective-permute-start(bf16[2,73,512]{2,1,0:T(8,128)(2,1)S(1)} %get-tuple-element.23), channel_id=1, source_target_pairs={{0,2},{2,0},{1,3},{3,1},{4,6},{6,4},{5,7},{7,5},{8,10},{10,8},{9,1... | collective-permute-start | bytes 448520 | tf_op jit(solution)/shard_map/ppermute | solution.py:33
  7.1 3.9 %collective-permute-start.1 = (bf16[128,128]{1,0:T(8,128)(2,1)S(1)}, bf16[128,128]{1,0:T(8,128)(2,1)S(1)}, u32[]{:S(2)}, u32[]{:S(2)}) collective-permute-start(bf16[128,128]{1,0:T(8,128)(2,1)S(1)} %get-tuple-element.20), channel_id=1, source_target_pairs={{1,4},{4,1},{5,8},{8,5},{9,12},{12,9},{0,16},{13,29},{17,20},{20,1... | collective-permute-start | bytes 98312 | tf_op jit(solution)/shard_map/ppermute | solution.py:28
  11.1 5.3 %collective-permute-start.3 = (bf16[2,73,512]{2,1,0:T(8,128)(2,1)S(1)}, bf16[2,73,512]{2,1,0:T(8,128)(2,1)S(1)}, u32[]{:S(2)}, u32[]{:S(2)}) collective-permute-start(bf16[2,73,512]{2,1,0:T(8,128)(2,1)S(1)} %collective-permute-done.2.outer_ref), channel_id=1, source_target_pairs={{1,4},{4,1},{5,8},{8,5},{9,12},{12,9},{0,16},{13,29},{17,20},{20,1... | collective-permute-start | bytes 448520 | tf_op jit(solution)/shard_map/ppermute | solution.py:28
  13.2 3.2 %collective-permute-start.5 = (bf16[2,73,512]{2,1,0:T(8,128)(2,1)S(1)}, bf16[2,73,512]{2,1,0:T(8,128)(2,1)S(1)}, u32[]{:S(2)}, u32[]{:S(2)}) collective-permute-start(bf16[2,73,512]{2,1,0:T(8,128)(2,1)S(1)} %collective-permute-done.4.inner_ref), channel_id=1, source_target_pairs={{0,1},{1,0},{2,3},{3,2},{4,5},{5,4},{6,7},{7,6},{8,9},{9,8},{10,11... | collective-permute-start | bytes 448520 | tf_op jit(solution)/shard_map/ppermute | solution.py:15

commit v3 on v2

--- a/solution.py
+++ b/solution.py
@@ -47,25 +47,36 @@
     return seen
 
 
-def split_rows(dims, wide, outer_ref, inner_ref):
+def split_rows(dims, wide, piece, outer_ref, inner_ref):
     fronts, states, cells = dims
     chan = lax.axis_index("chan")
-    for piece, first in ((outer_ref, 2 * chan), (inner_ref, 2 - 2 * chan)):
+    for ref, first in ((outer_ref, 2 * chan), (inner_ref, 2 - 2 * chan)):
         for i in range(2):
             for f in range(fronts):
                 rows = wide[pl.ds(f * states * 4 + first + i, states, stride=4), :]
-                piece[i, :, f * cells:(f + 1) * cells] = rows.astype(jnp.bfloat16)
-
-
-def split_kernel(dims, state_ref, outer_ref, inner_ref, wide):
+                piece[pl.ds(i * fronts + f, states, stride=2 * fronts), :] = rows
+        ref[...] = piece[...].astype(jnp.bfloat16)
+
+
+def spread_rows(dims, ref, piece, field, start, used):
+    fronts, states, pitch, cells = dims
+    piece[...] = jnp.where(used, ref[...].astype(jnp.float32), 0.0)
+    for i in range(2):
+        for f in range(fronts):
+            rows = piece[pl.ds(i * fronts + f, states, stride=2 * fronts), :]
+            spot = pl.ds(pl.multiple_of(start + i * pitch, 16), states)
+            field[spot, f * cells:(f + 1) * cells] = rows.astype(jnp.bfloat16)
+
+
+def split_kernel(dims, state_ref, outer_ref, inner_ref, wide, piece):
     wide[...] = state_ref[...]
-    split_rows(dims, wide, outer_ref, inner_ref)
+    split_rows(dims, wide, piece, outer_ref, inner_ref)
 
 
 def first_kernel(
     dims, layer_ref, mask_ref, innov_ref, slope_ref, out_ref, in_ref,
     outer_ref, inner_ref, forcing_ref, raw_ref,
-    layers, mask, innov, slope, taps_out, taps_in, wide, sem,
+    layers, mask, innov, slope, taps_out, taps_in, wide, piece, sem,
 ):
     fronts, states, cells, half = dims
 
@@ -86,7 +97,7 @@
     fetches[1].wait()
     fetches[2].wait()
     wide[...] = innov[...].astype(jnp.float32) * tile_mask(mask, cells)
-    split_rows((fronts, states, cells), wide, outer_ref, inner_ref)
+    split_rows((fronts, states, cells), wide, piece, outer_ref, inner_ref)
     forcing_ref[...] = wide[...].astype(jnp.bfloat16)
     fetches[3].wait()
     raw_ref[18 * half:, :] = slope[...]
@@ -128,9 +139,42 @@
     second_ref[...] = turned[:3 * pitch].astype(jnp.bfloat16)
 
 
+def hidden_row(dims, j, first_ref, slope, field, hidden_grad, spot):
+    fronts, pitch, hidden, cells = dims
+    for pair in range(fronts // 2):
+        taps = jnp.dot(
+            first_ref[:, :3 * pitch],
+            field[j * pitch:(j + 3) * pitch, 2 * pair * cells:2 * (pair + 1) * cells],
+            preferred_element_type=jnp.float32,
+        )
+        for f in range(2):
+            lanes = slice(f * cells, (f + 1) * cells)
+            total = (
+                taps[hidden:2 * hidden, lanes]
+                + lane_shift(taps[0:hidden, lanes], -1)
+                + lane_shift(taps[2 * hidden:3 * hidden, lanes], 1)
+            )
+            start = (2 * pair + f) * cells
+            hidden_grad[spot:spot + hidden, start:start + cells] = (slope * total).astype(jnp.bfloat16)
+
+
+def own_kernel(
+    dims, outer_ref, inner_ref, first_ref, slope_ref, field_ref, hidden_ref, piece,
+):
+    fronts, states, pitch, hidden, cells = dims
+    chan = lax.axis_index("chan")
+    live = lax.axis_index("tm") < lax.axis_size("tm") - 1
+    field_ref[...] = jnp.zeros_like(field_ref)
+    for ref, start in ((outer_ref, chan * 2 * pitch), (inner_ref, (1 - chan) * 2 * pitch)):
+        spread_rows((fronts, states, pitch, cells), ref, piece, field_ref, start, live)
+    for j in range(2):
+        slope = slope_ref[(j + 2) * hidden:(j + 3) * hidden, :].astype(jnp.float32)
+        hidden_row((fronts, pitch, hidden, cells), j, first_ref, slope, field_ref, hidden_ref, j * hidden)
+
+
 def step_kernel(
-    dims, halo_ref, outer_ref, inner_ref, other_ref, forcing_ref,
-    first_ref, second_ref, slope_ref, edge_ref, result_ref, field, hidden_grad,
+    dims, halo_ref, other_ref, own_ref, middle_ref, forcing_ref,
+    first_ref, second_ref, slope_ref, edge_ref, result_ref, field, hidden_grad, piece, result, sem,
 ):
     fronts, states, pitch, hidden, cells = dims
     chan, band = lax.axis_index("chan"), lax.axis_index("lat")
@@ -138,50 +182,46 @@
     live = lax.axis_index("tm") < lax.axis_size("tm") - 1
     border = (band == 0) & (chan == 0) | (band == lax.axis_size("lat") - 1) & (chan == 1)
     field[...] = jnp.zeros_like(field)
-    for spot, piece in enumerate((halo_ref, outer_ref, inner_ref, other_ref)):
-
-        @pl.when(live & ~border if spot == 0 else live)
-        def _():
-            place = spot + chan * (3 - 2 * spot)
-            for i in range(2):
-                start = pl.multiple_of(place * (2 * pitch) + i * pitch, 16)
-                field[pl.ds(start, states), :] = piece[i]
-
-    for j in range(rows + 2):
-        taps = jnp.dot(
-            first_ref[:, :3 * pitch], field[j * pitch:(j + 3) * pitch, :],
-            preferred_element_type=jnp.float32,
-        )
+    for ref, start, used in (
+        (halo_ref, chan * 6 * pitch, live & ~border),
+        (other_ref, (1 - chan) * 6 * pitch, live),
+    ):
+        spread_rows((fronts, states, pitch, cells), ref, piece, field, start, used)
+    field[2 * pitch:6 * pitch, :] = own_ref[...]
+    hidden_grad[2 * hidden:4 * hidden, :] = middle_ref[...]
+    for j in (0, 1, rows, rows + 1):
         slope = slope_ref[j * hidden:(j + 1) * hidden, :].astype(jnp.float32)
         if j in (0, rows + 1):
             beyond = jnp.where(border, 0.0, edge_ref[...].astype(jnp.float32))
             slope = jnp.where(chan == (0 if j == 0 else 1), beyond, slope)
-        for f in range(fronts):
-            lanes = slice(f * cells, (f + 1) * cells)
-            total = (
-                taps[hidden:2 * hidden, lanes]
-                + lane_shift(taps[0:hidden, lanes], -1)
-                + lane_shift(taps[2 * hidden:3 * hidden, lanes], 1)
+        hidden_row((fronts, pitch, hidden, cells), j, first_ref, slope, field, hidden_grad, j * hidden)
+
+    size = 2 * states * rows
+    copies = []
+    for pair in range(fronts // 2):
+        part = slice(pair * size, (pair + 1) * size)
+        result[part, :] = forcing_ref[part, :].astype(jnp.float32)
+        block = slice(2 * pair * cells, 2 * (pair + 1) * cells)
+        for h in range(rows):
+            taps = jnp.dot(
+                second_ref[...], hidden_grad[h * hidden:(h + 3) * hidden, block],
+                preferred_element_type=jnp.float32,
             )
-            hidden_grad[j * hidden:(j + 1) * hidden, lanes] = (slope * total).astype(jnp.bfloat16)
-
-    result_ref[...] = forcing_ref[...].astype(jnp.float32)
-    for h in range(rows):
-        taps = jnp.dot(
-            second_ref[...], hidden_grad[h * hidden:(h + 3) * hidden, :],
-            preferred_element_type=jnp.float32,
-        )
-        before = field[(h + 2) * pitch:(h + 3) * pitch, :].astype(jnp.float32)
-        for f in range(fronts):
-            lanes = slice(f * cells, (f + 1) * cells)
-            total = (
-                before[:, lanes]
-                + taps[pitch:2 * pitch, lanes]
-                + lane_shift(taps[0:pitch, lanes], -1)
-                + lane_shift(taps[2 * pitch:3 * pitch, lanes], 1)
-            )
-            spots = pl.ds(f * states * rows + h, states, stride=rows)
-            result_ref[spots, :] = result_ref[spots, :] + total[:states]
+            before = field[(h + 2) * pitch:(h + 3) * pitch, block].astype(jnp.float32)
+            for f in range(2):
+                lanes = slice(f * cells, (f + 1) * cells)
+                total = (
+                    before[:, lanes]
+                    + taps[pitch:2 * pitch, lanes]
+                    + lane_shift(taps[0:pitch, lanes], -1)
+                    + lane_shift(taps[2 * pitch:3 * pitch, lanes], 1)
+                )
+                spots = pl.ds((2 * pair + f) * states * rows + h, states, stride=rows)
+                result[spots, :] = result[spots, :] + total[:states]
+        copies.append(pltpu.make_async_copy(result.at[part], result_ref.at[part], sem.at[pair]))
+        copies[-1].start()
+    for copy in copies:
+        copy.wait()
 
 
 def per_device(innovations, obs_mask, slopes, layer_of, weight_in, weight_out):
@@ -195,7 +235,9 @@
     def array(shape, dtype=jnp.bfloat16):
         return jax.ShapeDtypeStruct(shape, dtype)
 
-    piece = array((2, states, fronts * cells))
+    piece = array((2 * states * fronts, cells))
+    piece_wide = pltpu.VMEM(piece.shape, jnp.float32)
+    field_shape, hidden_shape = (8 * pitch, fronts * cells), (6 * hidden, fronts * cells)
     modest = pltpu.CompilerParams(vmem_limit_bytes=8 << 20)
     outer, inner, forcing, raw_own = pl.pallas_call(
         functools.partial(first_kernel, (fronts, states, cells, half)),
@@ -210,6 +252,7 @@
             pltpu.VMEM((3, 3, half, states), jnp.bfloat16),
             pltpu.VMEM((3, 3, half, states), jnp.bfloat16),
             pltpu.VMEM(flat, jnp.float32),
+            piece_wide,
             pltpu.SemaphoreType.DMA((6,)),
         ],
         compiler_params=modest,
@@ -247,23 +290,35 @@
                 out_shape=(piece, piece),
                 in_specs=[VMEM],
                 out_specs=(VMEM, VMEM),
-                scratch_shapes=[pltpu.VMEM(flat, jnp.float32)],
+                scratch_shapes=[pltpu.VMEM(flat, jnp.float32), piece_wide],
                 compiler_params=modest,
             )(result)
             outer_in, inner_in = to_earlier(outer), to_earlier(inner)
         halo = swap_lat(outer_in)
         other = swap_chan(inner_in)
+        sizes = (fronts, states, pitch, hidden, cells)
+        own, middle = pl.pallas_call(
+            functools.partial(own_kernel, sizes),
+            out_shape=(array((4 * pitch, fronts * cells)), array((2 * hidden, fronts * cells))),
+            in_specs=[VMEM] * 4,
+            out_specs=(VMEM, VMEM),
+            scratch_shapes=[piece_wide],
+            compiler_params=modest,
+        )(outer_in, inner_in, first, slope)
         result = pl.pallas_call(
-            functools.partial(step_kernel, (fronts, states, pitch, hidden, cells)),
+            functools.partial(step_kernel, sizes),
             out_shape=array(flat, jnp.float32),
             in_specs=[VMEM] * 9,
-            out_specs=VMEM,
+            out_specs=HBM,
             scratch_shapes=[
-                pltpu.VMEM((8 * pitch, fronts * cells), jnp.bfloat16),
-                pltpu.VMEM((6 * hidden, fronts * cells), jnp.bfloat16),
+                pltpu.VMEM(field_shape, jnp.bfloat16),
+                pltpu.VMEM(hidden_shape, jnp.bfloat16),
+                piece_wide,
+                pltpu.VMEM(flat, jnp.float32),
+                pltpu.SemaphoreType.DMA((fronts // 2,)),
             ],
             compiler_params=modest,
-        )(halo, outer_in, inner_in, other, forcing, first, second, slope, edge)
+        )(halo, other, own, middle, forcing, first, second, slope, edge)
     return result.reshape(innovations.shape)
 
 

time: 18.9 us -> 18.6 us (0.984)
  waiting for transfers between devices: 6.19 us -> 5.34 us
  Pallas kernels: 4.69 us -> 5.2 us
    ppermute x2, waiting for transfers between devices: 1.84 us -> 0.95 us  [to_earlier(): lax.ppermute(block, 'tm', [(i, (i - 1) % count) for i in range(count)])]
    pallas_call x1 -> x2, Pallas kernels: 2.4 us -> 2.91 us  [the longest x1 2.21 us: per_device(): pl.pallas_call(functools.partial(step_kernel, sizes), out_shape=array(fla...]
  transfers between devices with their start and end apart: 6 -> 6, of which waited for: 4 -> 3; matrix products, arithmetic and copies ran while one was open for 0% -> 0% of each run, Pallas kernels for 3% -> 7%
where the time goes in v3:
time: 18.6 us; the launch traced here: 18.4 us
  starting transfers between devices  7.88 us (42%)
  waiting for transfers between devices  5.34 us (29%)
  Pallas kernels  5.2 us (28%)
    ppermute x2, waiting for transfers between devices, swap_lat(): return lax.ppermute(block, ('grp', 'lat', 'chan'), route)  4.38 us
    ppermute x2, starting transfers between devices, to_earlier(): lax.ppermute(block, 'tm', [(i, (i - 1) % count) for i in range(count)])  4.32 us
    ppermute x2, starting transfers between devices, swap_lat(): return lax.ppermute(block, ('grp', 'lat', 'chan'), route)  3.04 us
    pallas_call x1, Pallas kernels, per_device(): pl.pallas_call(functools.partial(step_kernel, sizes), out_shape=array(fla...  2.21 us
    pallas_call x1, Pallas kernels, per_device(): pl.pallas_call(functools.partial(first_kernel, (fronts, states, cells, ha...  1.77 us
    ppermute x2, waiting for transfers between devices, to_earlier(): lax.ppermute(block, 'tm', [(i, (i - 1) % count) for i in range(count)])  0.95 us
    pallas_call x1, Pallas kernels, per_device(): pl.pallas_call(functools.partial(own_kernel, sizes), out_shape=(array((4...  0.7 us
    ppermute x2, starting transfers between devices, swap_chan(): return lax.ppermute(block, 'chan', [(0, 1), (1, 0)])  0.52 us
  transfers between devices with their start and end apart: 6, of which 3 were waited for; matrix products, arithmetic and copies ran while one was open for 0% of the time, Pallas kernels for 7%

profile of v3, /device:TPU:0, one launch (start us, length us, event | category | flops | bytes accessed | tf_op | source)
XLA Modules:
  0.0 18.4 jit_solution(13418596422518939078)
XLA Ops:
  0.0 1.8 %shard_map.64 = (bf16[584,128]{1,0:T(8,128)(2,1)S(1)}, bf16[584,128]{1,0:T(8,128)(2,1)S(1)}, bf16[1168,128]{1,0:T(8,128)(2,1)S(1)}, bf16[1664,128]{1,0:T(8,128)(2,1)S(1)}) custom-call(s32[2]{0:T(128)} %layer_ref.1, s32[4]{0:T(128)} %bitcast.10, bf16[1168,128]{1,0:T(8,128)(2,1)} %bitcast.8, bf16[512,128]{1,0:T(8,128)(2,1)} %bitcast.9, ...), custom_call_target="tpu_custom_call" | custom-call | tf_op jit(solution)/shard_map/pallas_call | solution.py:242
  1.8 0.5 %collective-permute-start = (bf16[1664,128]{1,0:T(8,128)(2,1)S(1)}, bf16[1664,128]{1,0:T(8,128)(2,1)S(1)}, u32[]{:S(2)}, u32[]{:S(2)}) collective-permute-start(bf16[1664,128]{1,0:T(8,128)(2,1)S(1)} %get-tuple-element.19.own_ref), channel_id=1, source_target_pairs={{0,1},{1,0},{2,3},{3,2},{4,5},{5,4},{6,7},{7,6},{8,9},{9,8},{10,11... | collective-permute-start | bytes 1277960 | tf_op jit(solution)/shard_map/ppermute | solution.py:15
  2.3 2.6 %collective-permute-start.2 = (bf16[584,128]{1,0:T(8,128)(2,1)S(1)}, bf16[584,128]{1,0:T(8,128)(2,1)S(1)}, u32[]{:S(2)}, u32[]{:S(2)}) collective-permute-start(bf16[584,128]{1,0:T(8,128)(2,1)S(1)} %get-tuple-element.23), channel_id=1, source_target_pairs={{0,2},{2,0},{1,3},{3,1},{4,6},{6,4},{5,7},{7,5},{8,10},{10,8},{9,1... | collective-permute-start | bytes 448520 | tf_op jit(solution)/shard_map/ppermute | solution.py:33
  4.9 0.0 collective-permute-done.away_ref
  4.9 0.5 %shard_map.65 = (bf16[384,256]{1,0:T(8,128)(2,1)S(1)}, bf16[240,384]{1,0:T(8,128)(2,1)S(1)}, bf16[768,128]{1,0:T(8,128)(2,1)S(1)}, bf16[128,128]{1,0:T(8,128)(2,1)S(1)}) custom-call(bf16[1664,128]{1,0:T(8,128)(2,1)S(1)} %get-tuple-element.19.own_ref, bf16[1664,128]{1,0:T(8,128)(2,1)S(1)} %collective-permute-done.away_ref), custom_call_target="tpu_custom_call" | custom-call | tf_op jit(solution)/shard_map/pallas_call | solution.py:270
  5.4 1.8 %collective-permute-start.4 = (bf16[584,128]{1,0:T(8,128)(2,1)S(1)}, bf16[584,128]{1,0:T(8,128)(2,1)S(1)}, u32[]{:S(2)}, u32[]{:S(2)}) collective-permute-start(bf16[584,128]{1,0:T(8,128)(2,1)S(1)} %get-tuple-element.25), channel_id=1, source_target_pairs={{0,2},{2,0},{1,3},{3,1},{4,6},{6,4},{5,7},{7,5},{8,10},{10,8},{9,1... | collective-permute-start | bytes 448520 | tf_op jit(solution)/shard_map/ppermute | solution.py:33
  7.1 1.5 %collective-permute-start.1 = (bf16[128,128]{1,0:T(8,128)(2,1)S(1)}, bf16[128,128]{1,0:T(8,128)(2,1)S(1)}, u32[]{:S(2)}, u32[]{:S(2)}) collective-permute-start(bf16[128,128]{1,0:T(8,128)(2,1)S(1)} %get-tuple-element.22), channel_id=1, source_target_pairs={{1,4},{4,1},{5,8},{8,5},{9,12},{12,9},{0,16},{13,29},{17,20},{20,1... | collective-permute-start | bytes 98312 | tf_op jit(solution)/shard_map/ppermute | solution.py:28
  8.7 0.9 %collective-permute-done.2.outer_ref = bf16[584,128]{1,0:T(8,128)(2,1)S(1)} collective-permute-done((bf16[584,128]{1,0:T(8,128)(2,1)S(1)}, bf16[584,128]{1,0:T(8,128)(2,1)S(1)}, u32[]{:S(2)}, u32[]{:S(2)}) %collective-permute-start.2) | collective-permute-done | bytes 149536 | tf_op jit(solution)/shard_map/ppermute | solution.py:33
  9.6 1.4 %collective-permute-done.1.edge_ref = bf16[128,128]{1,0:T(8,128)(2,1)S(1)} collective-permute-done((bf16[128,128]{1,0:T(8,128)(2,1)S(1)}, bf16[128,128]{1,0:T(8,128)(2,1)S(1)}, u32[]{:S(2)}, u32[]{:S(2)}) %collective-permute-start.1) | collective-permute-done | bytes 32800 | tf_op jit(solution)/shard_map/ppermute | solution.py:28
  11.1 1.5 %collective-permute-start.3 = (bf16[584,128]{1,0:T(8,128)(2,1)S(1)}, bf16[584,128]{1,0:T(8,128)(2,1)S(1)}, u32[]{:S(2)}, u32[]{:S(2)}) collective-permute-start(bf16[584,128]{1,0:T(8,128)(2,1)S(1)} %collective-permute-done.2.outer_ref), channel_id=1, source_target_pairs={{1,4},{4,1},{5,8},{8,5},{9,12},{12,9},{0,16},{13,29},{17,20},{20,1... | collective-permute-start | bytes 448520 | tf_op jit(solution)/shard_map/ppermute | solution.py:28
  12.6 0.0 collective-permute-done.4.inner_ref
  12.6 0.0 collective-permute-start.5
  12.6 0.7 %shard_map.66 = (bf16[320,512]{1,0:T(8,128)(2,1)S(1)}, bf16[256,512]{1,0:T(8,128)(2,1)S(1)}) custom-call(bf16[584,128]{1,0:T(8,128)(2,1)S(1)} %collective-permute-done.2.outer_ref, bf16[584,128]{1,0:T(8,128)(2,1)S(1)} %collective-permute-done.4.inner_ref, bf16[384,256]{1,0:T(8,128)(2,1)S(1)} %get-tuple-element.26.first_ref, ...), custom_call_target="tpu_custom_call" | custom-call | tf_op jit(solution)/shard_map/pallas_call | solution.py:300
  13.3 2.9 %collective-permute-done.3.halo_ref = bf16[584,128]{1,0:T(8,128)(2,1)S(1)} collective-permute-done((bf16[584,128]{1,0:T(8,128)(2,1)S(1)}, bf16[584,128]{1,0:T(8,128)(2,1)S(1)}, u32[]{:S(2)}, u32[]{:S(2)}) %collective-permute-start.3) | collective-permute-done | bytes 149536 | tf_op jit(solution)/shard_map/ppermute | solution.py:28
  16.2 0.0 collective-permute-done.5.other_ref
  16.2 2.2 %shard_map.67 = f32[1168,128]{1,0:T(8,128)} custom-call(bf16[584,128]{1,0:T(8,128)(2,1)S(1)} %collective-permute-done.3.halo_ref, bf16[584,128]{1,0:T(8,128)(2,1)S(1)} %collective-permute-done.5.other_ref, bf16[320,512]{1,0:T(8,128)(2,1)S(1)} %get-tuple-element.28.own_ref, bf16[256,512]{1,0:T(8,128)(2,1)S(1)} %get-tuple-element.29.middle_ref, ...), custom_call_target="tpu_custom_call" | custom-call | tf_op jit(solution)/shard_map/pallas_call | solution.py:308
Async XLA Ops:
  1.8 3.1 %collective-permute-start = (bf16[1664,128]{1,0:T(8,128)(2,1)S(1)}, bf16[1664,128]{1,0:T(8,128)(2,1)S(1)}, u32[]{:S(2)}, u32[]{:S(2)}) collective-permute-start(bf16[1664,128]{1,0:T(8,128)(2,1)S(1)} %get-tuple-element.19.own_ref), channel_id=1, source_target_pairs={{0,1},{1,0},{2,3},{3,2},{4,5},{5,4},{6,7},{7,6},{8,9},{9,8},{10,11... | collective-permute-start | bytes 1277960 | tf_op jit(solution)/shard_map/ppermute | solution.py:15
  2.3 7.3 %collective-permute-start.2 = (bf16[584,128]{1,0:T(8,128)(2,1)S(1)}, bf16[584,128]{1,0:T(8,128)(2,1)S(1)}, u32[]{:S(2)}, u32[]{:S(2)}) collective-permute-start(bf16[584,128]{1,0:T(8,128)(2,1)S(1)} %get-tuple-element.23), channel_id=1, source_target_pairs={{0,2},{2,0},{1,3},{3,1},{4,6},{6,4},{5,7},{7,5},{8,10},{10,8},{9,1... | collective-permute-start | bytes 448520 | tf_op jit(solution)/shard_map/ppermute | solution.py:33
  5.4 7.2 %collective-permute-start.4 = (bf16[584,128]{1,0:T(8,128)(2,1)S(1)}, bf16[584,128]{1,0:T(8,128)(2,1)S(1)}, u32[]{:S(2)}, u32[]{:S(2)}) collective-permute-start(bf16[584,128]{1,0:T(8,128)(2,1)S(1)} %get-tuple-element.25), channel_id=1, source_target_pairs={{0,2},{2,0},{1,3},{3,1},{4,6},{6,4},{5,7},{7,5},{8,10},{10,8},{9,1... | collective-permute-start | bytes 448520 | tf_op jit(solution)/shard_map/ppermute | solution.py:33
  7.1 3.9 %collective-permute-start.1 = (bf16[128,128]{1,0:T(8,128)(2,1)S(1)}, bf16[128,128]{1,0:T(8,128)(2,1)S(1)}, u32[]{:S(2)}, u32[]{:S(2)}) collective-permute-start(bf16[128,128]{1,0:T(8,128)(2,1)S(1)} %get-tuple-element.22), channel_id=1, source_target_pairs={{1,4},{4,1},{5,8},{8,5},{9,12},{12,9},{0,16},{13,29},{17,20},{20,1... | collective-permute-start | bytes 98312 | tf_op jit(solution)/shard_map/ppermute | solution.py:28
  11.1 5.2 %collective-permute-start.3 = (bf16[584,128]{1,0:T(8,128)(2,1)S(1)}, bf16[584,128]{1,0:T(8,128)(2,1)S(1)}, u32[]{:S(2)}, u32[]{:S(2)}) collective-permute-start(bf16[584,128]{1,0:T(8,128)(2,1)S(1)} %collective-permute-done.2.outer_ref), channel_id=1, source_target_pairs={{1,4},{4,1},{5,8},{8,5},{9,12},{12,9},{0,16},{13,29},{17,20},{20,1... | collective-permute-start | bytes 448520 | tf_op jit(solution)/shard_map/ppermute | solution.py:28
  12.6 3.6 %collective-permute-start.5 = (bf16[584,128]{1,0:T(8,128)(2,1)S(1)}, bf16[584,128]{1,0:T(8,128)(2,1)S(1)}, u32[]{:S(2)}, u32[]{:S(2)}) collective-permute-start(bf16[584,128]{1,0:T(8,128)(2,1)S(1)} %collective-permute-done.4.inner_ref), channel_id=1, source_target_pairs={{0,1},{1,0},{2,3},{3,2},{4,5},{5,4},{6,7},{7,6},{8,9},{9,8},{10,11... | collective-permute-start | bytes 448520 | tf_op jit(solution)/shard_map/ppermute | solution.py:15

commit v4 on v3

--- a/solution.py
+++ b/solution.py
@@ -47,38 +47,43 @@
     return seen
 
 
-def split_rows(dims, wide, piece, outer_ref, inner_ref):
+def split_rows(dims, wide, piece, refs):
     fronts, states, cells = dims
     chan = lax.axis_index("chan")
-    for ref, first in ((outer_ref, 2 * chan), (inner_ref, 2 - 2 * chan)):
+    for p, ref in enumerate(refs):
+        first = 2 * chan if p < fronts // 2 else 2 - 2 * chan
+        front = 2 * (p % (fronts // 2))
         for i in range(2):
-            for f in range(fronts):
-                rows = wide[pl.ds(f * states * 4 + first + i, states, stride=4), :]
-                piece[pl.ds(i * fronts + f, states, stride=2 * fronts), :] = rows
+            for f in range(2):
+                rows = wide[pl.ds((front + f) * states * 4 + first + i, states, stride=4), :]
+                piece[pl.ds(i * 2 + f, states, stride=4), :] = rows
         ref[...] = piece[...].astype(jnp.bfloat16)
 
 
-def spread_rows(dims, ref, piece, field, start, used):
-    fronts, states, pitch, cells = dims
-    piece[...] = jnp.where(used, ref[...].astype(jnp.float32), 0.0)
+def spread_rows(dims, ref, front, piece, field, start, used):
+    states, pitch, cells = dims
+    piece[...] = jnp.where(used, ref[:4 * states, :].astype(jnp.float32), 0.0)
     for i in range(2):
-        for f in range(fronts):
-            rows = piece[pl.ds(i * fronts + f, states, stride=2 * fronts), :]
+        for f in range(2):
+            rows = piece[pl.ds(i * 2 + f, states, stride=4), :]
             spot = pl.ds(pl.multiple_of(start + i * pitch, 16), states)
-            field[spot, f * cells:(f + 1) * cells] = rows.astype(jnp.bfloat16)
-
-
-def split_kernel(dims, state_ref, outer_ref, inner_ref, wide, piece):
+            lanes = slice((front + f) * cells, (front + f + 1) * cells)
+            field[spot, lanes] = rows.astype(jnp.bfloat16)
+
+
+def split_kernel(dims, state_ref, *refs):
+    *pieces, wide, piece = refs
     wide[...] = state_ref[...]
-    split_rows(dims, wide, piece, outer_ref, inner_ref)
+    split_rows(dims, wide, piece, pieces)
 
 
 def first_kernel(
     dims, layer_ref, mask_ref, innov_ref, slope_ref, out_ref, in_ref,
-    outer_ref, inner_ref, forcing_ref, raw_ref,
-    layers, mask, innov, slope, taps_out, taps_in, wide, piece, sem,
+    *refs,
 ):
     fronts, states, cells, half = dims
+    *pieces, forcing_ref, raw_ref = refs[:fronts + 2]
+    layers, mask, innov, slope, taps_out, taps_in, wide, piece, sem = refs[fronts + 2:]
 
     def fetch(i, src, dst):
         copy = pltpu.make_async_copy(src, dst, sem.at[i])
@@ -97,7 +102,7 @@
     fetches[1].wait()
     fetches[2].wait()
     wide[...] = innov[...].astype(jnp.float32) * tile_mask(mask, cells)
-    split_rows((fronts, states, cells), wide, piece, outer_ref, inner_ref)
+    split_rows((fronts, states, cells), wide, piece, pieces)
     forcing_ref[...] = wide[...].astype(jnp.bfloat16)
     fetches[3].wait()
     raw_ref[18 * half:, :] = slope[...]
@@ -158,41 +163,50 @@
             hidden_grad[spot:spot + hidden, start:start + cells] = (slope * total).astype(jnp.bfloat16)
 
 
-def own_kernel(
-    dims, outer_ref, inner_ref, first_ref, slope_ref, field_ref, hidden_ref, piece,
-):
+def join_kernel(join, piece_ref, edge_ref, joined_ref):
+    joined_ref[:piece_ref.shape[0], :] = piece_ref[...]
+    joined_ref[join:, :] = edge_ref[...]
+
+
+def own_kernel(dims, *refs):
     fronts, states, pitch, hidden, cells = dims
+    pieces = refs[:fronts]
+    first_ref, slope_ref, field_ref, hidden_ref, piece = refs[fronts:]
     chan = lax.axis_index("chan")
     live = lax.axis_index("tm") < lax.axis_size("tm") - 1
     field_ref[...] = jnp.zeros_like(field_ref)
-    for ref, start in ((outer_ref, chan * 2 * pitch), (inner_ref, (1 - chan) * 2 * pitch)):
-        spread_rows((fronts, states, pitch, cells), ref, piece, field_ref, start, live)
+    for p, ref in enumerate(pieces):
+        start = (chan if p < fronts // 2 else 1 - chan) * 2 * pitch
+        front = 2 * (p % (fronts // 2))
+        spread_rows((states, pitch, cells), ref, front, piece, field_ref, start, live)
     for j in range(2):
         slope = slope_ref[(j + 2) * hidden:(j + 3) * hidden, :].astype(jnp.float32)
         hidden_row((fronts, pitch, hidden, cells), j, first_ref, slope, field_ref, hidden_ref, j * hidden)
 
 
-def step_kernel(
-    dims, halo_ref, other_ref, own_ref, middle_ref, forcing_ref,
-    first_ref, second_ref, slope_ref, edge_ref, result_ref, field, hidden_grad, piece, result, sem,
-):
+def step_kernel(dims, *refs):
     fronts, states, pitch, hidden, cells = dims
+    pieces = refs[:fronts]
+    own_ref, middle_ref, forcing_ref, first_ref, second_ref, slope_ref = refs[fronts:fronts + 6]
+    result_ref, field, hidden_grad, piece, result, sem = refs[fronts + 6:]
+    edge_ref = pieces[fronts // 2 - 1]
+    edge = edge_ref.shape[0] - hidden
     chan, band = lax.axis_index("chan"), lax.axis_index("lat")
     rows = 4
     live = lax.axis_index("tm") < lax.axis_size("tm") - 1
     border = (band == 0) & (chan == 0) | (band == lax.axis_size("lat") - 1) & (chan == 1)
     field[...] = jnp.zeros_like(field)
-    for ref, start, used in (
-        (halo_ref, chan * 6 * pitch, live & ~border),
-        (other_ref, (1 - chan) * 6 * pitch, live),
-    ):
-        spread_rows((fronts, states, pitch, cells), ref, piece, field, start, used)
+    for p, ref in enumerate(pieces):
+        used = live & ~border if p < fronts // 2 else live
+        start = (chan if p < fronts // 2 else 1 - chan) * 6 * pitch
+        front = 2 * (p % (fronts // 2))
+        spread_rows((states, pitch, cells), ref, front, piece, field, start, used)
     field[2 * pitch:6 * pitch, :] = own_ref[...]
     hidden_grad[2 * hidden:4 * hidden, :] = middle_ref[...]
     for j in (0, 1, rows, rows + 1):
         slope = slope_ref[j * hidden:(j + 1) * hidden, :].astype(jnp.float32)
         if j in (0, rows + 1):
-            beyond = jnp.where(border, 0.0, edge_ref[...].astype(jnp.float32))
+            beyond = jnp.where(border, 0.0, edge_ref[edge:, :].astype(jnp.float32))
             slope = jnp.where(chan == (0 if j == 0 else 1), beyond, slope)
         hidden_row((fronts, pitch, hidden, cells), j, first_ref, slope, field, hidden_grad, j * hidden)
 
@@ -235,15 +249,17 @@
     def array(shape, dtype=jnp.bfloat16):
         return jax.ShapeDtypeStruct(shape, dtype)
 
-    piece = array((2 * states * fronts, cells))
-    piece_wide = pltpu.VMEM(piece.shape, jnp.float32)
+    pairs = fronts // 2
+    pieces = (array((4 * states, cells)),) * fronts
+    piece_wide = pltpu.VMEM(pieces[0].shape, jnp.float32)
+    join = -(-4 * states // 16) * 16
     field_shape, hidden_shape = (8 * pitch, fronts * cells), (6 * hidden, fronts * cells)
     modest = pltpu.CompilerParams(vmem_limit_bytes=8 << 20)
-    outer, inner, forcing, raw_own = pl.pallas_call(
+    *sent, forcing, raw_own = pl.pallas_call(
         functools.partial(first_kernel, (fronts, states, cells, half)),
-        out_shape=(piece, piece, array(flat), array((26 * half, cells))),
+        out_shape=pieces + (array(flat), array((26 * half, cells))),
         in_specs=[HBM] * 6,
-        out_specs=(VMEM,) * 4,
+        out_specs=(VMEM,) * (fronts + 2),
         scratch_shapes=[
             pltpu.SMEM(layer_of.shape, jnp.int32),
             pltpu.SMEM(obs_mask.shape[2:], jnp.int32),
@@ -265,7 +281,7 @@
             )
         )
     )
-    outer_in = to_earlier(outer)
+    outer = [to_earlier(block) for block in sent[:pairs]]
     raw_away = swap_chan(raw_own)
     first, second, slope, edge = pl.pallas_call(
         functools.partial(order_kernel, (states, pitch, half, cells)),
@@ -278,37 +294,43 @@
         scratch_shapes=[pltpu.VMEM((8 * half, cells), jnp.float32)],
         compiler_params=modest,
     )(raw_own, raw_away)
-    edge, inner = lax.optimization_barrier((edge, inner))
-    inner_in = to_earlier(inner)
-    edge = swap_lat(edge)
-    edge, outer_in = lax.optimization_barrier((edge, outer_in))
+    edge, sent = lax.optimization_barrier((edge, sent))
+    inner = [to_earlier(block) for block in sent[pairs:]]
 
     for hop in range(1, owners):
         if hop > 1:
-            outer, inner = pl.pallas_call(
+            sent = pl.pallas_call(
                 functools.partial(split_kernel, (fronts, states, cells)),
-                out_shape=(piece, piece),
+                out_shape=pieces,
                 in_specs=[VMEM],
-                out_specs=(VMEM, VMEM),
+                out_specs=(VMEM,) * fronts,
                 scratch_shapes=[pltpu.VMEM(flat, jnp.float32), piece_wide],
                 compiler_params=modest,
             )(result)
-            outer_in, inner_in = to_earlier(outer), to_earlier(inner)
-        halo = swap_lat(outer_in)
-        other = swap_chan(inner_in)
+            outer = [to_earlier(block) for block in sent[:pairs]]
+            inner = [to_earlier(block) for block in sent[pairs:]]
+        joined = pl.pallas_call(
+            functools.partial(join_kernel, join),
+            out_shape=array((join + hidden, cells)),
+            in_specs=[VMEM, VMEM],
+            out_specs=VMEM,
+            compiler_params=modest,
+        )(outer[-1], edge)
+        halo = [swap_lat(block) for block in outer[:-1] + [joined]]
+        other = [swap_chan(block) for block in inner]
         sizes = (fronts, states, pitch, hidden, cells)
         own, middle = pl.pallas_call(
             functools.partial(own_kernel, sizes),
             out_shape=(array((4 * pitch, fronts * cells)), array((2 * hidden, fronts * cells))),
-            in_specs=[VMEM] * 4,
+            in_specs=[VMEM] * (fronts + 2),
             out_specs=(VMEM, VMEM),
             scratch_shapes=[piece_wide],
             compiler_params=modest,
-        )(outer_in, inner_in, first, slope)
+        )(*outer, *inner, first, slope)
         result = pl.pallas_call(
             functools.partial(step_kernel, sizes),
             out_shape=array(flat, jnp.float32),
-            in_specs=[VMEM] * 9,
+            in_specs=[VMEM] * (fronts + 6),
             out_specs=HBM,
             scratch_shapes=[
                 pltpu.VMEM(field_shape, jnp.bfloat16),
@@ -318,7 +340,7 @@
                 pltpu.SemaphoreType.DMA((fronts // 2,)),
             ],
             compiler_params=modest,
-        )(halo, other, own, middle, forcing, first, second, slope, edge)
+        )(*halo, *other, own, middle, forcing, first, second, slope)
     return result.reshape(innovations.shape)
 
 

time: 18.6 us -> 16.8 us (0.903)
  waiting for transfers between devices: 5.34 us -> 2.32 us
  starting transfers between devices: 7.88 us -> 9.17 us
    ppermute x2, waiting for transfers between devices: 4.38 us -> 1.16 us  [swap_lat(): return lax.ppermute(block, ('grp', 'lat', 'chan'), route)]
    ppermute x2, starting transfers between devices: 3.04 us -> 3.73 us  [swap_lat(): return lax.ppermute(block, ('grp', 'lat', 'chan'), route)]
    ppermute x2 -> x4, starting transfers between devices: 4.32 us -> 4.75 us  [to_earlier(): lax.ppermute(block, 'tm', [(i, (i - 1) % count) for i in range(count)])]
    ppermute x2 -> x4, waiting for transfers between devices: 0.95 us -> 1.15 us  [to_earlier(): lax.ppermute(block, 'tm', [(i, (i - 1) % count) for i in range(count)])]
    ppermute x2 -> x3, starting transfers between devices: 0.52 us -> 0.69 us  [swap_chan(): return lax.ppermute(block, 'chan', [(0, 1), (1, 0)])]
  transfers between devices with their start and end apart: 6 -> 9, of which waited for: 3 -> 3; matrix products, arithmetic and copies ran while one was open for 0% -> 0% of each run, Pallas kernels for 7% -> 7%
where the time goes in v4:
time: 16.8 us; the launch traced here: 16.6 us
  starting transfers between devices  9.17 us (55%)
  Pallas kernels  5.11 us (30%)
  waiting for transfers between devices  2.32 us (14%)
    ppermute x4, starting transfers between devices, to_earlier(): lax.ppermute(block, 'tm', [(i, (i - 1) % count) for i in range(count)])  4.75 us
    ppermute x2, starting transfers between devices, swap_lat(): return lax.ppermute(block, ('grp', 'lat', 'chan'), route)  3.73 us
    pallas_call x1, Pallas kernels, per_device(): pl.pallas_call(functools.partial(step_kernel, sizes), out_shape=array(fla...  2.16 us
    pallas_call x1, Pallas kernels, per_device(): pl.pallas_call(functools.partial(first_kernel, (fronts, states, cells, ha...  1.77 us
    ppermute x2, waiting for transfers between devices, swap_lat(): return lax.ppermute(block, ('grp', 'lat', 'chan'), route)  1.16 us
    ppermute x4, waiting for transfers between devices, to_earlier(): lax.ppermute(block, 'tm', [(i, (i - 1) % count) for i in range(count)])  1.15 us
    ppermute x3, starting transfers between devices, swap_chan(): return lax.ppermute(block, 'chan', [(0, 1), (1, 0)])  0.69 us
    pallas_call x1, Pallas kernels, per_device(): pl.pallas_call(functools.partial(own_kernel, sizes), out_shape=(array((4...  0.65 us
  transfers between devices with their start and end apart: 9, of which 3 were waited for; matrix products, arithmetic and copies ran while one was open for 0% of the time, Pallas kernels for 7%

profile of v4, /device:TPU:0, one launch (start us, length us, event | category | flops | bytes accessed | tf_op | source)
XLA Modules:
  0.0 16.6 jit_solution(15272271029841018290)
XLA Ops:
  0.0 1.8 %shard_map.64 = (bf16[292,128]{1,0:T(8,128)(2,1)S(1)}, bf16[292,128]{1,0:T(8,128)(2,1)S(1)}, bf16[292,128]{1,0:T(8,128)(2,1)S(1)}, bf16[292,128]{1,0:T(8,128)(2,...) custom-call(s32[2]{0:T(128)} %layer_ref.1, s32[4]{0:T(128)} %bitcast.10, bf16[1168,128]{1,0:T(8,128)(2,1)} %bitcast.8, ...), custom_call_target="tpu_custom_call" | custom-call | tf_op jit(solution)/shard_map/pallas_call | solution.py:258
  1.8 0.5 %collective-permute-start.3 = (bf16[1664,128]{1,0:T(8,128)(2,1)S(1)}, bf16[1664,128]{1,0:T(8,128)(2,1)S(1)}, u32[]{:S(2)}, u32[]{:S(2)}) collective-permute-start(bf16[1664,128]{1,0:T(8,128)(2,1)S(1)} %get-tuple-element.22.own_ref), channel_id=1, source_target_pairs={{0,1},{1,0},{2,3},{3,2},{4,5},{5,4},{6,7},{7,6},{8,9},{9,8},{10,11... | collective-permute-start | bytes 1277960 | tf_op jit(solution)/shard_map/ppermute | solution.py:15
  2.3 2.6 %collective-permute-start.2 = (bf16[292,128]{1,0:T(8,128)(2,1)S(1)}, bf16[292,128]{1,0:T(8,128)(2,1)S(1)}, u32[]{:S(2)}, u32[]{:S(2)}) collective-permute-start(bf16[292,128]{1,0:T(8,128)(2,1)S(1)} %get-tuple-element.21), channel_id=1, source_target_pairs={{0,2},{2,0},{1,3},{3,1},{4,6},{6,4},{5,7},{7,5},{8,10},{10,8},{9,1... | collective-permute-start | bytes 224264 | tf_op jit(solution)/shard_map/ppermute | solution.py:33
  4.9 0.1 collective-permute-start
  5.0 0.0 collective-permute-done.3.away_ref
  5.0 0.5 %shard_map.65 = (bf16[384,256]{1,0:T(8,128)(2,1)S(1)}, bf16[240,384]{1,0:T(8,128)(2,1)S(1)}, bf16[768,128]{1,0:T(8,128)(2,1)S(1)}, bf16[128,128]{1,0:T(8,128)(2,1)S(1)}) custom-call(bf16[1664,128]{1,0:T(8,128)(2,1)S(1)} %get-tuple-element.22.own_ref, bf16[1664,128]{1,0:T(8,128)(2,1)S(1)} %collective-permute-done.3.away_ref), custom_call_target="tpu_custom_call" | custom-call | tf_op jit(solution)/shard_map/pallas_call | solution.py:286
  5.5 2.0 %collective-permute-start.5 = (bf16[292,128]{1,0:T(8,128)(2,1)S(1)}, bf16[292,128]{1,0:T(8,128)(2,1)S(1)}, u32[]{:S(2)}, u32[]{:S(2)}) collective-permute-start(bf16[292,128]{1,0:T(8,128)(2,1)S(1)} %get-tuple-element.27), channel_id=1, source_target_pairs={{0,2},{2,0},{1,3},{3,1},{4,6},{6,4},{5,7},{7,5},{8,10},{10,8},{9,1... | collective-permute-start | bytes 224264 | tf_op jit(solution)/shard_map/ppermute | solution.py:33
  7.5 0.1 collective-permute-start.7
  7.6 0.3 %collective-permute-done.2.piece_ref.refs_1_ = bf16[292,128]{1,0:T(8,128)(2,1)S(1)} collective-permute-done((bf16[292,128]{1,0:T(8,128)(2,1)S(1)}, bf16[292,128]{1,0:T(8,128)(2,1)S(1)}, u32[]{:S(2)}, u32[]{:S(2)}) %collective-permute-start.2) | collective-permute-done | bytes 74784 | tf_op jit(solution)/shard_map/ppermute | solution.py:33
  7.9 2.2 %collective-permute-start.4 = (bf16[432,128]{1,0:T(8,128)(2,1)S(1)}, bf16[432,128]{1,0:T(8,128)(2,1)S(1)}, u32[]{:S(2)}, u32[]{:S(2)}) collective-permute-start(bf16[432,128]{1,0:T(8,128)(2,1)S(1)} %shard_map.66), channel_id=1, source_target_pairs={{1,4},{4,1},{5,8},{8,5},{9,12},{12,9},{0,16},{13,29},{17,20},{20,1... | collective-permute-start | bytes 331784 | tf_op jit(solution)/shard_map/ppermute | solution.py:28
  10.1 0.0 collective-permute-done.refs_0_
  10.1 1.5 %collective-permute-start.1 = (bf16[292,128]{1,0:T(8,128)(2,1)S(1)}, bf16[292,128]{1,0:T(8,128)(2,1)S(1)}, u32[]{:S(2)}, u32[]{:S(2)}) collective-permute-start(bf16[292,128]{1,0:T(8,128)(2,1)S(1)} %collective-permute-done.refs_0_), channel_id=1, source_target_pairs={{1,4},{4,1},{5,8},{8,5},{9,12},{12,9},{0,16},{13,29},{17,20},{20,1... | collective-permute-start | bytes 224264 | tf_op jit(solution)/shard_map/ppermute | solution.py:28
  11.6 0.0 collective-permute-done.5.refs_2_
  11.6 0.2 %collective-permute-start.6 = (bf16[292,128]{1,0:T(8,128)(2,1)S(1)}, bf16[292,128]{1,0:T(8,128)(2,1)S(1)}, u32[]{:S(2)}, u32[]{:S(2)}) collective-permute-start(bf16[292,128]{1,0:T(8,128)(2,1)S(1)} %collective-permute-done.5.refs_2_), channel_id=1, source_target_pairs={{0,1},{1,0},{2,3},{3,2},{4,5},{5,4},{6,7},{7,6},{8,9},{9,8},{10,11... | collective-permute-start | bytes 224264 | tf_op jit(solution)/shard_map/ppermute | solution.py:15
  11.8 0.8 %collective-permute-done.7.refs_3_ = bf16[292,128]{1,0:T(8,128)(2,1)S(1)} collective-permute-done((bf16[292,128]{1,0:T(8,128)(2,1)S(1)}, bf16[292,128]{1,0:T(8,128)(2,1)S(1)}, u32[]{:S(2)}, u32[]{:S(2)}) %collective-permute-start.7) | collective-permute-done | bytes 74784 | tf_op jit(solution)/shard_map/ppermute | solution.py:33
  12.6 0.0 collective-permute-start.8
  12.6 0.7 %shard_map.67 = (bf16[320,512]{1,0:T(8,128)(2,1)S(1)}, bf16[256,512]{1,0:T(8,128)(2,1)S(1)}) custom-call(bf16[292,128]{1,0:T(8,128)(2,1)S(1)} %collective-permute-done.refs_0_, bf16[292,128]{1,0:T(8,128)(2,1)S(1)} %collective-permute-done.2.piece_ref.refs_1_, bf16[292,128]{1,0:T(8,128)(2,1)S(1)} %collective-permute-done.5.refs_2_, ...), custom_call_target="tpu_custom_call" | custom-call | tf_op jit(solution)/shard_map/pallas_call | solution.py:322
  13.3 1.2 %collective-permute-done.1.refs_0_ = bf16[292,128]{1,0:T(8,128)(2,1)S(1)} collective-permute-done((bf16[292,128]{1,0:T(8,128)(2,1)S(1)}, bf16[292,128]{1,0:T(8,128)(2,1)S(1)}, u32[]{:S(2)}, u32[]{:S(2)}) %collective-permute-start.1) | collective-permute-done | bytes 74784 | tf_op jit(solution)/shard_map/ppermute | solution.py:28
  14.5 0.0 collective-permute-done.4.refs_1_
  14.5 0.0 collective-permute-done.6.refs_2_
  14.5 0.0 collective-permute-done.8.refs_3_
  14.5 2.2 %shard_map.68 = f32[1168,128]{1,0:T(8,128)} custom-call(bf16[292,128]{1,0:T(8,128)(2,1)S(1)} %collective-permute-done.1.refs_0_, bf16[432,128]{1,0:T(8,128)(2,1)S(1)} %collective-permute-done.4.refs_1_, bf16[292,128]{1,0:T(8,128)(2,1)S(1)} %collective-permute-done.6.refs_2_, bf16[292,128]{1,0:T(8,128)(2,1)S(1)} %collective-permute-done.8.refs_3_, ...), custom_call_target="tpu_custom_call" | custom-call | tf_op jit(solution)/shard_map/pallas_call | solution.py:330
  (1 shorter events, 0.0 us)
Async XLA Ops:
  1.8 3.2 %collective-permute-start.3 = (bf16[1664,128]{1,0:T(8,128)(2,1)S(1)}, bf16[1664,128]{1,0:T(8,128)(2,1)S(1)}, u32[]{:S(2)}, u32[]{:S(2)}) collective-permute-start(bf16[1664,128]{1,0:T(8,128)(2,1)S(1)} %get-tuple-element.22.own_ref), channel_id=1, source_target_pairs={{0,1},{1,0},{2,3},{3,2},{4,5},{5,4},{6,7},{7,6},{8,9},{9,8},{10,11... | collective-permute-start | bytes 1277960 | tf_op jit(solution)/shard_map/ppermute | solution.py:15
  2.3 5.6 %collective-permute-start.2 = (bf16[292,128]{1,0:T(8,128)(2,1)S(1)}, bf16[292,128]{1,0:T(8,128)(2,1)S(1)}, u32[]{:S(2)}, u32[]{:S(2)}) collective-permute-start(bf16[292,128]{1,0:T(8,128)(2,1)S(1)} %get-tuple-element.21), channel_id=1, source_target_pairs={{0,2},{2,0},{1,3},{3,1},{4,6},{6,4},{5,7},{7,5},{8,10},{10,8},{9,1... | collective-permute-start | bytes 224264 | tf_op jit(solution)/shard_map/ppermute | solution.py:33
  4.9 5.2 %collective-permute-start = (bf16[292,128]{1,0:T(8,128)(2,1)S(1)}, bf16[292,128]{1,0:T(8,128)(2,1)S(1)}, u32[]{:S(2)}, u32[]{:S(2)}) collective-permute-start(bf16[292,128]{1,0:T(8,128)(2,1)S(1)} %get-tuple-element.20), channel_id=1, source_target_pairs={{0,2},{2,0},{1,3},{3,1},{4,6},{6,4},{5,7},{7,5},{8,10},{10,8},{9,1... | collective-permute-start | bytes 224264 | tf_op jit(solution)/shard_map/ppermute | solution.py:33
  5.5 6.2 %collective-permute-start.5 = (bf16[292,128]{1,0:T(8,128)(2,1)S(1)}, bf16[292,128]{1,0:T(8,128)(2,1)S(1)}, u32[]{:S(2)}, u32[]{:S(2)}) collective-permute-start(bf16[292,128]{1,0:T(8,128)(2,1)S(1)} %get-tuple-element.27), channel_id=1, source_target_pairs={{0,2},{2,0},{1,3},{3,1},{4,6},{6,4},{5,7},{7,5},{8,10},{10,8},{9,1... | collective-permute-start | bytes 224264 | tf_op jit(solution)/shard_map/ppermute | solution.py:33
  7.5 5.2 %collective-permute-start.7 = (bf16[292,128]{1,0:T(8,128)(2,1)S(1)}, bf16[292,128]{1,0:T(8,128)(2,1)S(1)}, u32[]{:S(2)}, u32[]{:S(2)}) collective-permute-start(bf16[292,128]{1,0:T(8,128)(2,1)S(1)} %get-tuple-element.28), channel_id=1, source_target_pairs={{0,2},{2,0},{1,3},{3,1},{4,6},{6,4},{5,7},{7,5},{8,10},{10,8},{9,1... | collective-permute-start | bytes 224264 | tf_op jit(solution)/shard_map/ppermute | solution.py:33
  7.9 6.6 %collective-permute-start.4 = (bf16[432,128]{1,0:T(8,128)(2,1)S(1)}, bf16[432,128]{1,0:T(8,128)(2,1)S(1)}, u32[]{:S(2)}, u32[]{:S(2)}) collective-permute-start(bf16[432,128]{1,0:T(8,128)(2,1)S(1)} %shard_map.66), channel_id=1, source_target_pairs={{1,4},{4,1},{5,8},{8,5},{9,12},{12,9},{0,16},{13,29},{17,20},{20,1... | collective-permute-start | bytes 331784 | tf_op jit(solution)/shard_map/ppermute | solution.py:28
  10.1 4.4 %collective-permute-start.1 = (bf16[292,128]{1,0:T(8,128)(2,1)S(1)}, bf16[292,128]{1,0:T(8,128)(2,1)S(1)}, u32[]{:S(2)}, u32[]{:S(2)}) collective-permute-start(bf16[292,128]{1,0:T(8,128)(2,1)S(1)} %collective-permute-done.refs_0_), channel_id=1, source_target_pairs={{1,4},{4,1},{5,8},{8,5},{9,12},{12,9},{0,16},{13,29},{17,20},{20,1... | collective-permute-start | bytes 224264 | tf_op jit(solution)/shard_map/ppermute | solution.py:28
  11.6 2.8 %collective-permute-start.6 = (bf16[292,128]{1,0:T(8,128)(2,1)S(1)}, bf16[292,128]{1,0:T(8,128)(2,1)S(1)}, u32[]{:S(2)}, u32[]{:S(2)}) collective-permute-start(bf16[292,128]{1,0:T(8,128)(2,1)S(1)} %collective-permute-done.5.refs_2_), channel_id=1, source_target_pairs={{0,1},{1,0},{2,3},{3,2},{4,5},{5,4},{6,7},{7,6},{8,9},{9,8},{10,11... | collective-permute-start | bytes 224264 | tf_op jit(solution)/shard_map/ppermute | solution.py:15
  12.6 1.8 %collective-permute-start.8 = (bf16[292,128]{1,0:T(8,128)(2,1)S(1)}, bf16[292,128]{1,0:T(8,128)(2,1)S(1)}, u32[]{:S(2)}, u32[]{:S(2)}) collective-permute-start(bf16[292,128]{1,0:T(8,128)(2,1)S(1)} %collective-permute-done.7.refs_3_), channel_id=1, source_target_pairs={{0,1},{1,0},{2,3},{3,2},{4,5},{5,4},{6,7},{7,6},{8,9},{9,8},{10,11... | collective-permute-start | bytes 224264 | tf_op jit(solution)/shard_map/ppermute | solution.py:15

commit v5 on v4

--- a/solution.py
+++ b/solution.py
@@ -93,22 +93,23 @@
     fetches = [
         fetch(i, src, dst)
         for i, (src, dst) in enumerate(
-            ((layer_ref, layers), (mask_ref, mask), (innov_ref, innov), (slope_ref, slope))
+            ((layer_ref, layers), (mask_ref, mask), (innov_ref, innov), (slope_ref, raw_ref.at[18 * half:]))
         )
     ]
     fetches[0].wait()
     layer = layers[lax.axis_index("tm")]
-    fetches += [fetch(4, out_ref.at[layer], taps_out), fetch(5, in_ref.at[layer], taps_in)]
+    for i, (src, dst) in enumerate(((out_ref, taps_out), (in_ref, taps_in))):
+        fetches += [fetch(4 + 3 * i + a, src.at[layer, a], dst.at[a]) for a in range(3)]
     fetches[1].wait()
     fetches[2].wait()
     wide[...] = innov[...].astype(jnp.float32) * tile_mask(mask, cells)
     split_rows((fronts, states, cells), wide, piece, pieces)
     forcing_ref[...] = wide[...].astype(jnp.bfloat16)
     fetches[3].wait()
-    raw_ref[18 * half:, :] = slope[...]
     for i, taps in enumerate((taps_out, taps_in)):
-        fetches[4 + i].wait()
         for t in range(9):
+            if t % 3 == 0:
+                fetches[4 + 3 * i + t // 3].wait()
             start = (9 * i + t) * half
             raw_ref[start:start + half, :states] = taps[t // 3, t % 3]
 
@@ -269,7 +270,7 @@
             pltpu.VMEM((3, 3, half, states), jnp.bfloat16),
             pltpu.VMEM(flat, jnp.float32),
             piece_wide,
-            pltpu.SemaphoreType.DMA((6,)),
+            pltpu.SemaphoreType.DMA((10,)),
         ],
         compiler_params=modest,
     )(
@@ -294,7 +295,6 @@
         scratch_shapes=[pltpu.VMEM((8 * half, cells), jnp.float32)],
         compiler_params=modest,
     )(raw_own, raw_away)
-    edge, sent = lax.optimization_barrier((edge, sent))
     inner = [to_earlier(block) for block in sent[pairs:]]
 
     for hop in range(1, owners):

time: 16.8 us -> 16.7 us (level)
  no operation moved by 1% of the time
where the time goes in v5:
time: 16.7 us; the launch traced here: 16.6 us
  starting transfers between devices  9.1 us (54%)
  Pallas kernels  5.05 us (30%)
  waiting for transfers between devices  2.39 us (14%)
    ppermute x4, starting transfers between devices, to_earlier(): lax.ppermute(block, 'tm', [(i, (i - 1) % count) for i in range(count)])  4.68 us
    ppermute x2, starting transfers between devices, swap_lat(): return lax.ppermute(block, ('grp', 'lat', 'chan'), route)  3.73 us
    pallas_call x1, Pallas kernels, per_device(): pl.pallas_call(functools.partial(step_kernel, sizes), out_shape=array(fla...  2.17 us
    pallas_call x1, Pallas kernels, per_device(): pl.pallas_call(functools.partial(first_kernel, (fronts, states, cells, ha...  1.7 us
    ppermute x4, waiting for transfers between devices, to_earlier(): lax.ppermute(block, 'tm', [(i, (i - 1) % count) for i in range(count)])  1.21 us
    ppermute x2, waiting for transfers between devices, swap_lat(): return lax.ppermute(block, ('grp', 'lat', 'chan'), route)  1.16 us
    ppermute x3, starting transfers between devices, swap_chan(): return lax.ppermute(block, 'chan', [(0, 1), (1, 0)])  0.69 us
    pallas_call x1, Pallas kernels, per_device(): pl.pallas_call(functools.partial(own_kernel, sizes), out_shape=(array((4...  0.65 us
  transfers between devices with their start and end apart: 9, of which 3 were waited for; matrix products, arithmetic and copies ran while one was open for 0% of the time, Pallas kernels for 7%

profile of v5, /device:TPU:0, one launch (start us, length us, event | category | flops | bytes accessed | tf_op | source)
XLA Modules:
  0.0 16.6 jit_solution(7116157480169662528)
XLA Ops:
  0.0 1.7 %shard_map.64 = (bf16[292,128]{1,0:T(8,128)(2,1)S(1)}, bf16[292,128]{1,0:T(8,128)(2,1)S(1)}, bf16[292,128]{1,0:T(8,128)(2,1)S(1)}, bf16[292,128]{1,0:T(8,128)(2,...) custom-call(s32[2]{0:T(128)} %layer_ref.1, s32[4]{0:T(128)} %bitcast.10, bf16[1168,128]{1,0:T(8,128)(2,1)} %bitcast.8, ...), custom_call_target="tpu_custom_call" | custom-call | tf_op jit(solution)/shard_map/pallas_call | solution.py:259
  1.7 0.5 %collective-permute-start.3 = (bf16[1664,128]{1,0:T(8,128)(2,1)S(1)}, bf16[1664,128]{1,0:T(8,128)(2,1)S(1)}, u32[]{:S(2)}, u32[]{:S(2)}) collective-permute-start(bf16[1664,128]{1,0:T(8,128)(2,1)S(1)} %get-tuple-element.19.own_ref), channel_id=1, source_target_pairs={{0,1},{1,0},{2,3},{3,2},{4,5},{5,4},{6,7},{7,6},{8,9},{9,8},{10,11... | collective-permute-start | bytes 1277960 | tf_op jit(solution)/shard_map/ppermute | solution.py:15
  2.2 2.6 %collective-permute-start.2 = (bf16[292,128]{1,0:T(8,128)(2,1)S(1)}, bf16[292,128]{1,0:T(8,128)(2,1)S(1)}, u32[]{:S(2)}, u32[]{:S(2)}) collective-permute-start(bf16[292,128]{1,0:T(8,128)(2,1)S(1)} %get-tuple-element.18), channel_id=1, source_target_pairs={{0,2},{2,0},{1,3},{3,1},{4,6},{6,4},{5,7},{7,5},{8,10},{10,8},{9,1... | collective-permute-start | bytes 224264 | tf_op jit(solution)/shard_map/ppermute | solution.py:33
  4.8 0.1 collective-permute-start
  4.9 1.9 %collective-permute-start.5 = (bf16[292,128]{1,0:T(8,128)(2,1)S(1)}, bf16[292,128]{1,0:T(8,128)(2,1)S(1)}, u32[]{:S(2)}, u32[]{:S(2)}) collective-permute-start(bf16[292,128]{1,0:T(8,128)(2,1)S(1)} %get-tuple-element.21), channel_id=1, source_target_pairs={{0,2},{2,0},{1,3},{3,1},{4,6},{6,4},{5,7},{7,5},{8,10},{10,8},{9,1... | collective-permute-start | bytes 224264 | tf_op jit(solution)/shard_map/ppermute | solution.py:33
  6.8 0.1 collective-permute-start.7
  6.9 0.0 collective-permute-done.3.away_ref
  6.9 0.5 %shard_map.65 = (bf16[384,256]{1,0:T(8,128)(2,1)S(1)}, bf16[240,384]{1,0:T(8,128)(2,1)S(1)}, bf16[768,128]{1,0:T(8,128)(2,1)S(1)}, bf16[128,128]{1,0:T(8,128)(2,1)S(1)}) custom-call(bf16[1664,128]{1,0:T(8,128)(2,1)S(1)} %get-tuple-element.19.own_ref, bf16[1664,128]{1,0:T(8,128)(2,1)S(1)} %collective-permute-done.3.away_ref), custom_call_target="tpu_custom_call" | custom-call | tf_op jit(solution)/shard_map/pallas_call | solution.py:287
  7.4 0.4 %collective-permute-done.2.piece_ref.refs_1_ = bf16[292,128]{1,0:T(8,128)(2,1)S(1)} collective-permute-done((bf16[292,128]{1,0:T(8,128)(2,1)S(1)}, bf16[292,128]{1,0:T(8,128)(2,1)S(1)}, u32[]{:S(2)}, u32[]{:S(2)}) %collective-permute-start.2) | collective-permute-done | bytes 74784 | tf_op jit(solution)/shard_map/ppermute | solution.py:33
  7.8 2.2 %collective-permute-start.4 = (bf16[432,128]{1,0:T(8,128)(2,1)S(1)}, bf16[432,128]{1,0:T(8,128)(2,1)S(1)}, u32[]{:S(2)}, u32[]{:S(2)}) collective-permute-start(bf16[432,128]{1,0:T(8,128)(2,1)S(1)} %shard_map.66), channel_id=1, source_target_pairs={{1,4},{4,1},{5,8},{8,5},{9,12},{12,9},{0,16},{13,29},{17,20},{20,1... | collective-permute-start | bytes 331784 | tf_op jit(solution)/shard_map/ppermute | solution.py:28
  10.0 0.0 collective-permute-done.refs_0_
  10.0 1.5 %collective-permute-start.1 = (bf16[292,128]{1,0:T(8,128)(2,1)S(1)}, bf16[292,128]{1,0:T(8,128)(2,1)S(1)}, u32[]{:S(2)}, u32[]{:S(2)}) collective-permute-start(bf16[292,128]{1,0:T(8,128)(2,1)S(1)} %collective-permute-done.refs_0_), channel_id=1, source_target_pairs={{1,4},{4,1},{5,8},{8,5},{9,12},{12,9},{0,16},{13,29},{17,20},{20,1... | collective-permute-start | bytes 224264 | tf_op jit(solution)/shard_map/ppermute | solution.py:28
  11.6 0.0 collective-permute-done.5.refs_2_
  11.6 0.2 %collective-permute-start.6 = (bf16[292,128]{1,0:T(8,128)(2,1)S(1)}, bf16[292,128]{1,0:T(8,128)(2,1)S(1)}, u32[]{:S(2)}, u32[]{:S(2)}) collective-permute-start(bf16[292,128]{1,0:T(8,128)(2,1)S(1)} %collective-permute-done.5.refs_2_), channel_id=1, source_target_pairs={{0,1},{1,0},{2,3},{3,2},{4,5},{5,4},{6,7},{7,6},{8,9},{9,8},{10,11... | collective-permute-start | bytes 224264 | tf_op jit(solution)/shard_map/ppermute | solution.py:15
  11.7 0.8 %collective-permute-done.7.refs_3_ = bf16[292,128]{1,0:T(8,128)(2,1)S(1)} collective-permute-done((bf16[292,128]{1,0:T(8,128)(2,1)S(1)}, bf16[292,128]{1,0:T(8,128)(2,1)S(1)}, u32[]{:S(2)}, u32[]{:S(2)}) %collective-permute-start.7) | collective-permute-done | bytes 74784 | tf_op jit(solution)/shard_map/ppermute | solution.py:33
  12.6 0.0 collective-permute-start.8
  12.6 0.7 %shard_map.67 = (bf16[320,512]{1,0:T(8,128)(2,1)S(1)}, bf16[256,512]{1,0:T(8,128)(2,1)S(1)}) custom-call(bf16[292,128]{1,0:T(8,128)(2,1)S(1)} %collective-permute-done.refs_0_, bf16[292,128]{1,0:T(8,128)(2,1)S(1)} %collective-permute-done.2.piece_ref.refs_1_, bf16[292,128]{1,0:T(8,128)(2,1)S(1)} %collective-permute-done.5.refs_2_, ...), custom_call_target="tpu_custom_call" | custom-call | tf_op jit(solution)/shard_map/pallas_call | solution.py:322
  13.2 1.2 %collective-permute-done.1.refs_0_ = bf16[292,128]{1,0:T(8,128)(2,1)S(1)} collective-permute-done((bf16[292,128]{1,0:T(8,128)(2,1)S(1)}, bf16[292,128]{1,0:T(8,128)(2,1)S(1)}, u32[]{:S(2)}, u32[]{:S(2)}) %collective-permute-start.1) | collective-permute-done | bytes 74784 | tf_op jit(solution)/shard_map/ppermute | solution.py:28
  14.4 0.0 collective-permute-done.6.refs_2_
  14.4 0.0 collective-permute-done.8.refs_3_
  14.4 0.0 collective-permute-done.4.refs_1_
  14.4 2.2 %shard_map.68 = f32[1168,128]{1,0:T(8,128)} custom-call(bf16[292,128]{1,0:T(8,128)(2,1)S(1)} %collective-permute-done.1.refs_0_, bf16[432,128]{1,0:T(8,128)(2,1)S(1)} %collective-permute-done.4.refs_1_, bf16[292,128]{1,0:T(8,128)(2,1)S(1)} %collective-permute-done.6.refs_2_, bf16[292,128]{1,0:T(8,128)(2,1)S(1)} %collective-permute-done.8.refs_3_, ...), custom_call_target="tpu_custom_call" | custom-call | tf_op jit(solution)/shard_map/pallas_call | solution.py:330
  (1 shorter events, 0.0 us)
Async XLA Ops:
  1.7 5.2 %collective-permute-start.3 = (bf16[1664,128]{1,0:T(8,128)(2,1)S(1)}, bf16[1664,128]{1,0:T(8,128)(2,1)S(1)}, u32[]{:S(2)}, u32[]{:S(2)}) collective-permute-start(bf16[1664,128]{1,0:T(8,128)(2,1)S(1)} %get-tuple-element.19.own_ref), channel_id=1, source_target_pairs={{0,1},{1,0},{2,3},{3,2},{4,5},{5,4},{6,7},{7,6},{8,9},{9,8},{10,11... | collective-permute-start | bytes 1277960 | tf_op jit(solution)/shard_map/ppermute | solution.py:15
  2.2 5.6 %collective-permute-start.2 = (bf16[292,128]{1,0:T(8,128)(2,1)S(1)}, bf16[292,128]{1,0:T(8,128)(2,1)S(1)}, u32[]{:S(2)}, u32[]{:S(2)}) collective-permute-start(bf16[292,128]{1,0:T(8,128)(2,1)S(1)} %get-tuple-element.18), channel_id=1, source_target_pairs={{0,2},{2,0},{1,3},{3,1},{4,6},{6,4},{5,7},{7,5},{8,10},{10,8},{9,1... | collective-permute-start | bytes 224264 | tf_op jit(solution)/shard_map/ppermute | solution.py:33
  4.8 5.2 %collective-permute-start = (bf16[292,128]{1,0:T(8,128)(2,1)S(1)}, bf16[292,128]{1,0:T(8,128)(2,1)S(1)}, u32[]{:S(2)}, u32[]{:S(2)}) collective-permute-start(bf16[292,128]{1,0:T(8,128)(2,1)S(1)} %get-tuple-element.17), channel_id=1, source_target_pairs={{0,2},{2,0},{1,3},{3,1},{4,6},{6,4},{5,7},{7,5},{8,10},{10,8},{9,1... | collective-permute-start | bytes 224264 | tf_op jit(solution)/shard_map/ppermute | solution.py:33
  4.9 6.7 %collective-permute-start.5 = (bf16[292,128]{1,0:T(8,128)(2,1)S(1)}, bf16[292,128]{1,0:T(8,128)(2,1)S(1)}, u32[]{:S(2)}, u32[]{:S(2)}) collective-permute-start(bf16[292,128]{1,0:T(8,128)(2,1)S(1)} %get-tuple-element.21), channel_id=1, source_target_pairs={{0,2},{2,0},{1,3},{3,1},{4,6},{6,4},{5,7},{7,5},{8,10},{10,8},{9,1... | collective-permute-start | bytes 224264 | tf_op jit(solution)/shard_map/ppermute | solution.py:33
  6.8 5.8 %collective-permute-start.7 = (bf16[292,128]{1,0:T(8,128)(2,1)S(1)}, bf16[292,128]{1,0:T(8,128)(2,1)S(1)}, u32[]{:S(2)}, u32[]{:S(2)}) collective-permute-start(bf16[292,128]{1,0:T(8,128)(2,1)S(1)} %get-tuple-element.22), channel_id=1, source_target_pairs={{0,2},{2,0},{1,3},{3,1},{4,6},{6,4},{5,7},{7,5},{8,10},{10,8},{9,1... | collective-permute-start | bytes 224264 | tf_op jit(solution)/shard_map/ppermute | solution.py:33
  7.8 6.6 %collective-permute-start.4 = (bf16[432,128]{1,0:T(8,128)(2,1)S(1)}, bf16[432,128]{1,0:T(8,128)(2,1)S(1)}, u32[]{:S(2)}, u32[]{:S(2)}) collective-permute-start(bf16[432,128]{1,0:T(8,128)(2,1)S(1)} %shard_map.66), channel_id=1, source_target_pairs={{1,4},{4,1},{5,8},{8,5},{9,12},{12,9},{0,16},{13,29},{17,20},{20,1... | collective-permute-start | bytes 331784 | tf_op jit(solution)/shard_map/ppermute | solution.py:28
  10.0 4.4 %collective-permute-start.1 = (bf16[292,128]{1,0:T(8,128)(2,1)S(1)}, bf16[292,128]{1,0:T(8,128)(2,1)S(1)}, u32[]{:S(2)}, u32[]{:S(2)}) collective-permute-start(bf16[292,128]{1,0:T(8,128)(2,1)S(1)} %collective-permute-done.refs_0_), channel_id=1, source_target_pairs={{1,4},{4,1},{5,8},{8,5},{9,12},{12,9},{0,16},{13,29},{17,20},{20,1... | collective-permute-start | bytes 224264 | tf_op jit(solution)/shard_map/ppermute | solution.py:28
  11.6 2.8 %collective-permute-start.6 = (bf16[292,128]{1,0:T(8,128)(2,1)S(1)}, bf16[292,128]{1,0:T(8,128)(2,1)S(1)}, u32[]{:S(2)}, u32[]{:S(2)}) collective-permute-start(bf16[292,128]{1,0:T(8,128)(2,1)S(1)} %collective-permute-done.5.refs_2_), channel_id=1, source_target_pairs={{0,1},{1,0},{2,3},{3,2},{4,5},{5,4},{6,7},{7,6},{8,9},{9,8},{10,11... | collective-permute-start | bytes 224264 | tf_op jit(solution)/shard_map/ppermute | solution.py:15
  12.6 1.8 %collective-permute-start.8 = (bf16[292,128]{1,0:T(8,128)(2,1)S(1)}, bf16[292,128]{1,0:T(8,128)(2,1)S(1)}, u32[]{:S(2)}, u32[]{:S(2)}) collective-permute-start(bf16[292,128]{1,0:T(8,128)(2,1)S(1)} %collective-permute-done.7.refs_3_), channel_id=1, source_target_pairs={{0,1},{1,0},{2,3},{3,2},{4,5},{5,4},{6,7},{7,6},{8,9},{9,8},{10,11... | collective-permute-start | bytes 224264 | tf_op jit(solution)/shard_map/ppermute | solution.py:15

commit v6 on v5

--- a/solution.py
+++ b/solution.py
@@ -69,6 +69,11 @@
             spot = pl.ds(pl.multiple_of(start + i * pitch, 16), states)
             lanes = slice((front + f) * cells, (front + f + 1) * cells)
             field[spot, lanes] = rows.astype(jnp.bfloat16)
+
+
+def outside_grid():
+    chan, band = lax.axis_index("chan"), lax.axis_index("lat")
+    return (band == 0) & (chan == 0) | (band == lax.axis_size("lat") - 1) & (chan == 1)
 
 
 def split_kernel(dims, state_ref, *refs):
@@ -145,12 +150,14 @@
     second_ref[...] = turned[:3 * pitch].astype(jnp.bfloat16)
 
 
-def hidden_row(dims, j, first_ref, slope, field, hidden_grad, spot):
+def hidden_row(dims, j, first_ref, slope, field, hidden_grad, pairs):
     fronts, pitch, hidden, cells = dims
-    for pair in range(fronts // 2):
+    near = pl.ds(pl.multiple_of(j * pitch, 16), 3 * pitch)
+    spot = pl.ds(pl.multiple_of(j * hidden, 16), hidden)
+    for pair in pairs:
         taps = jnp.dot(
             first_ref[:, :3 * pitch],
-            field[j * pitch:(j + 3) * pitch, 2 * pair * cells:2 * (pair + 1) * cells],
+            field[near, 2 * pair * cells:2 * (pair + 1) * cells],
             preferred_element_type=jnp.float32,
         )
         for f in range(2):
@@ -161,7 +168,7 @@
                 + lane_shift(taps[2 * hidden:3 * hidden, lanes], 1)
             )
             start = (2 * pair + f) * cells
-            hidden_grad[spot:spot + hidden, start:start + cells] = (slope * total).astype(jnp.bfloat16)
+            hidden_grad[spot, start:start + cells] = (slope * total).astype(jnp.bfloat16)
 
 
 def join_kernel(join, piece_ref, edge_ref, joined_ref):
@@ -172,44 +179,60 @@
 def own_kernel(dims, *refs):
     fronts, states, pitch, hidden, cells = dims
     pieces = refs[:fronts]
-    first_ref, slope_ref, field_ref, hidden_ref, piece = refs[fronts:]
+    halo_ref, first_ref, slope_ref, field_ref, hidden_ref, piece = refs[fronts:]
+    sizes = (fronts, pitch, hidden, cells)
     chan = lax.axis_index("chan")
     live = lax.axis_index("tm") < lax.axis_size("tm") - 1
     field_ref[...] = jnp.zeros_like(field_ref)
     for p, ref in enumerate(pieces):
-        start = (chan if p < fronts // 2 else 1 - chan) * 2 * pitch
+        start = ((chan if p < fronts // 2 else 1 - chan) + 1) * 2 * pitch
         front = 2 * (p % (fronts // 2))
         spread_rows((states, pitch, cells), ref, front, piece, field_ref, start, live)
-    for j in range(2):
-        slope = slope_ref[(j + 2) * hidden:(j + 3) * hidden, :].astype(jnp.float32)
-        hidden_row((fronts, pitch, hidden, cells), j, first_ref, slope, field_ref, hidden_ref, j * hidden)
+    for j in (2, 3):
+        slope = slope_ref[j * hidden:(j + 1) * hidden, :].astype(jnp.float32)
+        hidden_row(sizes, j, first_ref, slope, field_ref, hidden_ref, range(fronts // 2))
+    pair = fronts // 2 - 1
+    outside = outside_grid()
+    spread_rows(
+        (states, pitch, cells), halo_ref, 2 * pair, piece, field_ref, chan * 6 * pitch, live & ~outside
+    )
+    edge = halo_ref[halo_ref.shape[0] - hidden:, :].astype(jnp.float32)
+    for i in range(2):
+        j = 4 * chan + i
+        slope = slope_ref[pl.ds(pl.multiple_of(j * hidden, 16), hidden), :].astype(jnp.float32)
+        slope = jnp.where(chan == i, jnp.where(outside, 0.0, edge), slope)
+        hidden_row(sizes, j, first_ref, slope, field_ref, hidden_ref, (pair,))
 
 
 def step_kernel(dims, *refs):
     fronts, states, pitch, hidden, cells = dims
     pieces = refs[:fronts]
-    own_ref, middle_ref, forcing_ref, first_ref, second_ref, slope_ref = refs[fronts:fronts + 6]
+    _, _, forcing_ref, first_ref, second_ref, slope_ref = refs[fronts:fronts + 6]
     result_ref, field, hidden_grad, piece, result, sem = refs[fronts + 6:]
     edge_ref = pieces[fronts // 2 - 1]
     edge = edge_ref.shape[0] - hidden
-    chan, band = lax.axis_index("chan"), lax.axis_index("lat")
+    chan = lax.axis_index("chan")
     rows = 4
+    sizes = (fronts, pitch, hidden, cells)
     live = lax.axis_index("tm") < lax.axis_size("tm") - 1
-    border = (band == 0) & (chan == 0) | (band == lax.axis_size("lat") - 1) & (chan == 1)
-    field[...] = jnp.zeros_like(field)
+    border = outside_grid()
     for p, ref in enumerate(pieces):
+        if p == fronts // 2 - 1:
+            continue
         used = live & ~border if p < fronts // 2 else live
         start = (chan if p < fronts // 2 else 1 - chan) * 6 * pitch
         front = 2 * (p % (fronts // 2))
         spread_rows((states, pitch, cells), ref, front, piece, field, start, used)
-    field[2 * pitch:6 * pitch, :] = own_ref[...]
-    hidden_grad[2 * hidden:4 * hidden, :] = middle_ref[...]
     for j in (0, 1, rows, rows + 1):
         slope = slope_ref[j * hidden:(j + 1) * hidden, :].astype(jnp.float32)
         if j in (0, rows + 1):
             beyond = jnp.where(border, 0.0, edge_ref[edge:, :].astype(jnp.float32))
             slope = jnp.where(chan == (0 if j == 0 else 1), beyond, slope)
-        hidden_row((fronts, pitch, hidden, cells), j, first_ref, slope, field, hidden_grad, j * hidden)
+        hidden_row(sizes, j, first_ref, slope, field, hidden_grad, range(fronts // 2 - 1))
+    for i in range(2):
+        j = 4 * (1 - chan) + i
+        slope = slope_ref[pl.ds(pl.multiple_of(j * hidden, 16), hidden), :].astype(jnp.float32)
+        hidden_row(sizes, j, first_ref, slope, field, hidden_grad, (fronts // 2 - 1,))
 
     size = 2 * states * rows
     copies = []
@@ -321,20 +344,19 @@
         sizes = (fronts, states, pitch, hidden, cells)
         own, middle = pl.pallas_call(
             functools.partial(own_kernel, sizes),
-            out_shape=(array((4 * pitch, fronts * cells)), array((2 * hidden, fronts * cells))),
-            in_specs=[VMEM] * (fronts + 2),
+            out_shape=(array(field_shape), array(hidden_shape)),
+            in_specs=[VMEM] * (fronts + 3),
             out_specs=(VMEM, VMEM),
             scratch_shapes=[piece_wide],
             compiler_params=modest,
-        )(*outer, *inner, first, slope)
-        result = pl.pallas_call(
+        )(*outer, *inner, halo[-1], first, slope)
+        result, _, _ = pl.pallas_call(
             functools.partial(step_kernel, sizes),
-            out_shape=array(flat, jnp.float32),
+            out_shape=(array(flat, jnp.float32), array(field_shape), array(hidden_shape)),
             in_specs=[VMEM] * (fronts + 6),
-            out_specs=HBM,
+            out_specs=(HBM, VMEM, VMEM),
+            input_output_aliases={fronts: 1, fronts + 1: 2},
             scratch_shapes=[
-                pltpu.VMEM(field_shape, jnp.bfloat16),
-                pltpu.VMEM(hidden_shape, jnp.bfloat16),
                 piece_wide,
                 pltpu.VMEM(flat, jnp.float32),
                 pltpu.SemaphoreType.DMA((fronts // 2,)),

time: 16.7 us -> 16.7 us (level)
  waiting for transfers between devices: 2.39 us -> 2.2 us
    ppermute x2, waiting for transfers between devices: 1.16 us -> 0.98 us  [swap_lat(): return lax.ppermute(block, ('grp', 'lat', 'chan'), route)]
  transfers between devices with their start and end apart: 9 -> 9, of which waited for: 3 -> 4; matrix products, arithmetic and copies ran while one was open for 0% -> 0% of each run, Pallas kernels for 7% -> 8%
where the time goes in v6:
time: 16.7 us; the launch traced here: 16.5 us
  starting transfers between devices  9.1 us (54%)
  Pallas kernels  5.17 us (31%)
  waiting for transfers between devices  2.2 us (13%)
    ppermute x4, starting transfers between devices, to_earlier(): lax.ppermute(block, 'tm', [(i, (i - 1) % count) for i in range(count)])  4.68 us
    ppermute x2, starting transfers between devices, swap_lat(): return lax.ppermute(block, ('grp', 'lat', 'chan'), route)  3.73 us
    pallas_call x1, Pallas kernels, per_device(): pl.pallas_call(functools.partial(step_kernel, sizes), out_shape=(array(fl...  2.11 us
    pallas_call x1, Pallas kernels, per_device(): pl.pallas_call(functools.partial(first_kernel, (fronts, states, cells, ha...  1.7 us
    ppermute x4, waiting for transfers between devices, to_earlier(): lax.ppermute(block, 'tm', [(i, (i - 1) % count) for i in range(count)])  1.21 us
    ppermute x2, waiting for transfers between devices, swap_lat(): return lax.ppermute(block, ('grp', 'lat', 'chan'), route)  0.98 us
    pallas_call x1, Pallas kernels, per_device(): pl.pallas_call(functools.partial(own_kernel, sizes), out_shape=(array(fie...  0.84 us
    ppermute x3, starting transfers between devices, swap_chan(): return lax.ppermute(block, 'chan', [(0, 1), (1, 0)])  0.69 us
  transfers between devices with their start and end apart: 9, of which 4 were waited for; matrix products, arithmetic and copies ran while one was open for 0% of the time, Pallas kernels for 8%

profile of v6, /device:TPU:0, one launch (start us, length us, event | category | flops | bytes accessed | tf_op | source)
XLA Modules:
  0.0 16.5 jit_solution(4326321604328686062)
XLA Ops:
  0.0 1.7 %shard_map.64 = (bf16[292,128]{1,0:T(8,128)(2,1)S(1)}, bf16[292,128]{1,0:T(8,128)(2,1)S(1)}, bf16[292,128]{1,0:T(8,128)(2,1)S(1)}, bf16[292,128]{1,0:T(8,128)(2,...) custom-call(s32[2]{0:T(128)} %layer_ref.1, s32[4]{0:T(128)} %bitcast.10, bf16[1168,128]{1,0:T(8,128)(2,1)} %bitcast.8, ...), custom_call_target="tpu_custom_call" | custom-call | tf_op jit(solution)/shard_map/pallas_call | solution.py:282
  1.7 0.5 %collective-permute-start.3 = (bf16[1664,128]{1,0:T(8,128)(2,1)S(1)}, bf16[1664,128]{1,0:T(8,128)(2,1)S(1)}, u32[]{:S(2)}, u32[]{:S(2)}) collective-permute-start(bf16[1664,128]{1,0:T(8,128)(2,1)S(1)} %get-tuple-element.20.own_ref), channel_id=1, source_target_pairs={{0,1},{1,0},{2,3},{3,2},{4,5},{5,4},{6,7},{7,6},{8,9},{9,8},{10,11... | collective-permute-start | bytes 1277960 | tf_op jit(solution)/shard_map/ppermute | solution.py:15
  2.2 2.6 %collective-permute-start.2 = (bf16[292,128]{1,0:T(8,128)(2,1)S(1)}, bf16[292,128]{1,0:T(8,128)(2,1)S(1)}, u32[]{:S(2)}, u32[]{:S(2)}) collective-permute-start(bf16[292,128]{1,0:T(8,128)(2,1)S(1)} %get-tuple-element.19), channel_id=1, source_target_pairs={{0,2},{2,0},{1,3},{3,1},{4,6},{6,4},{5,7},{7,5},{8,10},{10,8},{9,1... | collective-permute-start | bytes 224264 | tf_op jit(solution)/shard_map/ppermute | solution.py:33
  4.8 0.1 collective-permute-start
  4.9 1.9 %collective-permute-start.5 = (bf16[292,128]{1,0:T(8,128)(2,1)S(1)}, bf16[292,128]{1,0:T(8,128)(2,1)S(1)}, u32[]{:S(2)}, u32[]{:S(2)}) collective-permute-start(bf16[292,128]{1,0:T(8,128)(2,1)S(1)} %get-tuple-element.22), channel_id=1, source_target_pairs={{0,2},{2,0},{1,3},{3,1},{4,6},{6,4},{5,7},{7,5},{8,10},{10,8},{9,1... | collective-permute-start | bytes 224264 | tf_op jit(solution)/shard_map/ppermute | solution.py:33
  6.8 0.1 collective-permute-start.7
  6.9 0.0 collective-permute-done.3.away_ref
  6.9 0.5 %shard_map.65 = (bf16[384,256]{1,0:T(8,128)(2,1)S(1)}, bf16[240,384]{1,0:T(8,128)(2,1)S(1)}, bf16[768,128]{1,0:T(8,128)(2,1)S(1)}, bf16[128,128]{1,0:T(8,128)(2,1)S(1)}) custom-call(bf16[1664,128]{1,0:T(8,128)(2,1)S(1)} %get-tuple-element.20.own_ref, bf16[1664,128]{1,0:T(8,128)(2,1)S(1)} %collective-permute-done.3.away_ref), custom_call_target="tpu_custom_call" | custom-call | tf_op jit(solution)/shard_map/pallas_call | solution.py:310
  7.4 0.4 %collective-permute-done.2.piece_ref.refs_1_ = bf16[292,128]{1,0:T(8,128)(2,1)S(1)} collective-permute-done((bf16[292,128]{1,0:T(8,128)(2,1)S(1)}, bf16[292,128]{1,0:T(8,128)(2,1)S(1)}, u32[]{:S(2)}, u32[]{:S(2)}) %collective-permute-start.2) | collective-permute-done | bytes 74784 | tf_op jit(solution)/shard_map/ppermute | solution.py:33
  7.8 2.2 %collective-permute-start.4 = (bf16[432,128]{1,0:T(8,128)(2,1)S(1)}, bf16[432,128]{1,0:T(8,128)(2,1)S(1)}, u32[]{:S(2)}, u32[]{:S(2)}) collective-permute-start(bf16[432,128]{1,0:T(8,128)(2,1)S(1)} %shard_map.66), channel_id=1, source_target_pairs={{1,4},{4,1},{5,8},{8,5},{9,12},{12,9},{0,16},{13,29},{17,20},{20,1... | collective-permute-start | bytes 331784 | tf_op jit(solution)/shard_map/ppermute | solution.py:28
  10.0 0.0 collective-permute-done.refs_0_
  10.0 1.5 %collective-permute-start.1 = (bf16[292,128]{1,0:T(8,128)(2,1)S(1)}, bf16[292,128]{1,0:T(8,128)(2,1)S(1)}, u32[]{:S(2)}, u32[]{:S(2)}) collective-permute-start(bf16[292,128]{1,0:T(8,128)(2,1)S(1)} %collective-permute-done.refs_0_), channel_id=1, source_target_pairs={{1,4},{4,1},{5,8},{8,5},{9,12},{12,9},{0,16},{13,29},{17,20},{20,1... | collective-permute-start | bytes 224264 | tf_op jit(solution)/shard_map/ppermute | solution.py:28
  11.6 0.0 collective-permute-done.5.refs_2_
  11.6 0.2 %collective-permute-start.6 = (bf16[292,128]{1,0:T(8,128)(2,1)S(1)}, bf16[292,128]{1,0:T(8,128)(2,1)S(1)}, u32[]{:S(2)}, u32[]{:S(2)}) collective-permute-start(bf16[292,128]{1,0:T(8,128)(2,1)S(1)} %collective-permute-done.5.refs_2_), channel_id=1, source_target_pairs={{0,1},{1,0},{2,3},{3,2},{4,5},{5,4},{6,7},{7,6},{8,9},{9,8},{10,11... | collective-permute-start | bytes 224264 | tf_op jit(solution)/shard_map/ppermute | solution.py:15
  11.7 0.8 %collective-permute-done.7.refs_3_ = bf16[292,128]{1,0:T(8,128)(2,1)S(1)} collective-permute-done((bf16[292,128]{1,0:T(8,128)(2,1)S(1)}, bf16[292,128]{1,0:T(8,128)(2,1)S(1)}, u32[]{:S(2)}, u32[]{:S(2)}) %collective-permute-start.7) | collective-permute-done | bytes 74784 | tf_op jit(solution)/shard_map/ppermute | solution.py:33
  12.6 0.0 collective-permute-start.8
  12.6 0.2 %collective-permute-done.4.refs_4_.refs_1_ = bf16[432,128]{1,0:T(8,128)(2,1)S(1)} collective-permute-done((bf16[432,128]{1,0:T(8,128)(2,1)S(1)}, bf16[432,128]{1,0:T(8,128)(2,1)S(1)}, u32[]{:S(2)}, u32[]{:S(2)}) %collective-permute-start.4) | collective-permute-done | bytes 110624 | tf_op jit(solution)/shard_map/ppermute | solution.py:28
  12.7 0.8 %shard_map.67 = (bf16[640,512]{1,0:T(8,128)(2,1)S(1)}, bf16[768,512]{1,0:T(8,128)(2,1)S(1)}) custom-call(bf16[292,128]{1,0:T(8,128)(2,1)S(1)} %collective-permute-done.refs_0_, bf16[292,128]{1,0:T(8,128)(2,1)S(1)} %collective-permute-done.2.piece_ref.refs_1_, bf16[292,128]{1,0:T(8,128)(2,1)S(1)} %collective-permute-done.5.refs_2_, ...), custom_call_target="tpu_custom_call" | custom-call | tf_op jit(solution)/shard_map/pallas_call | solution.py:345
  13.6 0.8 %collective-permute-done.1.refs_0_ = bf16[292,128]{1,0:T(8,128)(2,1)S(1)} collective-permute-done((bf16[292,128]{1,0:T(8,128)(2,1)S(1)}, bf16[292,128]{1,0:T(8,128)(2,1)S(1)}, u32[]{:S(2)}, u32[]{:S(2)}) %collective-permute-start.1) | collective-permute-done | bytes 74784 | tf_op jit(solution)/shard_map/ppermute | solution.py:28
  14.4 0.0 collective-permute-done.6.refs_2_
  14.4 0.0 collective-permute-done.8.refs_3_
  14.4 2.1 %shard_map.68 = (f32[1168,128]{1,0:T(8,128)}, bf16[640,512]{1,0:T(8,128)(2,1)S(1)}, bf16[768,512]{1,0:T(8,128)(2,1)S(1)}) custom-call(bf16[292,128]{1,0:T(8,128)(2,1)S(1)} %collective-permute-done.1.refs_0_, bf16[432,128]{1,0:T(8,128)(2,1)S(1)} %collective-permute-done.4.refs_4_.refs_1_, ...), custom_call_target="tpu_custom_call", output_to_operand_aliasing={{1}: (4, {}), {2}: (5, {})} | custom-call | tf_op jit(solution)/shard_map/pallas_call | solution.py:353
  (1 shorter events, 0.0 us)
Async XLA Ops:
  1.7 5.2 %collective-permute-start.3 = (bf16[1664,128]{1,0:T(8,128)(2,1)S(1)}, bf16[1664,128]{1,0:T(8,128)(2,1)S(1)}, u32[]{:S(2)}, u32[]{:S(2)}) collective-permute-start(bf16[1664,128]{1,0:T(8,128)(2,1)S(1)} %get-tuple-element.20.own_ref), channel_id=1, source_target_pairs={{0,1},{1,0},{2,3},{3,2},{4,5},{5,4},{6,7},{7,6},{8,9},{9,8},{10,11... | collective-permute-start | bytes 1277960 | tf_op jit(solution)/shard_map/ppermute | solution.py:15
  2.2 5.6 %collective-permute-start.2 = (bf16[292,128]{1,0:T(8,128)(2,1)S(1)}, bf16[292,128]{1,0:T(8,128)(2,1)S(1)}, u32[]{:S(2)}, u32[]{:S(2)}) collective-permute-start(bf16[292,128]{1,0:T(8,128)(2,1)S(1)} %get-tuple-element.19), channel_id=1, source_target_pairs={{0,2},{2,0},{1,3},{3,1},{4,6},{6,4},{5,7},{7,5},{8,10},{10,8},{9,1... | collective-permute-start | bytes 224264 | tf_op jit(solution)/shard_map/ppermute | solution.py:33
  4.8 5.2 %collective-permute-start = (bf16[292,128]{1,0:T(8,128)(2,1)S(1)}, bf16[292,128]{1,0:T(8,128)(2,1)S(1)}, u32[]{:S(2)}, u32[]{:S(2)}) collective-permute-start(bf16[292,128]{1,0:T(8,128)(2,1)S(1)} %get-tuple-element.18), channel_id=1, source_target_pairs={{0,2},{2,0},{1,3},{3,1},{4,6},{6,4},{5,7},{7,5},{8,10},{10,8},{9,1... | collective-permute-start | bytes 224264 | tf_op jit(solution)/shard_map/ppermute | solution.py:33
  4.9 6.7 %collective-permute-start.5 = (bf16[292,128]{1,0:T(8,128)(2,1)S(1)}, bf16[292,128]{1,0:T(8,128)(2,1)S(1)}, u32[]{:S(2)}, u32[]{:S(2)}) collective-permute-start(bf16[292,128]{1,0:T(8,128)(2,1)S(1)} %get-tuple-element.22), channel_id=1, source_target_pairs={{0,2},{2,0},{1,3},{3,1},{4,6},{6,4},{5,7},{7,5},{8,10},{10,8},{9,1... | collective-permute-start | bytes 224264 | tf_op jit(solution)/shard_map/ppermute | solution.py:33
  6.8 5.8 %collective-permute-start.7 = (bf16[292,128]{1,0:T(8,128)(2,1)S(1)}, bf16[292,128]{1,0:T(8,128)(2,1)S(1)}, u32[]{:S(2)}, u32[]{:S(2)}) collective-permute-start(bf16[292,128]{1,0:T(8,128)(2,1)S(1)} %get-tuple-element.23), channel_id=1, source_target_pairs={{0,2},{2,0},{1,3},{3,1},{4,6},{6,4},{5,7},{7,5},{8,10},{10,8},{9,1... | collective-permute-start | bytes 224264 | tf_op jit(solution)/shard_map/ppermute | solution.py:33
  7.8 4.9 %collective-permute-start.4 = (bf16[432,128]{1,0:T(8,128)(2,1)S(1)}, bf16[432,128]{1,0:T(8,128)(2,1)S(1)}, u32[]{:S(2)}, u32[]{:S(2)}) collective-permute-start(bf16[432,128]{1,0:T(8,128)(2,1)S(1)} %shard_map.66), channel_id=1, source_target_pairs={{1,4},{4,1},{5,8},{8,5},{9,12},{12,9},{0,16},{13,29},{17,20},{20,1... | collective-permute-start | bytes 331784 | tf_op jit(solution)/shard_map/ppermute | solution.py:28
  10.0 4.4 %collective-permute-start.1 = (bf16[292,128]{1,0:T(8,128)(2,1)S(1)}, bf16[292,128]{1,0:T(8,128)(2,1)S(1)}, u32[]{:S(2)}, u32[]{:S(2)}) collective-permute-start(bf16[292,128]{1,0:T(8,128)(2,1)S(1)} %collective-permute-done.refs_0_), channel_id=1, source_target_pairs={{1,4},{4,1},{5,8},{8,5},{9,12},{12,9},{0,16},{13,29},{17,20},{20,1... | collective-permute-start | bytes 224264 | tf_op jit(solution)/shard_map/ppermute | solution.py:28
  11.6 2.8 %collective-permute-start.6 = (bf16[292,128]{1,0:T(8,128)(2,1)S(1)}, bf16[292,128]{1,0:T(8,128)(2,1)S(1)}, u32[]{:S(2)}, u32[]{:S(2)}) collective-permute-start(bf16[292,128]{1,0:T(8,128)(2,1)S(1)} %collective-permute-done.5.refs_2_), channel_id=1, source_target_pairs={{0,1},{1,0},{2,3},{3,2},{4,5},{5,4},{6,7},{7,6},{8,9},{9,8},{10,11... | collective-permute-start | bytes 224264 | tf_op jit(solution)/shard_map/ppermute | solution.py:15
  12.6 1.8 %collective-permute-start.8 = (bf16[292,128]{1,0:T(8,128)(2,1)S(1)}, bf16[292,128]{1,0:T(8,128)(2,1)S(1)}, u32[]{:S(2)}, u32[]{:S(2)}) collective-permute-start(bf16[292,128]{1,0:T(8,128)(2,1)S(1)} %collective-permute-done.7.refs_3_), channel_id=1, source_target_pairs={{0,1},{1,0},{2,3},{3,2},{4,5},{5,4},{6,7},{7,6},{8,9},{9,8},{10,11... | collective-permute-start | bytes 224264 | tf_op jit(solution)/shard_map/ppermute | solution.py:15

commit v7 on v6

--- a/solution.py
+++ b/solution.py
@@ -179,7 +179,7 @@
 def own_kernel(dims, *refs):
     fronts, states, pitch, hidden, cells = dims
     pieces = refs[:fronts]
-    halo_ref, first_ref, slope_ref, field_ref, hidden_ref, piece = refs[fronts:]
+    halo_ref, forcing_ref, first_ref, slope_ref, field_ref, hidden_ref, ready_ref, piece = refs[fronts:]
     sizes = (fronts, pitch, hidden, cells)
     chan = lax.axis_index("chan")
     live = lax.axis_index("tm") < lax.axis_size("tm") - 1
@@ -191,6 +191,12 @@
     for j in (2, 3):
         slope = slope_ref[j * hidden:(j + 1) * hidden, :].astype(jnp.float32)
         hidden_row(sizes, j, first_ref, slope, field_ref, hidden_ref, range(fronts // 2))
+    ready_ref[...] = forcing_ref[...].astype(jnp.float32)
+    for h in range(4):
+        for f in range(fronts):
+            before = field_ref[(h + 2) * pitch:(h + 3) * pitch, f * cells:(f + 1) * cells].astype(jnp.float32)
+            spots = pl.ds(f * states * 4 + h, states, stride=4)
+            ready_ref[spots, :] = ready_ref[spots, :] + before[:states]
     pair = fronts // 2 - 1
     outside = outside_grid()
     spread_rows(
@@ -207,8 +213,8 @@
 def step_kernel(dims, *refs):
     fronts, states, pitch, hidden, cells = dims
     pieces = refs[:fronts]
-    _, _, forcing_ref, first_ref, second_ref, slope_ref = refs[fronts:fronts + 6]
-    result_ref, field, hidden_grad, piece, result, sem = refs[fronts + 6:]
+    _, _, _, first_ref, second_ref, slope_ref = refs[fronts:fronts + 6]
+    result_ref, field, hidden_grad, result, piece, sem = refs[fronts + 6:]
     edge_ref = pieces[fronts // 2 - 1]
     edge = edge_ref.shape[0] - hidden
     chan = lax.axis_index("chan")
@@ -238,19 +244,16 @@
     copies = []
     for pair in range(fronts // 2):
         part = slice(pair * size, (pair + 1) * size)
-        result[part, :] = forcing_ref[part, :].astype(jnp.float32)
         block = slice(2 * pair * cells, 2 * (pair + 1) * cells)
         for h in range(rows):
             taps = jnp.dot(
                 second_ref[...], hidden_grad[h * hidden:(h + 3) * hidden, block],
                 preferred_element_type=jnp.float32,
             )
-            before = field[(h + 2) * pitch:(h + 3) * pitch, block].astype(jnp.float32)
             for f in range(2):
                 lanes = slice(f * cells, (f + 1) * cells)
                 total = (
-                    before[:, lanes]
-                    + taps[pitch:2 * pitch, lanes]
+                    taps[pitch:2 * pitch, lanes]
                     + lane_shift(taps[0:pitch, lanes], -1)
                     + lane_shift(taps[2 * pitch:3 * pitch, lanes], 1)
                 )
@@ -342,27 +345,26 @@
         halo = [swap_lat(block) for block in outer[:-1] + [joined]]
         other = [swap_chan(block) for block in inner]
         sizes = (fronts, states, pitch, hidden, cells)
-        own, middle = pl.pallas_call(
+        own, middle, ready = pl.pallas_call(
             functools.partial(own_kernel, sizes),
-            out_shape=(array(field_shape), array(hidden_shape)),
-            in_specs=[VMEM] * (fronts + 3),
-            out_specs=(VMEM, VMEM),
+            out_shape=(array(field_shape), array(hidden_shape), array(flat, jnp.float32)),
+            in_specs=[VMEM] * (fronts + 4),
+            out_specs=(VMEM,) * 3,
             scratch_shapes=[piece_wide],
             compiler_params=modest,
-        )(*outer, *inner, halo[-1], first, slope)
-        result, _, _ = pl.pallas_call(
+        )(*outer, *inner, halo[-1], forcing, first, slope)
+        result, _, _, _ = pl.pallas_call(
             functools.partial(step_kernel, sizes),
-            out_shape=(array(flat, jnp.float32), array(field_shape), array(hidden_shape)),
+            out_shape=(array(flat, jnp.float32), array(field_shape), array(hidden_shape), array(flat, jnp.float32)),
             in_specs=[VMEM] * (fronts + 6),
-            out_specs=(HBM, VMEM, VMEM),
-            input_output_aliases={fronts: 1, fronts + 1: 2},
+            out_specs=(HBM, VMEM, VMEM, VMEM),
+            input_output_aliases={fronts: 1, fronts + 1: 2, fronts + 2: 3},
             scratch_shapes=[
                 piece_wide,
-                pltpu.VMEM(flat, jnp.float32),
                 pltpu.SemaphoreType.DMA((fronts // 2,)),
             ],
             compiler_params=modest,
-        )(*halo, *other, own, middle, forcing, first, second, slope)
+        )(*halo, *other, own, middle, ready, first, second, slope)
     return result.reshape(innovations.shape)
 
 

time: 16.7 us -> 16.7 us (level)
  transfers between devices with their start and end apart: 9 -> 9, of which waited for: 4 -> 4; matrix products, arithmetic and copies ran while one was open for 0% -> 0% of each run, Pallas kernels for 8% -> 9%
where the time goes in v7:
time: 16.7 us; the launch traced here: 16.5 us
  starting transfers between devices  9.1 us (54%)
  Pallas kernels  5.27 us (32%)
  waiting for transfers between devices  2.09 us (13%)
    ppermute x4, starting transfers between devices, to_earlier(): lax.ppermute(block, 'tm', [(i, (i - 1) % count) for i in range(count)])  4.68 us
    ppermute x2, starting transfers between devices, swap_lat(): return lax.ppermute(block, ('grp', 'lat', 'chan'), route)  3.73 us
    pallas_call x1, Pallas kernels, per_device(): pl.pallas_call(functools.partial(step_kernel, sizes), out_shape=(array(fl...  2.1 us
    pallas_call x1, Pallas kernels, per_device(): pl.pallas_call(functools.partial(first_kernel, (fronts, states, cells, ha...  1.7 us
    ppermute x4, waiting for transfers between devices, to_earlier(): lax.ppermute(block, 'tm', [(i, (i - 1) % count) for i in range(count)])  1.22 us
    pallas_call x1, Pallas kernels, per_device(): pl.pallas_call(functools.partial(own_kernel, sizes), out_shape=(array(fie...  0.95 us
    ppermute x2, waiting for transfers between devices, swap_lat(): return lax.ppermute(block, ('grp', 'lat', 'chan'), route)  0.87 us
    ppermute x3, starting transfers between devices, swap_chan(): return lax.ppermute(block, 'chan', [(0, 1), (1, 0)])  0.69 us
  transfers between devices with their start and end apart: 9, of which 4 were waited for; matrix products, arithmetic and copies ran while one was open for 0% of the time, Pallas kernels for 9%

profile of v7, /device:TPU:0, one launch (start us, length us, event | category | flops | bytes accessed | tf_op | source)
XLA Modules:
  0.0 16.5 jit_solution(10587574367002320345)
XLA Ops:
  0.0 1.7 %shard_map.64 = (bf16[292,128]{1,0:T(8,128)(2,1)S(1)}, bf16[292,128]{1,0:T(8,128)(2,1)S(1)}, bf16[292,128]{1,0:T(8,128)(2,1)S(1)}, bf16[292,128]{1,0:T(8,128)(2,...) custom-call(s32[2]{0:T(128)} %layer_ref.1, s32[4]{0:T(128)} %bitcast.10, bf16[1168,128]{1,0:T(8,128)(2,1)} %bitcast.8, ...), custom_call_target="tpu_custom_call" | custom-call | tf_op jit(solution)/shard_map/pallas_call | solution.py:285
  1.7 0.5 %collective-permute-start.3 = (bf16[1664,128]{1,0:T(8,128)(2,1)S(1)}, bf16[1664,128]{1,0:T(8,128)(2,1)S(1)}, u32[]{:S(2)}, u32[]{:S(2)}) collective-permute-start(bf16[1664,128]{1,0:T(8,128)(2,1)S(1)} %get-tuple-element.21.own_ref), channel_id=1, source_target_pairs={{0,1},{1,0},{2,3},{3,2},{4,5},{5,4},{6,7},{7,6},{8,9},{9,8},{10,11... | collective-permute-start | bytes 1277960 | tf_op jit(solution)/shard_map/ppermute | solution.py:15
  2.2 2.6 %collective-permute-start.2 = (bf16[292,128]{1,0:T(8,128)(2,1)S(1)}, bf16[292,128]{1,0:T(8,128)(2,1)S(1)}, u32[]{:S(2)}, u32[]{:S(2)}) collective-permute-start(bf16[292,128]{1,0:T(8,128)(2,1)S(1)} %get-tuple-element.20), channel_id=1, source_target_pairs={{0,2},{2,0},{1,3},{3,1},{4,6},{6,4},{5,7},{7,5},{8,10},{10,8},{9,1... | collective-permute-start | bytes 224264 | tf_op jit(solution)/shard_map/ppermute | solution.py:33
  4.8 0.1 collective-permute-start
  4.9 1.9 %collective-permute-start.5 = (bf16[292,128]{1,0:T(8,128)(2,1)S(1)}, bf16[292,128]{1,0:T(8,128)(2,1)S(1)}, u32[]{:S(2)}, u32[]{:S(2)}) collective-permute-start(bf16[292,128]{1,0:T(8,128)(2,1)S(1)} %get-tuple-element.23), channel_id=1, source_target_pairs={{0,2},{2,0},{1,3},{3,1},{4,6},{6,4},{5,7},{7,5},{8,10},{10,8},{9,1... | collective-permute-start | bytes 224264 | tf_op jit(solution)/shard_map/ppermute | solution.py:33
  6.8 0.1 collective-permute-start.7
  6.9 0.0 collective-permute-done.3.away_ref
  6.9 0.5 %shard_map.65 = (bf16[384,256]{1,0:T(8,128)(2,1)S(1)}, bf16[240,384]{1,0:T(8,128)(2,1)S(1)}, bf16[768,128]{1,0:T(8,128)(2,1)S(1)}, bf16[128,128]{1,0:T(8,128)(2,1)S(1)}) custom-call(bf16[1664,128]{1,0:T(8,128)(2,1)S(1)} %get-tuple-element.21.own_ref, bf16[1664,128]{1,0:T(8,128)(2,1)S(1)} %collective-permute-done.3.away_ref), custom_call_target="tpu_custom_call" | custom-call | tf_op jit(solution)/shard_map/pallas_call | solution.py:313
  7.4 0.4 %collective-permute-done.2.piece_ref.refs_1_ = bf16[292,128]{1,0:T(8,128)(2,1)S(1)} collective-permute-done((bf16[292,128]{1,0:T(8,128)(2,1)S(1)}, bf16[292,128]{1,0:T(8,128)(2,1)S(1)}, u32[]{:S(2)}, u32[]{:S(2)}) %collective-permute-start.2) | collective-permute-done | bytes 74784 | tf_op jit(solution)/shard_map/ppermute | solution.py:33
  7.8 2.2 %collective-permute-start.4 = (bf16[432,128]{1,0:T(8,128)(2,1)S(1)}, bf16[432,128]{1,0:T(8,128)(2,1)S(1)}, u32[]{:S(2)}, u32[]{:S(2)}) collective-permute-start(bf16[432,128]{1,0:T(8,128)(2,1)S(1)} %shard_map.66), channel_id=1, source_target_pairs={{1,4},{4,1},{5,8},{8,5},{9,12},{12,9},{0,16},{13,29},{17,20},{20,1... | collective-permute-start | bytes 331784 | tf_op jit(solution)/shard_map/ppermute | solution.py:28
  10.0 0.0 collective-permute-done.refs_0_
  10.0 1.5 %collective-permute-start.1 = (bf16[292,128]{1,0:T(8,128)(2,1)S(1)}, bf16[292,128]{1,0:T(8,128)(2,1)S(1)}, u32[]{:S(2)}, u32[]{:S(2)}) collective-permute-start(bf16[292,128]{1,0:T(8,128)(2,1)S(1)} %collective-permute-done.refs_0_), channel_id=1, source_target_pairs={{1,4},{4,1},{5,8},{8,5},{9,12},{12,9},{0,16},{13,29},{17,20},{20,1... | collective-permute-start | bytes 224264 | tf_op jit(solution)/shard_map/ppermute | solution.py:28
  11.6 0.0 collective-permute-done.5.refs_2_
  11.6 0.2 %collective-permute-start.6 = (bf16[292,128]{1,0:T(8,128)(2,1)S(1)}, bf16[292,128]{1,0:T(8,128)(2,1)S(1)}, u32[]{:S(2)}, u32[]{:S(2)}) collective-permute-start(bf16[292,128]{1,0:T(8,128)(2,1)S(1)} %collective-permute-done.5.refs_2_), channel_id=1, source_target_pairs={{0,1},{1,0},{2,3},{3,2},{4,5},{5,4},{6,7},{7,6},{8,9},{9,8},{10,11... | collective-permute-start | bytes 224264 | tf_op jit(solution)/shard_map/ppermute | solution.py:15
  11.7 0.8 %collective-permute-done.7.refs_3_ = bf16[292,128]{1,0:T(8,128)(2,1)S(1)} collective-permute-done((bf16[292,128]{1,0:T(8,128)(2,1)S(1)}, bf16[292,128]{1,0:T(8,128)(2,1)S(1)}, u32[]{:S(2)}, u32[]{:S(2)}) %collective-permute-start.7) | collective-permute-done | bytes 74784 | tf_op jit(solution)/shard_map/ppermute | solution.py:33
  12.6 0.0 collective-permute-start.8
  12.6 0.2 %collective-permute-done.4.refs_4_.refs_1_ = bf16[432,128]{1,0:T(8,128)(2,1)S(1)} collective-permute-done((bf16[432,128]{1,0:T(8,128)(2,1)S(1)}, bf16[432,128]{1,0:T(8,128)(2,1)S(1)}, u32[]{:S(2)}, u32[]{:S(2)}) %collective-permute-start.4) | collective-permute-done | bytes 110624 | tf_op jit(solution)/shard_map/ppermute | solution.py:28
  12.7 0.9 %shard_map.67 = (bf16[640,512]{1,0:T(8,128)(2,1)S(1)}, bf16[768,512]{1,0:T(8,128)(2,1)S(1)}, f32[1168,128]{1,0:T(8,128)S(1)}) custom-call(bf16[292,128]{1,0:T(8,128)(2,1)S(1)} %collective-permute-done.refs_0_, bf16[292,128]{1,0:T(8,128)(2,1)S(1)} %collective-permute-done.2.piece_ref.refs_1_, bf16[292,128]{1,0:T(8,128)(2,1)S(1)} %collective-permute-done.5.refs_2_, ...), custom_call_target="tpu_custom_call" | custom-call | tf_op jit(solution)/shard_map/pallas_call | solution.py:348
  13.7 0.7 %collective-permute-done.1.refs_0_ = bf16[292,128]{1,0:T(8,128)(2,1)S(1)} collective-permute-done((bf16[292,128]{1,0:T(8,128)(2,1)S(1)}, bf16[292,128]{1,0:T(8,128)(2,1)S(1)}, u32[]{:S(2)}, u32[]{:S(2)}) %collective-permute-start.1) | collective-permute-done | bytes 74784 | tf_op jit(solution)/shard_map/ppermute | solution.py:28
  14.4 0.0 collective-permute-done.6.refs_2_
  14.4 0.0 collective-permute-done.8.refs_3_
  14.4 2.1 %shard_map.68 = (f32[1168,128]{1,0:T(8,128)}, bf16[640,512]{1,0:T(8,128)(2,1)S(1)}, bf16[768,512]{1,0:T(8,128)(2,1)S(1)}, f32[1168,128]{1,0:T(8,128)S(1)}) custom-call(bf16[292,128]{1,0:T(8,128)(2,1)S(1)} %collective-permute-done.1.refs_0_, ...), custom_call_target="tpu_custom_call", output_to_operand_aliasing={{1}: (4, {}), {2}: (5, {}), {3}: (6, {})} | custom-call | tf_op jit(solution)/shard_map/pallas_call | solution.py:356
  (1 shorter events, 0.0 us)
Async XLA Ops:
  1.7 5.2 %collective-permute-start.3 = (bf16[1664,128]{1,0:T(8,128)(2,1)S(1)}, bf16[1664,128]{1,0:T(8,128)(2,1)S(1)}, u32[]{:S(2)}, u32[]{:S(2)}) collective-permute-start(bf16[1664,128]{1,0:T(8,128)(2,1)S(1)} %get-tuple-element.21.own_ref), channel_id=1, source_target_pairs={{0,1},{1,0},{2,3},{3,2},{4,5},{5,4},{6,7},{7,6},{8,9},{9,8},{10,11... | collective-permute-start | bytes 1277960 | tf_op jit(solution)/shard_map/ppermute | solution.py:15
  2.2 5.6 %collective-permute-start.2 = (bf16[292,128]{1,0:T(8,128)(2,1)S(1)}, bf16[292,128]{1,0:T(8,128)(2,1)S(1)}, u32[]{:S(2)}, u32[]{:S(2)}) collective-permute-start(bf16[292,128]{1,0:T(8,128)(2,1)S(1)} %get-tuple-element.20), channel_id=1, source_target_pairs={{0,2},{2,0},{1,3},{3,1},{4,6},{6,4},{5,7},{7,5},{8,10},{10,8},{9,1... | collective-permute-start | bytes 224264 | tf_op jit(solution)/shard_map/ppermute | solution.py:33
  4.8 5.2 %collective-permute-start = (bf16[292,128]{1,0:T(8,128)(2,1)S(1)}, bf16[292,128]{1,0:T(8,128)(2,1)S(1)}, u32[]{:S(2)}, u32[]{:S(2)}) collective-permute-start(bf16[292,128]{1,0:T(8,128)(2,1)S(1)} %get-tuple-element.19), channel_id=1, source_target_pairs={{0,2},{2,0},{1,3},{3,1},{4,6},{6,4},{5,7},{7,5},{8,10},{10,8},{9,1... | collective-permute-start | bytes 224264 | tf_op jit(solution)/shard_map/ppermute | solution.py:33
  4.9 6.7 %collective-permute-start.5 = (bf16[292,128]{1,0:T(8,128)(2,1)S(1)}, bf16[292,128]{1,0:T(8,128)(2,1)S(1)}, u32[]{:S(2)}, u32[]{:S(2)}) collective-permute-start(bf16[292,128]{1,0:T(8,128)(2,1)S(1)} %get-tuple-element.23), channel_id=1, source_target_pairs={{0,2},{2,0},{1,3},{3,1},{4,6},{6,4},{5,7},{7,5},{8,10},{10,8},{9,1... | collective-permute-start | bytes 224264 | tf_op jit(solution)/shard_map/ppermute | solution.py:33
  6.8 5.8 %collective-permute-start.7 = (bf16[292,128]{1,0:T(8,128)(2,1)S(1)}, bf16[292,128]{1,0:T(8,128)(2,1)S(1)}, u32[]{:S(2)}, u32[]{:S(2)}) collective-permute-start(bf16[292,128]{1,0:T(8,128)(2,1)S(1)} %get-tuple-element.24), channel_id=1, source_target_pairs={{0,2},{2,0},{1,3},{3,1},{4,6},{6,4},{5,7},{7,5},{8,10},{10,8},{9,1... | collective-permute-start | bytes 224264 | tf_op jit(solution)/shard_map/ppermute | solution.py:33
  7.8 4.9 %collective-permute-start.4 = (bf16[432,128]{1,0:T(8,128)(2,1)S(1)}, bf16[432,128]{1,0:T(8,128)(2,1)S(1)}, u32[]{:S(2)}, u32[]{:S(2)}) collective-permute-start(bf16[432,128]{1,0:T(8,128)(2,1)S(1)} %shard_map.66), channel_id=1, source_target_pairs={{1,4},{4,1},{5,8},{8,5},{9,12},{12,9},{0,16},{13,29},{17,20},{20,1... | collective-permute-start | bytes 331784 | tf_op jit(solution)/shard_map/ppermute | solution.py:28
  10.0 4.4 %collective-permute-start.1 = (bf16[292,128]{1,0:T(8,128)(2,1)S(1)}, bf16[292,128]{1,0:T(8,128)(2,1)S(1)}, u32[]{:S(2)}, u32[]{:S(2)}) collective-permute-start(bf16[292,128]{1,0:T(8,128)(2,1)S(1)} %collective-permute-done.refs_0_), channel_id=1, source_target_pairs={{1,4},{4,1},{5,8},{8,5},{9,12},{12,9},{0,16},{13,29},{17,20},{20,1... | collective-permute-start | bytes 224264 | tf_op jit(solution)/shard_map/ppermute | solution.py:28
  11.6 2.8 %collective-permute-start.6 = (bf16[292,128]{1,0:T(8,128)(2,1)S(1)}, bf16[292,128]{1,0:T(8,128)(2,1)S(1)}, u32[]{:S(2)}, u32[]{:S(2)}) collective-permute-start(bf16[292,128]{1,0:T(8,128)(2,1)S(1)} %collective-permute-done.5.refs_2_), channel_id=1, source_target_pairs={{0,1},{1,0},{2,3},{3,2},{4,5},{5,4},{6,7},{7,6},{8,9},{9,8},{10,11... | collective-permute-start | bytes 224264 | tf_op jit(solution)/shard_map/ppermute | solution.py:15
  12.6 1.8 %collective-permute-start.8 = (bf16[292,128]{1,0:T(8,128)(2,1)S(1)}, bf16[292,128]{1,0:T(8,128)(2,1)S(1)}, u32[]{:S(2)}, u32[]{:S(2)}) collective-permute-start(bf16[292,128]{1,0:T(8,128)(2,1)S(1)} %collective-permute-done.7.refs_3_), channel_id=1, source_target_pairs={{0,1},{1,0},{2,3},{3,2},{4,5},{5,4},{6,7},{7,6},{8,9},{9,8},{10,11... | collective-permute-start | bytes 224264 | tf_op jit(solution)/shard_map/ppermute | solution.py:15
